TPU v7x, 32 devices: a whole 2x2x4 slice. The times are simulated.
32 devices in a mesh: group: 4 (over z), dp: 8 (over y, x, core).
Axes of the slice: x: 2, y: 2, z: 4, core: 2. Of those that a mesh axis runs over, the one named last changes fastest.
Arguments:
- queries: bfloat16 [64, 128, 512], P(('group', 'dp')), may hold values from -256 to 256
- passages: bfloat16 [192, 128, 512], P(('group', 'dp')), may hold values from -6 to 6
- candidates: int32 [64, 16], replicated, may hold values from 0 to 191, as said below
- positives: int32 [64, 128], P(('group', 'dp')), may hold values from 0 to 2047
- row_weight: float32 [64, 128], P(('group', 'dp')), may hold values from 0.25 to 4
- owner_map: int32 [192], replicated, may hold values from 0 to 191, as said below
Outputs:
- grad_query: bfloat16 [64, 128, 512], P(('group', 'dp'))
- grad_passage: bfloat16 [192, 128, 512], P(('group', 'dp'))
Inputs may be any that keep to these rules, and one draw needn't show every extreme that they name: `owner_map`: A permutation: entry i is the row block of passages that holds block id i. `candidates`: each row lists 16 different block ids: 12 held by devices of the query block's own group, the others held by devices of other groups with the same dp index. Over all query blocks of one device, at most 2 distinct listed blocks lie on any one device of its group and at most 2 on the devices of any one other group; for every device both bounds are reached.
All inputs are finite; a program needn't handle non-finite values.
Results may differ from a plain program's by a relative error of at most 0.0057.
Values may be sent and summed in bfloat16 or wider, within the bound.
No kernel may reach another device: no remote copies, remote signals or barrier semaphores. Data moves between devices by JAX's collectives and lax.ppermute only.
A program may use at most 128 MiB of HBM per device.

v0:
```python
import math

import jax
import jax.numpy as jnp
from jax import lax
from jax.sharding import PartitionSpec as P

NLOCAL = 12


def route_plan(
    listed_rows, home_group, owner_map, owned_blocks, dp_size, group_size, local_cap, remote_cap
):
    listed_ids = listed_rows.reshape(-1)
    count = listed_ids.shape[0]
    positions = jnp.take(owner_map, listed_ids)
    owner = positions // owned_blocks
    block_slot = positions % owned_blocks
    owner_group = owner // dp_size
    owner_column = owner % dp_size
    is_local = owner_group == home_group
    peer = jnp.where(is_local, owner_column, owner_group)
    listing = jnp.arange(count, dtype=jnp.int32)
    same_block = listed_ids[:, None] == listed_ids[None, :]
    earlier = same_block & (listing[None, :] < listing[:, None])
    unique = jnp.logical_not(jnp.any(earlier, axis=1))
    first_seen = jnp.min(jnp.where(same_block, listing[None, :], count), axis=1)
    ahead = (
        (peer[None, :] == peer[:, None])
        & (is_local[None, :] == is_local[:, None])
        & unique[None, :]
        & (listing[None, :] < first_seen[:, None])
    )
    slot_rank = jnp.sum(ahead.astype(jnp.int32), axis=1)
    local_index = jnp.clip(owner_column * local_cap + slot_rank, 0, dp_size * local_cap - 1)
    remote_index = jnp.clip(owner_group * remote_cap + slot_rank, 0, group_size * remote_cap - 1)
    payload = jnp.where(unique, block_slot + 1, 0)
    local_hit = (
        is_local[:, None, None]
        & (owner_column[:, None, None] == jnp.arange(dp_size, dtype=jnp.int32)[None, :, None])
        & (slot_rank[:, None, None] == jnp.arange(local_cap, dtype=jnp.int32)[None, None, :])
    )
    local_table = jnp.sum(jnp.where(local_hit, payload[:, None, None], 0), axis=0) - 1
    remote_hit = (
        jnp.logical_not(is_local)[:, None, None]
        & (owner_group[:, None, None] == jnp.arange(group_size, dtype=jnp.int32)[None, :, None])
        & (slot_rank[:, None, None] == jnp.arange(remote_cap, dtype=jnp.int32)[None, None, :])
    )
    remote_table = jnp.sum(jnp.where(remote_hit, payload[:, None, None], 0), axis=0) - 1
    return (is_local, local_index, remote_index, local_table, remote_table)


def serve_blocks(table, passages):
    valid = table >= 0
    blocks = jnp.take(passages, jnp.maximum(table, 0), axis=0)
    return jnp.where(valid[..., None, None], blocks, jnp.zeros_like(blocks))


def shards(queries, passages, candidates, positives, row_weight, owner_map):
    dp_size = lax.axis_size("dp")
    group_size = lax.axis_size("group")
    my_group = lax.axis_index("group")
    my_column = lax.axis_index("dp")
    query_blocks, block_rows, width = queries.shape
    owned_blocks = passages.shape[0]
    cand_count = candidates.shape[1]
    local_cap = (NLOCAL + dp_size - 1) // dp_size
    remote_cap = (cand_count - NLOCAL + group_size - 2) // (group_size - 1)
    local_slots_all = dp_size * local_cap
    total_slots = local_slots_all + group_size * remote_cap
    all_lists = candidates.reshape(group_size, dp_size, query_blocks, cand_count)

    def plan_for(listed_rows, home_group):
        return route_plan(
            listed_rows,
            home_group,
            owner_map,
            owned_blocks,
            dp_size,
            group_size,
            local_cap,
            remote_cap,
        )

    my_lists = all_lists[my_group, my_column]
    is_local, local_index, remote_index, own_local, own_remote = plan_for(my_lists, my_group)
    peers_local = jax.vmap(plan_for, in_axes=(0, None))(all_lists[my_group], my_group)[3]
    peers_remote = jax.vmap(plan_for)(
        all_lists[:, my_column], jnp.arange(group_size, dtype=jnp.int32)
    )[4]
    asked_local = jnp.take(peers_local, my_column, axis=1)
    asked_remote = jnp.take(peers_remote, my_group, axis=1)
    local_buffer = lax.all_to_all(
        serve_blocks(asked_local, passages), "dp", split_axis=0, concat_axis=0, tiled=True
    )
    remote_buffer = lax.all_to_all(
        serve_blocks(asked_remote, passages), "group", split_axis=0, concat_axis=0, tiled=True
    )
    local_flat = local_buffer.reshape(local_slots_all, block_rows, width)
    remote_flat = remote_buffer.reshape(group_size * remote_cap, block_rows, width)
    score_scale = 3.0 / math.sqrt(width)
    slot_index = jnp.where(is_local, local_index, local_slots_all + remote_index)
    slot_grid = slot_index.reshape(query_blocks, cand_count)
    local_pick = is_local.reshape(query_blocks, cand_count)
    order = jnp.argsort(jnp.logical_not(local_pick).astype(jnp.int32), axis=1, stable=True)
    inverse = jnp.argsort(order, axis=1)
    slot_grid = jnp.take_along_axis(slot_grid, order, axis=1)
    near_slots = slot_grid[:, :NLOCAL].reshape(-1)
    far_slots = (slot_grid[:, NLOCAL:] - local_slots_all).reshape(-1)
    near_cand = jnp.take(local_flat, near_slots, axis=0).reshape(
        query_blocks, NLOCAL, block_rows, width
    )
    near_scores = jnp.einsum(
        "brd,bkjd->brkj", queries, near_cand, preferred_element_type=jnp.float32
    )
    far_cand = jnp.take(remote_flat, far_slots, axis=0).reshape(
        query_blocks, cand_count - NLOCAL, block_rows, width
    )
    far_scores = jnp.einsum("brd,bkjd->brkj", queries, far_cand, preferred_element_type=jnp.float32)
    scores = jnp.concatenate([near_scores, far_scores], axis=2) * score_scale
    candidate = jnp.concatenate([near_cand, far_cand], axis=1)
    moved_block = jnp.take_along_axis(inverse, positives // block_rows, axis=1)
    target_rows = moved_block * block_rows + positives % block_rows
    flat_scores = scores.reshape(query_blocks, block_rows, cand_count * block_rows)
    probability = jax.nn.softmax(flat_scores, axis=-1)
    target = (
        jnp.arange(cand_count * block_rows, dtype=jnp.int32)[None, None, :]
        == target_rows[:, :, None]
    ).astype(jnp.float32)
    dscore = ((probability - target) * (row_weight[:, :, None] * score_scale)).astype(jnp.bfloat16)
    dscore = dscore.reshape(query_blocks, block_rows, cand_count, block_rows)
    grad_query = jnp.einsum(
        "brkj,bkjd->brd", dscore, candidate, preferred_element_type=jnp.float32
    ).astype(jnp.bfloat16)

    def add_block(index, totals):
        block_terms = jnp.einsum(
            "rkj,rd->kjd", dscore[index], queries[index], preferred_element_type=jnp.float32
        )
        return totals.at[slot_grid[index]].add(block_terms)

    slot_terms = lax.fori_loop(
        0, query_blocks, add_block, jnp.zeros((total_slots, block_rows, width), jnp.float32)
    )
    slot_terms = slot_terms.astype(jnp.bfloat16)
    local_out = slot_terms[:local_slots_all].reshape(dp_size, local_cap, block_rows, width)
    remote_out = slot_terms[local_slots_all:].reshape(group_size, remote_cap, block_rows, width)
    local_back = lax.all_to_all(local_out, "dp", split_axis=0, concat_axis=0, tiled=True)
    remote_back = lax.all_to_all(remote_out, "group", split_axis=0, concat_axis=0, tiled=True)
    owned = jnp.arange(owned_blocks, dtype=jnp.int32)
    local_owner = (asked_local[..., None] == owned).astype(jnp.bfloat16)
    remote_owner = (asked_remote[..., None] == owned).astype(jnp.bfloat16)
    grad_sum = jnp.einsum(
        "qcp,qcxd->pxd", local_owner, local_back, preferred_element_type=jnp.float32
    )
    grad_sum = grad_sum + jnp.einsum(
        "qcp,qcxd->pxd", remote_owner, remote_back, preferred_element_type=jnp.float32
    )
    return (grad_query, grad_sum.astype(jnp.bfloat16))


def solution(mesh):
    return jax.shard_map(
        shards,
        mesh=mesh,
        in_specs=(
            P(("group", "dp"), None, None),
            P(("group", "dp"), None, None),
            P(),
            P(("group", "dp"), None),
            P(("group", "dp"), None),
            P(),
        ),
        out_specs=(P(("group", "dp"), None, None), P(("group", "dp"), None, None)),
        check_vma=False,
    )
```

profile of v0, /device:TPU:0, one launch (start us, length us, event | category | flops | bytes accessed | tf_op | source)
XLA Modules:
  0.0 176.4 jit_solution(8413663674855671735)
XLA Ops:
  7.0 6.3 %all-to-all-start.1 = ((bf16[4,2,128,512]{3,2,1,0:T(8,128)(2,1)}), bf16[4,2,128,512]{3,2,1,0:T(8,128)(2,1)}, u32[]{:S(2)}, u32[]{:S(2)}) async-start(bf16[4,2,128,512]{3,2,1,0:T(8,128)(2,1)} %select_select_fusion.1), calls=%async_computation.1 | async-start | bytes 2097152 | tf_op jit(solution)/shard_map/all_to_all | solution.py:96
  23.8 15.3 %all-to-all-done.1 = bf16[4,2,128,512]{3,2,1,0:T(8,128)(2,1)} async-done(((bf16[4,2,128,512]{3,2,1,0:T(8,128)(2,1)}), bf16[4,2,128,512]{3,2,1,0:T(8,128)(2,1)}, u32[]{:S(2)}, u32[]{:S(2)}) %all-to-all-start.1) | async-done | bytes 1048608 | tf_op jit(solution)/shard_map/all_to_all | solution.py:96
  39.1 3.8 %all-to-all-start = ((bf16[8,2,128,512]{3,2,1,0:T(8,128)(2,1)}), bf16[8,2,128,512]{3,2,1,0:T(8,128)(2,1)S(1)}, u32[]{:S(2)}, u32[]{:S(2)}) async-start(bf16[8,2,128,512]{3,2,1,0:T(8,128)(2,1)} %select_select_fusion), calls=%async_computation | async-start | bytes 4194304 | tf_op jit(solution)/shard_map/all_to_all | solution.py:93
  43.6 2.0 %gather_fusion.8 = s32[256]{0:T(256)S(1)} fusion(s32[2,16]{0,1:T(8,128)S(1)} %get-tuple-element.99, s32[256]{0:T(256)S(1)} %get-tuple-element.143), kind=kCustom, calls=%fused_computation.8 | custom fusion | bytes 4096 | tf_op jit(solution)/shard_map/jit(take_along_axis)/gather | solution.py:122
  45.8 2.8 %gather_fusion.6 = bf16[8,128,512]{2,1,0:T(8,128)(2,1)} fusion(bf16[8,128,512]{2,1,0:T(8,128)(2,1)} %bitcast.19, s32[1024]{0:T(1024)S(1)} %pad_clamp_fusion), kind=kCustom, calls=%fused_computation.6 | custom fusion | bytes 2097184 | tf_op jit(solution)/shard_map/jit(_take)/gather | solution.py:116
  51.5 18.0 %all-to-all-done = bf16[8,2,128,512]{3,2,1,0:T(8,128)(2,1)S(1)} async-done(((bf16[8,2,128,512]{3,2,1,0:T(8,128)(2,1)}), bf16[8,2,128,512]{3,2,1,0:T(8,128)(2,1)S(1)}, u32[]{:S(2)}, u32[]{:S(2)}) %all-to-all-start) | async-done | bytes 2097184 | tf_op jit(solution)/shard_map/all_to_all | solution.py:93
  69.5 2.5 %gather_fusion.3 = bf16[24,128,512]{2,1,0:T(8,128)(2,1)} fusion(bf16[16,128,512]{2,1,0:T(8,128)(2,1)S(1)} %bitcast.103, s32[1024]{0:T(1024)S(1)} %pad_clamp_fusion.3), kind=kCustom, calls=%fused_computation.3 | custom fusion | bytes 6291552 | tf_op jit(solution)/shard_map/jit(_take)/gather | solution.py:110
  72.0 2.3 %broadcast_select_fusion = bf16[2,12,128,512]{3,2,1,0:T(8,128)(2,1)S(1)} fusion(bf16[2,12,128,512]{3,2,1,0:T(8,128)(2,1)} %bitcast.104, pred[2,12]{1,0:T(4,128)(4,1)S(1)} %compare_and_fusion.4), kind=kLoop, calls=%fused_computation.24 | loop fusion | flops 1572864 | bytes 6291480 | tf_op jit(solution)/shard_map/jit(_take)/select_n | solution.py:110
  77.5 3.5 %broadcast_in_dim.258 = f32[24,128,512]{2,1,0:T(8,128)} broadcast(f32[]{:T(128)} %constant.338.clone.1), dimensions={} | broadcast | bytes 6291460 | tf_op jit(solution)/shard_map/broadcast_in_dim | solution.py:143
  81.0 24.9 %while.15 = (s32[]{:T(128)}, f32[24,128,512]{2,1,0:T(8,128)}, s32[2,16]{1,0:T(2,128)S(1)}, bf16[2,128,16,128]{1,3,2,0:T(8,128)(2,1)S(1)}, bf16[2,128,512]{2,1,0:T(8,128)(2,1)S(1)}, /*index=5*/s32[]{:T(128)}) while((s32[]{:T(128)}, f32[24,128,512]{2,1,0:T(8,128)}, s32[2,16]{1,0:T(2,128)S(1)}, bf16[2,128,16,128]{1,3,2,0:T(8,128)(2,1)S(1)}, ...), condition=%wide.region_17.18_spmd, body=%wide.region_15.17_spmd.sunk | while | flops 269484096 | bytes 17433872 | solution.py:142
  81.0 2.7 %fusion.77 = f32[16,128,512]{2,1,0:T(8,128)} fusion(bf16[2,128,16,128]{1,3,2,0:T(8,128)(2,1)S(1)} %get-tuple-element.210, s32[]{:T(128)S(6)} %copy.97, bf16[2,128,512]{2,1,0:T(8,128)(2,1)S(1)} %get-tuple-element.211), kind=kOutput, calls=%fused_computation.10.clone.1 | convolution fusion | flops 268435456 | bytes 4850688 | tf_op jit(solution)/shard_map/while/body/eval_jaxpr/rkj,rd->kjd/dot_general | solution.py:137
  83.7 9.7 %scatter_fusion = f32[24,128,512]{2,1,0:T(8,128)} fusion(f32[24,128,512]{2,1,0:T(8,128)} %get-tuple-element.202, s32[16]{0:T(128)S(1)} %fusion.76, f32[16,128,512]{2,1,0:T(8,128)} %fusion.77), kind=kCustom, calls=%fused_computation.9.clone.1 | custom fusion | flops 1048576 | bytes 12582976 | tf_op jit(solution)/shard_map/while/body/eval_jaxpr/scatter-add | solution.py:140
  93.5 2.7 %fusion.77 = f32[16,128,512]{2,1,0:T(8,128)} fusion(bf16[2,128,16,128]{1,3,2,0:T(8,128)(2,1)S(1)} %get-tuple-element.210, s32[]{:T(128)S(6)} %copy.97, bf16[2,128,512]{2,1,0:T(8,128)(2,1)S(1)} %get-tuple-element.211), kind=kOutput, calls=%fused_computation.10.clone.1 | convolution fusion | flops 268435456 | bytes 4850688 | tf_op jit(solution)/shard_map/while/body/eval_jaxpr/rkj,rd->kjd/dot_general | solution.py:137
  96.2 9.7 %scatter_fusion = f32[24,128,512]{2,1,0:T(8,128)} fusion(f32[24,128,512]{2,1,0:T(8,128)} %get-tuple-element.202, s32[16]{0:T(128)S(1)} %fusion.76, f32[16,128,512]{2,1,0:T(8,128)} %fusion.77), kind=kCustom, calls=%fused_computation.9.clone.1 | custom fusion | flops 1048576 | bytes 12582976 | tf_op jit(solution)/shard_map/while/body/eval_jaxpr/scatter-add | solution.py:140
  105.9 3.2 %convert_element_type.38 = bf16[24,128,512]{2,1,0:T(8,128)(2,1)S(1)} convert(f32[24,128,512]{2,1,0:T(8,128)} %get-tuple-element.100) | non-fusion elementwise | flops 1572864 | bytes 9437184 | tf_op jit(solution)/shard_map/convert_element_type | solution.py:145
  110.8 3.5 %copy.80 = bf16[8,2,128,512]{3,1,2,0:T(2,128)(2,1)} copy(bf16[8,2,128,512]{3,2,1,0:T(8,128)(2,1)S(1)} %bitcast.107) | data formatting | bytes 4194304 | tf_op jit(solution)/shard_map/reshape | solution.py:146
  114.3 4.4 %all-to-all-start.2 = ((bf16[8,2,128,512]{3,1,2,0:T(2,128)(2,1)}), bf16[8,2,128,512]{3,1,2,0:T(2,128)(2,1)}, u32[]{:S(2)}, u32[]{:S(2)}) async-start(bf16[8,2,128,512]{3,1,2,0:T(2,128)(2,1)} %copy.80), calls=%async_computation.2 | async-start | bytes 4194304 | tf_op jit(solution)/shard_map/all_to_all | solution.py:148
  119.9 2.1 %copy.82 = bf16[4,2,128,512]{3,1,2,0:T(2,128)(2,1)} copy(bf16[4,2,128,512]{3,2,1,0:T(8,128)(2,1)S(1)} %bitcast.105) | data formatting | bytes 2097152 | tf_op jit(solution)/shard_map/reshape | solution.py:147
  122.0 23.4 %all-to-all-done.2 = bf16[8,2,128,512]{3,1,2,0:T(2,128)(2,1)} async-done(((bf16[8,2,128,512]{3,1,2,0:T(2,128)(2,1)}), bf16[8,2,128,512]{3,1,2,0:T(2,128)(2,1)}, u32[]{:S(2)}, u32[]{:S(2)}) %all-to-all-start.2) | async-done | bytes 2097184 | tf_op jit(solution)/shard_map/all_to_all | solution.py:148
  145.3 4.5 %all-to-all-start.3 = ((bf16[4,2,128,512]{3,1,2,0:T(2,128)(2,1)}), bf16[4,2,128,512]{3,1,2,0:T(2,128)(2,1)}, u32[]{:S(2)}, u32[]{:S(2)}) async-start(bf16[4,2,128,512]{3,1,2,0:T(2,128)(2,1)} %copy.82), calls=%async_computation.3 | async-start | bytes 2097152 | tf_op jit(solution)/shard_map/all_to_all | solution.py:149
  149.8 3.4 %fusion.19 = bf16[2,128,512]{2,1,0:T(8,128)(2,1)} fusion(bf16[2,128,16,128]{1,3,2,0:T(8,128)(2,1)S(1)} %get-tuple-element.214, bf16[2,4,128,512]{3,2,1,0:T(8,128)(2,1)S(1)} %copy-done.7, bf16[2,12,128,512]{3,2,1,0:T(8,128)(2,1)} %copy-done.2), kind=kOutput, calls=%fused_computation.37 | convolution fusion | flops 539099136 | bytes 5505024 | tf_op jit(solution)/shard_map/brkj,bkjd->brd/dot_general | solution.py:132
  153.3 2.9 %fusion.13 = f32[6,128,512,1]{2,0,3,1:T(8,128)S(1)} fusion(bf16[8,2,128,512]{3,1,2,0:T(2,128)(2,1)} %all-to-all-done.2, s32[8,2]{0,1:T(2,128)S(1)} %bitcast.115), kind=kOutput, calls=%fused_computation.28 | convolution fusion | flops 12583008 | bytes 3670080 | tf_op jit(solution)/shard_map/qcp,qcxd->pxd/dot_general | solution.py:153
  156.2 16.5 %all-to-all-done.3 = bf16[4,2,128,512]{3,1,2,0:T(2,128)(2,1)} async-done(((bf16[4,2,128,512]{3,1,2,0:T(2,128)(2,1)}), bf16[4,2,128,512]{3,1,2,0:T(2,128)(2,1)}, u32[]{:S(2)}, u32[]{:S(2)}) %all-to-all-start.3) | async-done | bytes 1048608 | tf_op jit(solution)/shard_map/all_to_all | solution.py:149
  172.7 2.6 %fusion.12 = bf16[6,128,512]{2,0,1:T(8,128)(2,1)S(1)} fusion(f32[6,128,512,1]{2,0,3,1:T(8,128)S(1)} %fusion.13, bf16[4,2,128,512]{3,1,2,0:T(2,128)(2,1)} %all-to-all-done.3, s32[4,2]{0,1:T(2,128)S(1)} %bitcast.114), kind=kOutput, calls=%fused_computation.27 | convolution fusion | flops 7077936 | bytes 3407904 | tf_op jit(solution)/shard_map/qcp,qcxd->pxd/dot_general | solution.py:156
  (131 shorter events, 27.4 us)
Async XLA Ops:
  0.6 4.5 %copy-start = (bf16[6,128,512]{2,1,0:T(8,128)(2,1)S(1)}, bf16[6,128,512]{2,1,0:T(8,128)(2,1)}, u32[]{:S(2)}) copy-start(bf16[6,128,512]{2,1,0:T(8,128)(2,1)} %param.9) | copy-start | bytes 2359300
  5.8 8.1 %copy-start.1 = (s32[192]{0:T(256)S(1)}, s32[192]{0:T(256)}, u32[]{:S(2)}) copy-start(s32[192]{0:T(256)} %param.13) | copy-start | bytes 2308
  7.0 32.1 %all-to-all-start.1 = ((bf16[4,2,128,512]{3,2,1,0:T(8,128)(2,1)}), bf16[4,2,128,512]{3,2,1,0:T(8,128)(2,1)}, u32[]{:S(2)}, u32[]{:S(2)}) async-start(bf16[4,2,128,512]{3,2,1,0:T(8,128)(2,1)} %select_select_fusion.1), calls=%async_computation.1 | async-start | bytes 2097152 | tf_op jit(solution)/shard_map/all_to_all | solution.py:96
  21.4 0.7 copy-start.8
  23.8 22.0 %copy-start.9 = (f32[2,128]{1,0:T(2,128)S(1)}, f32[2,128]{1,0:T(2,128)}, u32[]{:S(2)}) copy-start(f32[2,128]{1,0:T(2,128)} %param.12) | copy-start | bytes 3076
  39.1 30.4 %all-to-all-start = ((bf16[8,2,128,512]{3,2,1,0:T(8,128)(2,1)}), bf16[8,2,128,512]{3,2,1,0:T(8,128)(2,1)S(1)}, u32[]{:S(2)}, u32[]{:S(2)}) async-start(bf16[8,2,128,512]{3,2,1,0:T(8,128)(2,1)} %select_select_fusion), calls=%async_computation | async-start | bytes 4194304 | tf_op jit(solution)/shard_map/all_to_all | solution.py:93
  48.6 2.4 %copy-start.4 = (bf16[2,128,512]{2,1,0:T(8,128)(2,1)S(1)}, bf16[2,128,512]{2,1,0:T(8,128)(2,1)}, u32[]{:S(2)}) copy-start(bf16[2,128,512]{2,1,0:T(8,128)(2,1)} %param.8) | copy-start | bytes 786436
  50.1 1.0 copy-start.6
  72.0 2.3 %copy-start.5 = (bf16[2,128,512]{2,1,0:T(8,128)(2,1)S(1)}, bf16[2,128,512]{2,1,0:T(8,128)(2,1)}, u32[]{:S(2)}) copy-start(bf16[2,128,512]{2,1,0:T(8,128)(2,1)} %param.8) | copy-start | bytes 786436
  74.3 1.8 copy-start.2
  109.1 1.7 copy-start.3
  114.3 31.0 %all-to-all-start.2 = ((bf16[8,2,128,512]{3,1,2,0:T(2,128)(2,1)}), bf16[8,2,128,512]{3,1,2,0:T(2,128)(2,1)}, u32[]{:S(2)}, u32[]{:S(2)}) async-start(bf16[8,2,128,512]{3,1,2,0:T(2,128)(2,1)} %copy.80), calls=%async_computation.2 | async-start | bytes 4194304 | tf_op jit(solution)/shard_map/all_to_all | solution.py:148
  118.7 1.2 slice-start
  119.9 29.9 %copy-start.7 = (bf16[2,4,128,512]{3,2,1,0:T(8,128)(2,1)S(1)}, bf16[2,4,128,512]{3,2,1,0:T(8,128)(2,1)}, u32[]{:S(2)}) copy-start(bf16[2,4,128,512]{3,2,1,0:T(8,128)(2,1)} %copy-done.6) | copy-start | bytes 3145732
  145.3 27.4 %all-to-all-start.3 = ((bf16[4,2,128,512]{3,1,2,0:T(2,128)(2,1)}), bf16[4,2,128,512]{3,1,2,0:T(2,128)(2,1)}, u32[]{:S(2)}, u32[]{:S(2)}) async-start(bf16[4,2,128,512]{3,1,2,0:T(2,128)(2,1)} %copy.82), calls=%async_computation.3 | async-start | bytes 2097152 | tf_op jit(solution)/shard_map/all_to_all | solution.py:149
where the time goes:
time: 178 us; the launch traced here: 176 us
  waiting for transfers between devices  73.2 us (41%)
  other arithmetic  35.6 us (20%)
  local copies, waits for them, and re-layouts  31.8 us (18%)
  starting transfers between devices  18.9 us (11%)
  matrix products  15.8 us (9%)
    all_to_all x1, waiting for transfers between devices, shards(): lax.all_to_all(local_out, 'dp', split_axis=0, concat_axis=0, tiled=True)  23.4 us
    scatter-add x2, other arithmetic, add_block(): return totals.at[slot_grid[index]].add(block_terms)  19.4 us
    all_to_all x1, waiting for transfers between devices, shards(): lax.all_to_all(serve_blocks(asked_local, passages), 'dp', split_axis=0, c...  18 us
    all_to_all x1, waiting for transfers between devices, shards(): lax.all_to_all(remote_out, 'group', split_axis=0, concat_axis=0, tiled=True)  16.5 us
    all_to_all x1, waiting for transfers between devices, shards(): lax.all_to_all(serve_blocks(asked_remote, passages), 'group', split_axis=...  15.3 us
    all_to_all x1, starting transfers between devices, shards(): lax.all_to_all(serve_blocks(asked_remote, passages), 'group', split_axis=...  6.32 us
    dot_general x2, matrix products, add_block(): jnp.einsum('rkj,rd->kjd', dscore[index], queries[index], preferred_elemen...  5.45 us
    unnamed x22, local copies, waits for them, and re-layouts  5.19 us
  transfers between devices with their start and end apart: 4, of which 4 were waited for; matrix products, arithmetic and copies ran while one was open for 15% of the time, Pallas kernels for 0%

commit v1 on v0

v1 whole, which is shorter than its diff:
```python
import functools
import math

import jax
import jax.numpy as jnp
from jax import lax
from jax.experimental import pallas as pl
from jax.experimental.pallas import tpu as pltpu
from jax.sharding import PartitionSpec as P

NLOCAL = 12
VMEM_BYTES = 32 * 1024 * 1024


def swap(x, axis, mask):
    size = lax.axis_size(axis)
    return lax.ppermute(x, axis, [(i, i ^ mask) for i in range(size)])


def slot_table(listing, cap):
    listed = jnp.max(listing, axis=1) >= 0
    blocks = listed.shape[1]
    number = jnp.arange(blocks, dtype=jnp.int32)
    ahead = listed[:, None, :] & (number[None, None, :] < number[None, :, None])
    rank = jnp.sum(ahead.astype(jnp.int32), axis=2)
    taken = listed[:, None, :] & (
        rank[:, None, :] == jnp.arange(cap, dtype=jnp.int32)[None, :, None]
    )
    block = jnp.max(jnp.where(taken, number, 0), axis=2)
    entry = jnp.max(jnp.where(taken[:, None], listing[:, :, None, :], -1), axis=3)
    return block, entry.reshape(entry.shape[0], -1)


def serve_kernel(sources, me, block, passages, *rest):
    outs, sems = rest[:-1], rest[-1]
    copies = []
    for out, pieces in zip(outs, sources(me)):
        for piece, (owner, slot) in enumerate(pieces):
            copies.append(
                pltpu.make_async_copy(
                    passages.at[block[owner, slot]], out.at[piece], sems.at[len(copies)]
                )
            )
    for copy in copies:
        copy.start()
    for copy in copies:
        copy.wait()


def serve(sources, counts, me, block, passages):
    smem = pl.BlockSpec(memory_space=pltpu.SMEM)
    hbm = pl.BlockSpec(memory_space=pl.ANY)
    return pl.pallas_call(
        functools.partial(serve_kernel, sources),
        out_shape=[
            jax.ShapeDtypeStruct((count,) + passages.shape[1:], passages.dtype) for count in counts
        ],
        in_specs=[smem, smem, hbm],
        out_specs=[hbm] * len(counts),
        scratch_shapes=[pltpu.SemaphoreType.DMA((sum(counts),))],
        compiler_params=pltpu.CompilerParams(vmem_limit_bytes=VMEM_BYTES),
    )(me, block, passages)


def masked_scores(scale, entry, holder, cap, query, block_rows, pieces):
    slots = pieces.shape[0] // block_rows
    scores = (
        lax.dot_general(
            query, pieces, (((1,), (1,)), ((), ())), preferred_element_type=jnp.float32
        )
        * scale
    )
    for block in range(query.shape[0] // block_rows):
        for slot in range(slots):
            listing = entry[holder, block * cap + slot]
            bias = jnp.where(listing >= 0, 0.0, -jnp.inf).astype(jnp.float32)
            rows = slice(block * block_rows, (block + 1) * block_rows)
            columns = slice(slot * block_rows, (slot + 1) * block_rows)
            yield block, slot, listing, scores[rows, columns] + bias


def holders_of(me, columns, groups):
    group, column = me[0], me[1]
    near = [group * columns + peer for peer in range(columns)]
    far = [(group ^ mask) * columns + column for mask in range(1, groups)]
    return near, far


def held_pieces(me, columns, groups, near_ref, far_refs):
    near, far = holders_of(me, columns, groups)
    width = near_ref.shape[-1]
    caps = near_ref.shape[0] // columns
    for peer, holder in enumerate(near):
        yield holder, near_ref[peer * caps : (peer + 1) * caps].reshape(-1, width)
    for ref, holder in zip(far_refs, far):
        yield holder, ref[...].reshape(-1, width)


def stats_kernel(
    scale, cap, columns, groups, me, entry, queries, weight, positives, near, *rest
):
    far, stat, scores_ref, peak_ref = rest[: groups - 1], rest[-3], rest[-2], rest[-1]
    query_blocks, block_rows, width = queries.shape
    rows = query_blocks * block_rows
    query = queries[...].reshape(rows, width)
    peak_ref[...] = jnp.full_like(peak_ref, -jnp.inf)
    at = 0
    for holder, pieces in held_pieces(me, columns, groups, near, far):
        for block, slot, _, part in masked_scores(
            scale, entry, holder, cap, query, block_rows, pieces
        ):
            mine = slice(block * block_rows, (block + 1) * block_rows)
            scores_ref[at + slot, mine] = part
            peak_ref[mine] = jnp.maximum(peak_ref[mine], part)
        at += pieces.shape[0] // block_rows
    peak = jnp.max(peak_ref[...], axis=1, keepdims=True)
    total = jnp.zeros((rows, block_rows), jnp.float32)
    for index in range(at):
        total = total + jnp.exp(scores_ref[index] - peak)
    total = jnp.sum(total, axis=1, keepdims=True)
    lane = lax.broadcasted_iota(jnp.int32, (rows, 128), 1)
    turned = jnp.where(lane == 0, peak, total).T
    stat[...] = jnp.zeros_like(stat)
    stat[0:2] = turned[0:2]
    for block in range(query_blocks):
        mine = slice(block * block_rows, (block + 1) * block_rows)
        stat[2:3, mine] = weight[block : block + 1] * scale
        stat[3:4, mine] = positives[block : block + 1].astype(jnp.float32)


def query_kernel(scale, cap, columns, groups, me, entry, queries, stat, near, *rest):
    far, out, total, dscore_ref = rest[: groups - 1], rest[-3], rest[-2], rest[-1]
    query_blocks, block_rows, width = queries.shape
    rows = query_blocks * block_rows
    query = queries[...].reshape(rows, width)
    turned = jnp.concatenate(
        [stat[...], jnp.zeros((128 - stat.shape[0], rows), jnp.float32)], axis=0
    ).T
    peak, inverse = turned[:, 0:1], 1.0 / turned[:, 1:2]
    weight, positive = turned[:, 2:3], turned[:, 3:4]
    place = lax.broadcasted_iota(jnp.int32, (block_rows, block_rows), 1)
    total[...] = jnp.zeros_like(total)
    for holder, pieces in held_pieces(me, columns, groups, near, far):
        for block, slot, listing, part in masked_scores(
            scale, entry, holder, cap, query, block_rows, pieces
        ):
            mine = slice(block * block_rows, (block + 1) * block_rows)
            number = (place + listing * block_rows).astype(jnp.float32)
            target = jnp.where(positive[mine] == number, 1.0, 0.0)
            chance = jnp.exp(part - peak[mine]) * inverse[mine]
            dscore_ref[mine, slot * block_rows : (slot + 1) * block_rows] = (
                (chance - target) * weight[mine]
            ).astype(jnp.bfloat16)
        total[...] += jnp.dot(
            dscore_ref[:, : pieces.shape[0]], pieces, preferred_element_type=jnp.float32
        )
    out[...] = total[...].reshape(out.shape).astype(out.dtype)


def passage_kernel(
    scale, cap, near_cap, far_cap, columns, groups, me, block, entry, passages, even, odd, *rest
):
    far_count = groups - 1
    far, near_stats = rest[:far_count], rest[far_count : far_count + columns // 2]
    far_stats = rest[far_count + columns // 2 : 2 * far_count + columns // 2]
    out, total = rest[-2], rest[-1]
    query_blocks, block_rows, width = even.shape[1:]
    rows = query_blocks * block_rows
    group, column = me[0], me[1]
    units = []
    for pair in range(columns // 2):
        for core, side in enumerate((even, odd)):
            owner = group * columns + (column ^ (2 * pair + core))
            units.append((owner, near_cap, side.at[pair], near_stats[pair].at[core]))
    for mask in range(1, groups):
        owner = (group ^ mask) * columns + column
        units.append((owner, far_cap, far[mask - 1], far_stats[mask - 1]))
    total[...] = jnp.zeros_like(total)
    lane = lax.broadcasted_iota(jnp.int32, (1, rows), 1)
    place = lax.broadcasted_iota(jnp.int32, (block_rows, rows), 0)
    for owner, slots, query_ref, stat in units:
        query = query_ref[...].reshape(rows, width)
        peak, inverse = stat[0:1], 1.0 / stat[1:2]
        weight, positive = stat[2:3], stat[3:4]
        held = [block[owner, slot] for slot in range(slots)]
        mine = jnp.concatenate([passages[index] for index in held], axis=0)
        scores = (
            lax.dot_general(
                mine, query, (((1,), (1,)), ((), ())), preferred_element_type=jnp.float32
            )
            * scale
        )
        parts = []
        for slot in range(slots):
            listing = jnp.full((1, rows), entry[owner, slot], jnp.int32)
            for query_block in range(1, query_blocks):
                listing = jnp.where(
                    lane >= query_block * block_rows, entry[owner, query_block * cap + slot], listing
                )
            bias = jnp.where(listing >= 0, 0.0, -jnp.inf)
            number = (place + listing * block_rows).astype(jnp.float32)
            part = scores[slot * block_rows : (slot + 1) * block_rows] + bias
            target = jnp.where(positive == number, 1.0, 0.0)
            chance = jnp.exp(part - peak) * inverse
            parts.append(((chance - target) * weight).astype(jnp.bfloat16))
        term = jnp.dot(
            jnp.concatenate(parts, axis=0), query, preferred_element_type=jnp.float32
        ).astype(jnp.bfloat16)
        for slot, index in enumerate(held):
            total[index] += term[slot * block_rows : (slot + 1) * block_rows].astype(jnp.float32)
    out[...] = total[...].astype(out.dtype)


def call(kernel, out, scratch, flops, smem_args, vmem_args):
    return pl.pallas_call(
        kernel,
        out_shape=out,
        in_specs=[pl.BlockSpec(memory_space=pltpu.SMEM)] * len(smem_args)
        + [pl.BlockSpec(memory_space=pltpu.VMEM)] * len(vmem_args),
        out_specs=pl.BlockSpec(memory_space=pltpu.VMEM),
        scratch_shapes=scratch,
        compiler_params=pltpu.CompilerParams(vmem_limit_bytes=VMEM_BYTES),
        cost_estimate=pl.CostEstimate(
            flops=flops,
            bytes_accessed=sum(math.prod(a.shape) * a.dtype.itemsize for a in vmem_args),
            transcendentals=0,
        ),
    )(*smem_args, *vmem_args)


def gather_columns(x, axis):
    size = lax.axis_size(axis)
    half = x.shape[0] // 2
    held = {0: x}
    for mask in range(2, size, 2):
        high = 1 << (mask.bit_length() - 1)
        low = mask & -mask
        if high == low:
            held[mask] = swap(x, axis, mask)
        else:
            held[mask] = jnp.concatenate(
                [
                    swap(held[mask ^ high][:half], axis, high),
                    swap(held[mask ^ low][half:], axis, low),
                ]
            )
    even = jnp.stack([held[mask] for mask in range(0, size, 2)])
    return even, swap(even, axis, 1)


def gather_groups(x, axis):
    held = {0: x}
    mask = lax.axis_size(axis) - 1
    while mask:
        held.update({at ^ mask: swap(piece, axis, mask) for at, piece in list(held.items())})
        mask >>= 1
    return [held[at] for at in range(1, lax.axis_size(axis))]


def shards(queries, passages, candidates, positives, row_weight, owner_map):
    columns = lax.axis_size("dp")
    groups = lax.axis_size("group")
    my_group = lax.axis_index("group").astype(jnp.int32)
    my_column = lax.axis_index("dp").astype(jnp.int32)
    device = my_group * columns + my_column
    me = jnp.stack([my_group, my_column])
    query_blocks, block_rows, width = queries.shape
    rows = query_blocks * block_rows
    blocks = passages.shape[0]
    listed = candidates.shape[1]
    near_cap = (NLOCAL + columns - 1) // columns
    far_cap = (listed - NLOCAL + groups - 2) // (groups - 1)
    cap = max(near_cap, far_cap)
    devices = columns * groups
    scale = 3.0 / math.sqrt(width)

    far_queries = gather_groups(queries, "group")
    even, odd = gather_columns(queries, "dp")

    number = jnp.arange(listed, dtype=jnp.int32)
    held_at = device * blocks + jnp.arange(blocks, dtype=jnp.int32)
    block_id = jnp.sum(
        jnp.where(
            owner_map[None, :] == held_at[:, None],
            jnp.arange(owner_map.shape[0], dtype=jnp.int32)[None, :],
            0,
        ),
        axis=1,
    )
    asked = jnp.max(
        jnp.where(
            candidates[:, None, :] == block_id[None, :, None], number[None, None, :], -1
        ),
        axis=2,
    ).reshape(devices, query_blocks, blocks)
    asked_block, asked_entry = slot_table(asked, cap)

    def far_sources(me):
        _, far = holders_of(me, columns, groups)
        return [[(owner, slot) for slot in range(far_cap)] for owner in far]

    def near_sources(me):
        near, _ = holders_of(me, columns, groups)
        return [[(owner, slot) for owner in near for slot in range(near_cap)]]

    far_out = serve(far_sources, [far_cap] * (groups - 1), me, asked_block, passages)
    far_blocks = [swap(piece, "group", mask + 1) for mask, piece in enumerate(far_out)]
    (near_out,) = serve(near_sources, [columns * near_cap], me, asked_block, passages)
    near_blocks = lax.all_to_all(near_out, "dp", split_axis=0, concat_axis=0, tiled=True)

    my_lists = lax.dynamic_slice_in_dim(candidates, device * query_blocks, query_blocks, 0)
    my_places = jnp.take(owner_map, my_lists)
    place = jnp.arange(devices * blocks, dtype=jnp.int32).reshape(devices, blocks)
    wanted = jnp.max(
        jnp.where(
            my_places[None, :, None, :] == place[:, None, :, None], number, -1
        ),
        axis=3,
    )
    _, my_entry = slot_table(wanted, cap)

    slots = columns * near_cap + (groups - 1) * far_cap
    flops = 2 * rows * slots * block_rows * width
    stat = call(
        functools.partial(stats_kernel, scale, cap, columns, groups),
        jax.ShapeDtypeStruct((8, rows), jnp.float32),
        [
            pltpu.VMEM((slots, rows, block_rows), jnp.float32),
            pltpu.VMEM((rows, block_rows), jnp.float32),
        ],
        flops,
        [me, my_entry],
        [queries, row_weight, positives, near_blocks, *far_blocks],
    )
    pair = jnp.stack([stat, swap(stat, "dp", 1)])
    near_stats = [pair] + [swap(pair, "dp", mask) for mask in range(2, columns, 2)]
    far_stats = [swap(stat, "group", mask) for mask in range(1, groups)]
    grad_query = call(
        functools.partial(query_kernel, scale, cap, columns, groups),
        jax.ShapeDtypeStruct(queries.shape, queries.dtype),
        [
            pltpu.VMEM((rows, width), jnp.float32),
            pltpu.VMEM((rows, cap * block_rows), jnp.bfloat16),
        ],
        2 * flops,
        [me, my_entry],
        [queries, stat, near_blocks, *far_blocks],
    )
    grad_passage = call(
        functools.partial(passage_kernel, scale, cap, near_cap, far_cap, columns, groups),
        jax.ShapeDtypeStruct(passages.shape, passages.dtype),
        [pltpu.VMEM(passages.shape, jnp.float32)],
        2 * flops,
        [me, asked_block, asked_entry],
        [passages, even, odd, *far_queries, *near_stats, *far_stats],
    )
    return (grad_query, grad_passage)


def solution(mesh):
    return jax.shard_map(
        shards,
        mesh=mesh,
        in_specs=(
            P(("group", "dp"), None, None),
            P(("group", "dp"), None, None),
            P(),
            P(("group", "dp"), None),
            P(("group", "dp"), None),
            P(),
        ),
        out_specs=(P(("group", "dp"), None, None), P(("group", "dp"), None, None)),
        check_vma=False,
    )
```

time: 178 us -> 114 us (0.64)
  other arithmetic: 35.6 us -> 3.27 us
  local copies, waits for them, and re-layouts: 31.8 us -> 5.45 us
  waiting for transfers between devices: 73.2 us -> 53.3 us
  Pallas kernels: 0 us -> 17.1 us
  matrix products: 15.8 us -> 0 us
  starting transfers between devices: 18.9 us -> 33.6 us
    all_to_all x4 -> x1, waiting for transfers between devices: 73.2 us -> 0.01 us  [shards(): lax.all_to_all(near_out, 'dp', split_axis=0, concat_axis=0, tiled=True)]
    ppermute x0 -> x18, waiting for transfers between devices: none -> 53.3 us  [swap(): return lax.ppermute(x, axis, [(i, i ^ mask) for i in range(size)])]
    ppermute x0 -> x18, starting transfers between devices: none -> 28.3 us  [swap(): return lax.ppermute(x, axis, [(i, i ^ mask) for i in range(size)])]
    scatter-add x2 -> x0, other arithmetic: 19.4 us -> none  [add_block(): return totals.at[slot_grid[index]].add(block_terms)]
    pallas_call x0 -> x5, Pallas kernels: none -> 17.1 us  [the longest x3 11.6 us: call(): pl.pallas_call(kernel, out_shape=out, in_specs=[pl.BlockSpec(memory_space...]
    dot_general x7 -> x0, matrix products: 15.8 us -> none  [the longest x2 5.45 us: add_block(): jnp.einsum('rkj,rd->kjd', dscore[index], queries[index], preferred_elemen...]
    all_to_all x4 -> x1, starting transfers between devices: 18.9 us -> 5.3 us  [shards(): lax.all_to_all(near_out, 'dp', split_axis=0, concat_axis=0, tiled=True)]
    gather x14 -> x2, local copies, waits for them, and re-layouts: 14.1 us -> 1.47 us  [shards(): my_places = jnp.take(owner_map, my_lists)]
  transfers between devices with their start and end apart: 4 -> 19, of which waited for: 4 -> 5; matrix products, arithmetic and copies ran while one was open for 15% -> 1% of each run, Pallas kernels for 0% -> 7%
where the time goes in v1:
time: 114 us
  waiting for transfers between devices  53.3 us (47%)
  starting transfers between devices  33.6 us (29%)
  Pallas kernels  17.1 us (15%)
  local copies, waits for them, and re-layouts  5.45 us (5%)
  other arithmetic  3.27 us (3%)
    ppermute x18, waiting for transfers between devices, swap(): return lax.ppermute(x, axis, [(i, i ^ mask) for i in range(size)])  53.3 us
    ppermute x18, starting transfers between devices, swap(): return lax.ppermute(x, axis, [(i, i ^ mask) for i in range(size)])  28.3 us
    pallas_call x3, Pallas kernels, call(): pl.pallas_call(kernel, out_shape=out, in_specs=[pl.BlockSpec(memory_space...  11.6 us
    pallas_call x2, Pallas kernels, serve(): pl.pallas_call(functools.partial(serve_kernel, sources), out_shape=[jax.S...  5.44 us
    all_to_all x1, starting transfers between devices, shards(): lax.all_to_all(near_out, 'dp', split_axis=0, concat_axis=0, tiled=True)  5.3 us
    unnamed x14, local copies, waits for them, and re-layouts  2.65 us
  transfers between devices with their start and end apart: 19, of which 5 were waited for; matrix products, arithmetic and copies ran while one was open for 1% of the time, Pallas kernels for 7%

profile of v1, /device:TPU:0, one launch (start us, length us, event | category | flops | bytes accessed | tf_op | source)
XLA Modules:
  0.0 113.5 jit_solution(16493963885023432739)
XLA Ops:
  3.5 1.4 %gather_fusion = s32[32]{0:T(128)S(1)} fusion(s32[192]{0:T(256)} %param.11, s32[1024]{0:T(1024)S(1)} %pad_clamp_fusion), kind=kCustom, calls=%fused_computation | custom fusion | bytes 384 | tf_op jit(solution)/shard_map/jit(_take)/gather | solution.py:312
  5.4 1.1 copy-done.1
  6.6 3.7 %shard_map.77 = bf16[16,128,512]{2,1,0:T(8,128)(2,1)S(1)} custom-call(s32[2]{0:T(128)S(1)} %pad_add_fusion.me, s32[32,2]{1,0:T(8,128)S(1)} %copy.30.block, bf16[6,128,512]{2,1,0:T(8,128)(2,1)S(1)} %copy-done.1), custom_call_target="tpu_custom_call" | custom-call | tf_op jit(solution)/shard_map/pallas_call | solution.py:53
  10.3 1.3 %copy-done = bf16[16,128,512]{2,1,0:T(8,128)(2,1)} copy-done((bf16[16,128,512]{2,1,0:T(8,128)(2,1)}, bf16[16,128,512]{2,1,0:T(8,128)(2,1)S(1)}, u32[]{:S(2)}) %copy-start) | copy-done | bytes 2097176
  11.6 5.3 %all-to-all-start = ((bf16[16,128,512]{2,1,0:T(8,128)(2,1)}), bf16[16,128,512]{2,1,0:T(8,128)(2,1)S(1)}, u32[]{:S(2)}, u32[]{:S(2)}) async-start(bf16[16,128,512]{2,1,0:T(8,128)(2,1)} %copy-done), calls=%async_computation | async-start | bytes 4194304 | tf_op jit(solution)/shard_map/all_to_all | solution.py:309
  17.0 2.1 %collective-permute-start.4 = (bf16[2,128,512]{2,1,0:T(8,128)(2,1)S(1)}, bf16[2,128,512]{2,1,0:T(8,128)(2,1)S(1)}, u32[]{:S(2)}, u32[]{:S(2)}) collective-permute-start(bf16[2,128,512]{2,1,0:T(8,128)(2,1)S(1)} %copy-done.3), channel_id=1, source_target_pairs={{0,4},{1,5},{2,6},{3,7},{4,0},{5,1},{6,2},{7,3},{8,12},{9,13},{10,... | collective-permute-start | bytes 786440 | tf_op jit(solution)/shard_map/ppermute | solution.py:17
  19.0 1.5 %collective-permute-start.3 = (bf16[2,128,512]{2,1,0:T(8,128)(2,1)S(1)}, bf16[2,128,512]{2,1,0:T(8,128)(2,1)S(1)}, u32[]{:S(2)}, u32[]{:S(2)}) collective-permute-start(bf16[2,128,512]{2,1,0:T(8,128)(2,1)S(1)} %copy-done.3), channel_id=1, source_target_pairs={{0,2},{1,3},{2,0},{3,1},{4,6},{5,7},{6,4},{7,5},{8,10},{9,11},{10,... | collective-permute-start | bytes 786440 | tf_op jit(solution)/shard_map/ppermute | solution.py:17
  20.5 27.7 %collective-permute-done.4 = bf16[2,128,512]{2,1,0:T(8,128)(2,1)S(1)} collective-permute-done((bf16[2,128,512]{2,1,0:T(8,128)(2,1)S(1)}, bf16[2,128,512]{2,1,0:T(8,128)(2,1)S(1)}, u32[]{:S(2)}, u32[]{:S(2)}) %collective-permute-start.4) | collective-permute-done | bytes 262176 | tf_op jit(solution)/shard_map/ppermute | solution.py:17
  48.3 1.5 %collective-permute-start.6 = (bf16[1,128,512]{2,1,0:T(8,128)(2,1)S(1)}, bf16[1,128,512]{2,1,0:T(8,128)(2,1)S(1)}, u32[]{:S(2)}, u32[]{:S(2)}) collective-permute-start(bf16[1,128,512]{2,1,0:T(8,128)(2,1)S(1)} %slice.11), channel_id=1, source_target_pairs={{0,2},{1,3},{2,0},{3,1},{4,6},{5,7},{6,4},{7,5},{8,10},{9,11},{10,... | collective-permute-start | bytes 393224 | tf_op jit(solution)/shard_map/ppermute | solution.py:17
  50.2 3.3 %collective-permute-done.6 = bf16[1,128,512]{2,1,0:T(8,128)(2,1)S(1)} collective-permute-done((bf16[1,128,512]{2,1,0:T(8,128)(2,1)S(1)}, bf16[1,128,512]{2,1,0:T(8,128)(2,1)S(1)}, u32[]{:S(2)}, u32[]{:S(2)}) %collective-permute-start.6) | collective-permute-done | bytes 131104 | tf_op jit(solution)/shard_map/ppermute | solution.py:17
  53.5 1.5 %collective-permute-done.5 = bf16[1,128,512]{2,1,0:T(8,128)(2,1)S(1)} collective-permute-done((bf16[1,128,512]{2,1,0:T(8,128)(2,1)S(1)}, bf16[1,128,512]{2,1,0:T(8,128)(2,1)S(1)}, u32[]{:S(2)}, u32[]{:S(2)}) %collective-permute-start.5) | collective-permute-done | bytes 131104 | tf_op jit(solution)/shard_map/ppermute | solution.py:17
  55.1 1.1 pad_maximum_fusion.even
  56.2 3.6 %collective-permute-start.9 = (bf16[2,128,512]{2,1,0:T(8,128)(2,1)S(1)}, bf16[2,128,512]{2,1,0:T(8,128)(2,1)}, u32[]{:S(2)}, u32[]{:S(2)}) collective-permute-start(bf16[2,128,512]{2,1,0:T(8,128)(2,1)S(1)} %copy-done.3), channel_id=1, source_target_pairs={{0,24},{8,16},{16,8},{24,0},{1,25},{9,17},{17,9},{25,1},{2,26},{10... | collective-permute-start | bytes 786440 | tf_op jit(solution)/shard_map/ppermute | solution.py:17
  59.8 1.7 %shard_map.78 = (bf16[2,128,512]{2,1,0:T(8,128)(2,1)}, bf16[2,128,512]{2,1,0:T(8,128)(2,1)}, bf16[2,128,512]{2,1,0:T(8,128)(2,1)}) custom-call(s32[2]{0:T(128)S(1)} %pad_add_fusion.me, s32[32,2]{1,0:T(8,128)S(1)} %copy.30.block, bf16[6,128,512]{2,1,0:T(8,128)(2,1)S(1)} %copy-done.2), custom_call_target="tpu_custom_call" | custom-call | tf_op jit(solution)/shard_map/pallas_call | solution.py:53
  62.4 3.6 %collective-permute-start.2 = (bf16[2,128,512]{2,1,0:T(8,128)(2,1)}, bf16[2,128,512]{2,1,0:T(8,128)(2,1)}, u32[]{:S(2)}, u32[]{:S(2)}) collective-permute-start(bf16[2,128,512]{2,1,0:T(8,128)(2,1)} %get-tuple-element.7), channel_id=1, source_target_pairs={{0,24},{8,16},{16,8},{24,0},{1,25},{9,17},{17,9},{25,1},{2,26},{10... | collective-permute-start | bytes 786440 | tf_op jit(solution)/shard_map/ppermute | solution.py:17
  66.2 7.3 %collective-permute-done.rest_0_ = bf16[2,128,512]{2,1,0:T(8,128)(2,1)S(1)} collective-permute-done((bf16[2,128,512]{2,1,0:T(8,128)(2,1)}, bf16[2,128,512]{2,1,0:T(8,128)(2,1)S(1)}, u32[]{:S(2)}, u32[]{:S(2)}) %collective-permute-start) | collective-permute-done | bytes 262176 | tf_op jit(solution)/shard_map/ppermute | solution.py:17
  75.5 13.4 %collective-permute-done.1.rest_1_ = bf16[2,128,512]{2,1,0:T(8,128)(2,1)} collective-permute-done((bf16[2,128,512]{2,1,0:T(8,128)(2,1)}, bf16[2,128,512]{2,1,0:T(8,128)(2,1)}, u32[]{:S(2)}, u32[]{:S(2)}) %collective-permute-start.1) | collective-permute-done | bytes 262176 | tf_op jit(solution)/shard_map/ppermute | solution.py:17
  89.0 2.5 %shard_map.79.stat = f32[8,256]{1,0:T(8,128)S(1)} custom-call(s32[2]{0:T(128)S(1)} %pad_add_fusion.me, s32[32,4]{1,0:T(8,128)S(1)} %copy.33.entry, bf16[2,128,512]{2,1,0:T(8,128)(2,1)S(1)} %copy-done.3, f32[2,128]{1,0:T(2,128)S(1)} %copy-done.4, s32[2,128]{1,0:T(2,128)S(1)} %copy-done.5, bf16[16,128,512]{2,1,0:T(8,128)(2,1)S(1)} %all-to-all-done.near, ...), custom_call_target="tpu_custom_call" | custom-call | flops 738197504 | bytes 3147776 | tf_op jit(solution)/shard_map/pallas_call | solution.py:215
  91.7 5.8 %collective-permute-start.15 = (f32[8,256]{1,0:T(8,128)S(1)}, f32[8,256]{1,0:T(8,128)S(1)}, u32[]{:S(2)}, u32[]{:S(2)}) collective-permute-start(f32[8,256]{1,0:T(8,128)S(1)} %shard_map.79.stat), channel_id=1, source_target_pairs={{0,8},{8,0},{16,24},{24,16},{1,9},{9,1},{17,25},{25,17},{2,10},{10... | collective-permute-start | bytes 24584 | tf_op jit(solution)/shard_map/ppermute | solution.py:17
  97.4 2.1 %collective-permute-start.16 = (f32[8,256]{1,0:T(8,128)S(1)}, f32[8,256]{1,0:T(8,128)S(1)}, u32[]{:S(2)}, u32[]{:S(2)}) collective-permute-start(f32[8,256]{1,0:T(8,128)S(1)} %shard_map.79.stat), channel_id=1, source_target_pairs={{0,16},{8,24},{16,0},{24,8},{1,17},{9,25},{17,1},{25,9},{2,18},{10... | collective-permute-start | bytes 24584 | tf_op jit(solution)/shard_map/ppermute | solution.py:17
  99.6 1.3 %collective-permute-start.17 = (f32[8,256]{1,0:T(8,128)S(1)}, f32[8,256]{1,0:T(8,128)S(1)}, u32[]{:S(2)}, u32[]{:S(2)}) collective-permute-start(f32[8,256]{1,0:T(8,128)S(1)} %shard_map.79.stat), channel_id=1, source_target_pairs={{0,24},{8,16},{16,8},{24,0},{1,25},{9,17},{17,9},{25,1},{2,26},{10... | collective-permute-start | bytes 24584 | tf_op jit(solution)/shard_map/ppermute | solution.py:17
  101.7 2.7 %collective-permute-start.14 = (f32[2,8,256]{2,1,0:T(8,128)S(1)}, f32[2,8,256]{2,1,0:T(8,128)S(1)}, u32[]{:S(2)}, u32[]{:S(2)}) collective-permute-start(f32[2,8,256]{2,1,0:T(8,128)S(1)} %pad_maximum_fusion.1.rest_3_), channel_id=1, source_target_pairs={{0,6},{1,7},{2,4},{3,5},{4,2},{5,3},{6,0},{7,1},{8,14},{9,15},{10,... | collective-permute-start | bytes 49160 | tf_op jit(solution)/shard_map/ppermute | solution.py:17
  104.4 4.0 %shard_map.80 = bf16[2,128,512]{2,1,0:T(8,128)(2,1)} custom-call(s32[2]{0:T(128)S(1)} %pad_add_fusion.me, s32[32,4]{1,0:T(8,128)S(1)} %copy.33.entry, bf16[2,128,512]{2,1,0:T(8,128)(2,1)S(1)} %copy-done.3, f32[8,256]{1,0:T(8,128)S(1)} %shard_map.79.stat, bf16[16,128,512]{2,1,0:T(8,128)(2,1)S(1)} %all-to-all-done.near, ...), custom_call_target="tpu_custom_call" | custom-call | flops 1476395008 | bytes 3153920 | tf_op jit(solution)/shard_map/pallas_call | solution.py:215
  108.4 5.1 %shard_map.81 = bf16[6,128,512]{2,1,0:T(8,128)(2,1)} custom-call(s32[2]{0:T(128)S(1)} %pad_add_fusion.me, s32[32,2]{1,0:T(8,128)S(1)} %copy.30.block, s32[32,4]{1,0:T(8,128)S(1)} %copy.36.entry, bf16[6,128,512]{2,1,0:T(8,128)(2,1)S(1)} %copy-done.2, bf16[4,2,128,512]{3,2,1,0:T(8,128)(2,1)} %pad_maximum_fusion.even, ...), custom_call_target="tpu_custom_call" | custom-call | flops 1476395008 | bytes 3760128 | tf_op jit(solution)/shard_map/pallas_call | solution.py:215
  (64 shorter events, 7.9 us)
Async XLA Ops:
  10.3 1.3 %copy-start = (bf16[16,128,512]{2,1,0:T(8,128)(2,1)}, bf16[16,128,512]{2,1,0:T(8,128)(2,1)S(1)}, u32[]{:S(2)}) copy-start(bf16[16,128,512]{2,1,0:T(8,128)(2,1)S(1)} %shard_map.77) | copy-start | bytes 6291460
  11.6 5.3 %copy-start.3 = (bf16[2,128,512]{2,1,0:T(8,128)(2,1)S(1)}, bf16[2,128,512]{2,1,0:T(8,128)(2,1)}, u32[]{:S(2)}) copy-start(bf16[2,128,512]{2,1,0:T(8,128)(2,1)} %queries.3) | copy-start | bytes 786436
  11.6 77.3 %all-to-all-start = ((bf16[16,128,512]{2,1,0:T(8,128)(2,1)}), bf16[16,128,512]{2,1,0:T(8,128)(2,1)S(1)}, u32[]{:S(2)}, u32[]{:S(2)}) async-start(bf16[16,128,512]{2,1,0:T(8,128)(2,1)} %copy-done), calls=%async_computation | async-start | bytes 4194304 | tf_op jit(solution)/shard_map/all_to_all | solution.py:309
  16.9 42.9 %copy-start.2 = (bf16[6,128,512]{2,1,0:T(8,128)(2,1)S(1)}, bf16[6,128,512]{2,1,0:T(8,128)(2,1)}, u32[]{:S(2)}) copy-start(bf16[6,128,512]{2,1,0:T(8,128)(2,1)} %passages.5) | copy-start | bytes 2359300
  16.9 72.0 %copy-start.4 = (f32[2,128]{1,0:T(2,128)S(1)}, f32[2,128]{1,0:T(2,128)}, u32[]{:S(2)}) copy-start(f32[2,128]{1,0:T(2,128)} %weight.1) | copy-start | bytes 3076
  17.0 72.0 %copy-start.5 = (s32[2,128]{1,0:T(2,128)S(1)}, s32[2,128]{1,0:T(2,128)}, u32[]{:S(2)}) copy-start(s32[2,128]{1,0:T(2,128)} %positives.1) | copy-start | bytes 3076
  17.0 31.3 %collective-permute-start.4 = (bf16[2,128,512]{2,1,0:T(8,128)(2,1)S(1)}, bf16[2,128,512]{2,1,0:T(8,128)(2,1)S(1)}, u32[]{:S(2)}, u32[]{:S(2)}) collective-permute-start(bf16[2,128,512]{2,1,0:T(8,128)(2,1)S(1)} %copy-done.3), channel_id=1, source_target_pairs={{0,4},{1,5},{2,6},{3,7},{4,0},{5,1},{6,2},{7,3},{8,12},{9,13},{10,... | collective-permute-start | bytes 786440 | tf_op jit(solution)/shard_map/ppermute | solution.py:17
  19.0 30.7 %collective-permute-start.3 = (bf16[2,128,512]{2,1,0:T(8,128)(2,1)S(1)}, bf16[2,128,512]{2,1,0:T(8,128)(2,1)S(1)}, u32[]{:S(2)}, u32[]{:S(2)}) collective-permute-start(bf16[2,128,512]{2,1,0:T(8,128)(2,1)S(1)} %copy-done.3), channel_id=1, source_target_pairs={{0,2},{1,3},{2,0},{3,1},{4,6},{5,7},{6,4},{7,5},{8,10},{9,11},{10,... | collective-permute-start | bytes 786440 | tf_op jit(solution)/shard_map/ppermute | solution.py:17
  48.3 5.3 %collective-permute-start.6 = (bf16[1,128,512]{2,1,0:T(8,128)(2,1)S(1)}, bf16[1,128,512]{2,1,0:T(8,128)(2,1)S(1)}, u32[]{:S(2)}, u32[]{:S(2)}) collective-permute-start(bf16[1,128,512]{2,1,0:T(8,128)(2,1)S(1)} %slice.11), channel_id=1, source_target_pairs={{0,2},{1,3},{2,0},{3,1},{4,6},{5,7},{6,4},{7,5},{8,10},{9,11},{10,... | collective-permute-start | bytes 393224 | tf_op jit(solution)/shard_map/ppermute | solution.py:17
  49.8 5.3 %collective-permute-start.5 = (bf16[1,128,512]{2,1,0:T(8,128)(2,1)S(1)}, bf16[1,128,512]{2,1,0:T(8,128)(2,1)S(1)}, u32[]{:S(2)}, u32[]{:S(2)}) collective-permute-start(bf16[1,128,512]{2,1,0:T(8,128)(2,1)S(1)} %slice.10), channel_id=1, source_target_pairs={{0,4},{1,5},{2,6},{3,7},{4,0},{5,1},{6,2},{7,3},{8,12},{9,13},{10,... | collective-permute-start | bytes 393224 | tf_op jit(solution)/shard_map/ppermute | solution.py:17
  56.2 45.0 %collective-permute-start.7 = (bf16[4,2,128,512]{3,2,1,0:T(8,128)(2,1)}, bf16[4,2,128,512]{3,2,1,0:T(8,128)(2,1)}, u32[]{:S(2)}, u32[]{:S(2)}) collective-permute-start(bf16[4,2,128,512]{3,2,1,0:T(8,128)(2,1)} %pad_maximum_fusion.even), channel_id=1, source_target_pairs={{0,1},{1,0},{2,3},{3,2},{4,5},{5,4},{6,7},{7,6},{8,9},{9,8},{10,11... | collective-permute-start | bytes 3145736 | tf_op jit(solution)/shard_map/ppermute | solution.py:17
  56.2 18.4 %collective-permute-start.9 = (bf16[2,128,512]{2,1,0:T(8,128)(2,1)S(1)}, bf16[2,128,512]{2,1,0:T(8,128)(2,1)}, u32[]{:S(2)}, u32[]{:S(2)}) collective-permute-start(bf16[2,128,512]{2,1,0:T(8,128)(2,1)S(1)} %copy-done.3), channel_id=1, source_target_pairs={{0,24},{8,16},{16,8},{24,0},{1,25},{9,17},{17,9},{25,1},{2,26},{10... | collective-permute-start | bytes 786440 | tf_op jit(solution)/shard_map/ppermute | solution.py:17
  61.6 11.9 %collective-permute-start = (bf16[2,128,512]{2,1,0:T(8,128)(2,1)}, bf16[2,128,512]{2,1,0:T(8,128)(2,1)S(1)}, u32[]{:S(2)}, u32[]{:S(2)}) collective-permute-start(bf16[2,128,512]{2,1,0:T(8,128)(2,1)} %get-tuple-element.5), channel_id=1, source_target_pairs={{0,8},{8,0},{16,24},{24,16},{1,9},{9,1},{17,25},{25,17},{2,10},{10... | collective-permute-start | bytes 786440 | tf_op jit(solution)/shard_map/ppermute | solution.py:17
  61.6 27.3 %collective-permute-start.1 = (bf16[2,128,512]{2,1,0:T(8,128)(2,1)}, bf16[2,128,512]{2,1,0:T(8,128)(2,1)}, u32[]{:S(2)}, u32[]{:S(2)}) collective-permute-start(bf16[2,128,512]{2,1,0:T(8,128)(2,1)} %get-tuple-element.6), channel_id=1, source_target_pairs={{0,16},{8,24},{16,0},{24,8},{1,17},{9,25},{17,1},{25,9},{2,18},{10... | collective-permute-start | bytes 786440 | tf_op jit(solution)/shard_map/ppermute | solution.py:17
  62.4 26.5 %collective-permute-start.2 = (bf16[2,128,512]{2,1,0:T(8,128)(2,1)}, bf16[2,128,512]{2,1,0:T(8,128)(2,1)}, u32[]{:S(2)}, u32[]{:S(2)}) collective-permute-start(bf16[2,128,512]{2,1,0:T(8,128)(2,1)} %get-tuple-element.7), channel_id=1, source_target_pairs={{0,24},{8,16},{16,8},{24,0},{1,25},{9,17},{17,9},{25,1},{2,26},{10... | collective-permute-start | bytes 786440 | tf_op jit(solution)/shard_map/ppermute | solution.py:17
  73.5 26.1 %collective-permute-start.8 = (bf16[2,128,512]{2,1,0:T(8,128)(2,1)S(1)}, bf16[2,128,512]{2,1,0:T(8,128)(2,1)}, u32[]{:S(2)}, u32[]{:S(2)}) collective-permute-start(bf16[2,128,512]{2,1,0:T(8,128)(2,1)S(1)} %copy-done.3), channel_id=1, source_target_pairs={{0,8},{8,0},{16,24},{24,16},{1,9},{9,1},{17,25},{25,17},{2,10},{10... | collective-permute-start | bytes 786440 | tf_op jit(solution)/shard_map/ppermute | solution.py:17
  74.6 26.2 %collective-permute-start.10 = (bf16[2,128,512]{2,1,0:T(8,128)(2,1)}, bf16[2,128,512]{2,1,0:T(8,128)(2,1)}, u32[]{:S(2)}, u32[]{:S(2)}) collective-permute-start(bf16[2,128,512]{2,1,0:T(8,128)(2,1)} %collective-permute-done.9.rest_2_), channel_id=1, source_target_pairs={{0,8},{8,0},{16,24},{24,16},{1,9},{9,1},{17,25},{25,17},{2,10},{10... | collective-permute-start | bytes 786440 | tf_op jit(solution)/shard_map/ppermute | solution.py:17
  91.5 5.9 %collective-permute-start.11 = (f32[8,256]{1,0:T(8,128)S(1)}, f32[8,256]{1,0:T(8,128)S(1)}, u32[]{:S(2)}, u32[]{:S(2)}) collective-permute-start(f32[8,256]{1,0:T(8,128)S(1)} %shard_map.79.stat), channel_id=1, source_target_pairs={{0,1},{1,0},{2,3},{3,2},{4,5},{5,4},{6,7},{7,6},{8,9},{9,8},{10,11... | collective-permute-start | bytes 24584 | tf_op jit(solution)/shard_map/ppermute | solution.py:17
  91.7 10.0 %collective-permute-start.15 = (f32[8,256]{1,0:T(8,128)S(1)}, f32[8,256]{1,0:T(8,128)S(1)}, u32[]{:S(2)}, u32[]{:S(2)}) collective-permute-start(f32[8,256]{1,0:T(8,128)S(1)} %shard_map.79.stat), channel_id=1, source_target_pairs={{0,8},{8,0},{16,24},{24,16},{1,9},{9,1},{17,25},{25,17},{2,10},{10... | collective-permute-start | bytes 24584 | tf_op jit(solution)/shard_map/ppermute | solution.py:17
  97.4 10.9 %collective-permute-start.16 = (f32[8,256]{1,0:T(8,128)S(1)}, f32[8,256]{1,0:T(8,128)S(1)}, u32[]{:S(2)}, u32[]{:S(2)}) collective-permute-start(f32[8,256]{1,0:T(8,128)S(1)} %shard_map.79.stat), channel_id=1, source_target_pairs={{0,16},{8,24},{16,0},{24,8},{1,17},{9,25},{17,1},{25,9},{2,18},{10... | collective-permute-start | bytes 24584 | tf_op jit(solution)/shard_map/ppermute | solution.py:17
  99.6 8.8 %collective-permute-start.17 = (f32[8,256]{1,0:T(8,128)S(1)}, f32[8,256]{1,0:T(8,128)S(1)}, u32[]{:S(2)}, u32[]{:S(2)}) collective-permute-start(f32[8,256]{1,0:T(8,128)S(1)} %shard_map.79.stat), channel_id=1, source_target_pairs={{0,24},{8,16},{16,8},{24,0},{1,25},{9,17},{17,9},{25,1},{2,26},{10... | collective-permute-start | bytes 24584 | tf_op jit(solution)/shard_map/ppermute | solution.py:17
  100.9 7.5 %collective-permute-start.12 = (f32[2,8,256]{2,1,0:T(8,128)S(1)}, f32[2,8,256]{2,1,0:T(8,128)S(1)}, u32[]{:S(2)}, u32[]{:S(2)}) collective-permute-start(f32[2,8,256]{2,1,0:T(8,128)S(1)} %pad_maximum_fusion.1.rest_3_), channel_id=1, source_target_pairs={{0,2},{1,3},{2,0},{3,1},{4,6},{5,7},{6,4},{7,5},{8,10},{9,11},{10,... | collective-permute-start | bytes 49160 | tf_op jit(solution)/shard_map/ppermute | solution.py:17
  101.2 7.2 %collective-permute-start.13 = (f32[2,8,256]{2,1,0:T(8,128)S(1)}, f32[2,8,256]{2,1,0:T(8,128)S(1)}, u32[]{:S(2)}, u32[]{:S(2)}) collective-permute-start(f32[2,8,256]{2,1,0:T(8,128)S(1)} %pad_maximum_fusion.1.rest_3_), channel_id=1, source_target_pairs={{0,4},{1,5},{2,6},{3,7},{4,0},{5,1},{6,2},{7,3},{8,12},{9,13},{10,... | collective-permute-start | bytes 49160 | tf_op jit(solution)/shard_map/ppermute | solution.py:17
  101.7 6.7 %collective-permute-start.14 = (f32[2,8,256]{2,1,0:T(8,128)S(1)}, f32[2,8,256]{2,1,0:T(8,128)S(1)}, u32[]{:S(2)}, u32[]{:S(2)}) collective-permute-start(f32[2,8,256]{2,1,0:T(8,128)S(1)} %pad_maximum_fusion.1.rest_3_), channel_id=1, source_target_pairs={{0,6},{1,7},{2,4},{3,5},{4,2},{5,3},{6,0},{7,1},{8,14},{9,15},{10,... | collective-permute-start | bytes 49160 | tf_op jit(solution)/shard_map/ppermute | solution.py:17
  (1 other events, 1.1 us)

commit v2 on v1

v2 whole, which is shorter than its diff:
```python
import functools
import math

import jax
import jax.numpy as jnp
from jax import lax
from jax.experimental import pallas as pl
from jax.experimental.pallas import tpu as pltpu
from jax.sharding import PartitionSpec as P

NLOCAL = 12
VMEM_BYTES = 32 * 1024 * 1024
PLAN_VMEM_BYTES = 60 * 1024 * 1024
PLAN_BYTES = 16 * 1024 * 1024
NEAR_BYTES = 64 * 1024 * 1024


def swap(x, axis, mask):
    size = lax.axis_size(axis)
    return lax.ppermute(x, axis, [(i, i ^ mask) for i in range(size)])


def local_call(kernel, tables, inputs, outs, scratch, cost):
    smem = pl.BlockSpec(memory_space=pltpu.SMEM)
    vmem = pl.BlockSpec(memory_space=pltpu.VMEM)
    return pl.pallas_call(
        kernel,
        out_shape=outs,
        in_specs=[smem] * len(tables) + [vmem] * len(inputs),
        out_specs=jax.tree.map(lambda _: vmem, outs),
        scratch_shapes=scratch,
        compiler_params=pltpu.CompilerParams(vmem_limit_bytes=VMEM_BYTES),
        cost_estimate=pl.CostEstimate(flops=0, bytes_accessed=cost, transcendentals=0),
    )(*tables, *inputs)


def start_all(pairs, sems):
    copies = [
        pltpu.make_async_copy(source, target, sems.at[index])
        for index, (source, target) in enumerate(pairs)
    ]
    for copy in copies:
        copy.start()
    return copies


def owners_of(columns, groups):
    group, column = lax.axis_index("group"), lax.axis_index("dp")
    near = [group * columns + (column ^ mask) for mask in range(columns)]
    far = [(group ^ mask) * columns + column for mask in range(1, groups)]
    return near, far


def slot_rows(listings, cap, devices_of):
    query_blocks = len(listings[0])
    shape = listings[0][0].shape
    held = [jnp.zeros(shape, jnp.float32) for _ in range(cap)]
    entry = [jnp.full(shape, -1.0, jnp.float32) for _ in range(query_blocks * cap)]
    rank = jnp.zeros(shape, jnp.float32)
    for index, listing in enumerate(listings):
        listed = devices_of(functools.reduce(jnp.maximum, listing) >= 0.0)
        for slot in range(cap):
            here = listed & (rank == slot)
            held[slot] = jnp.where(here, float(index), held[slot])
            for block in range(query_blocks):
                at = block * cap + slot
                entry[at] = jnp.where(here, listing[block], entry[at])
        rank = rank + jnp.where(listed, 1.0, 0.0)
    return held + entry


def write_rows(rows, out):
    out[...] = jnp.zeros_like(out)
    for index, row in enumerate(rows):
        out[index : index + 1] = row.astype(jnp.int32)


def plan_kernel(scale, cap, near_cap, far_cap, columns, groups, query_blocks, *refs):
    lists_in, owners_in, weight_in, positives_in, passages_in = refs[:5]
    fars, (near_out, asked, wanted, row_data) = refs[5 : 4 + groups], refs[4 + groups : 8 + groups]
    lists, owners, weight, positives, passages, scalars, sems, out_sems, scalar_sem = refs[8 + groups :]
    loads = start_all(
        (
            (lists_in, lists),
            (owners_in, owners),
            (passages_in, passages),
            (weight_in, weight),
            (positives_in, positives),
        ),
        sems,
    )
    devices = columns * groups
    blocks = passages.shape[0]
    listed, lanes = lists.shape
    group, column = lax.axis_index("group"), lax.axis_index("dp")
    device = group * columns + column
    loads[0].wait()
    loads[1].wait()
    number = lax.broadcasted_iota(jnp.int32, (listed, lanes), 0).astype(jnp.float32)
    ids = lax.broadcasted_iota(jnp.int32, owners.shape, 1)
    listings = []
    for block in range(blocks):
        here = owners[...] == device * blocks + block
        block_id = jnp.max(jnp.where(here, ids, 0).astype(jnp.float32), axis=1, keepdims=True)
        match = lists[...] == block_id.astype(jnp.int32)
        listings.append([jnp.max(jnp.where(match, number, -1.0), axis=0, keepdims=True)])
    lane = lax.broadcasted_iota(jnp.int32, (1, lanes), 1)
    place_in = lax.rem(lane, query_blocks)

    def of_device(flags):
        value = jnp.where(flags, 1.0, 0.0)
        most = value
        for other in range(1, query_blocks):
            ahead = jnp.concatenate([value[:, other:], value[:, :other]], axis=1)
            behind = jnp.concatenate([value[:, -other:], value[:, :-other]], axis=1)
            most = jnp.maximum(most, jnp.where(place_in + other < query_blocks, ahead, 0.0))
            most = jnp.maximum(most, jnp.where(place_in >= other, behind, 0.0))
        return most > 0.0

    write_rows(slot_rows(listings, cap, of_device), asked)
    to_scalars = pltpu.make_async_copy(asked, scalars, scalar_sem)
    to_scalars.start()
    loads[2].wait()
    to_scalars.wait()
    pairs = []
    near, far = owners_of(columns, groups)
    for out, owner in zip(fars, far):
        for slot in range(far_cap):
            pairs.append((passages.at[scalars[slot, owner * query_blocks]], out.at[slot]))
    for peer in range(columns):
        owner = group * columns + peer
        for slot in range(near_cap):
            source = passages.at[scalars[slot, owner * query_blocks]]
            pairs.append((source, near_out.at[peer * near_cap + slot]))
    copies = start_all(pairs, out_sems)
    lane = lax.broadcasted_iota(jnp.int32, (listed, lanes), 1)
    place = lax.broadcasted_iota(jnp.int32, (listed, owners.shape[1]), 1)
    first = lax.broadcasted_iota(jnp.int32, (listed, devices), 1) * blocks
    number = lax.broadcasted_iota(jnp.int32, (listed, devices), 0).astype(jnp.float32)
    positions = []
    for block in range(query_blocks):
        mine = jnp.where(lane == device * query_blocks + block, lists[...], 0)
        mine = jnp.max(mine.astype(jnp.float32), axis=1, keepdims=True).astype(jnp.int32)
        found = jnp.where(place == mine, owners[...], 0).astype(jnp.float32)
        positions.append(jnp.max(found, axis=1, keepdims=True).astype(jnp.int32))
    listings = [
        [
            jnp.max(jnp.where(position == first + block, number, -1.0), axis=0, keepdims=True)
            for position in positions
        ]
        for block in range(blocks)
    ]
    write_rows(slot_rows(listings, cap, lambda flags: flags)[cap:], wanted)
    loads[3].wait()
    loads[4].wait()
    row_data[...] = jnp.zeros_like(row_data)
    block_rows = weight.shape[1]
    for block in range(query_blocks):
        mine = slice(block * block_rows, (block + 1) * block_rows)
        row_data[2:3, mine] = weight[block : block + 1] * scale
        row_data[3:4, mine] = positives[block : block + 1].astype(jnp.float32)
    for copy in copies:
        copy.wait()


def near_pieces(near, columns):
    group = lax.axis_index("group")
    cap = near.shape[0] // columns
    for peer in range(columns):
        piece = near[peer * cap : (peer + 1) * cap].reshape(-1, near.shape[-1])
        yield group * columns + peer, piece


def far_pieces(fars, columns, groups):
    for ref, holder in zip(fars, owners_of(columns, groups)[1]):
        yield holder, ref[...].reshape(-1, ref.shape[-1])


def block_scores(scale, entry, cap, holder, query, piece, block_rows):
    scores = (
        lax.dot_general(query, piece, (((1,), (1,)), ((), ())), preferred_element_type=jnp.float32)
        * scale
    )
    for block in range(query.shape[0] // block_rows):
        for slot in range(piece.shape[0] // block_rows):
            listing = entry[block * cap + slot, holder]
            bias = jnp.where(listing >= 0, 0.0, -jnp.inf).astype(jnp.float32)
            rows = slice(block * block_rows, (block + 1) * block_rows)
            columns = slice(slot * block_rows, (slot + 1) * block_rows)
            yield block, slot, listing, scores[rows, columns] + bias


def peak_and_total(scale, entry, cap, queries, pieces, scores_ref, peak_ref):
    query_blocks, block_rows, width = queries.shape
    rows = query_blocks * block_rows
    query = queries[...].reshape(rows, width)
    peak_ref[...] = jnp.full_like(peak_ref, -jnp.inf)
    at = 0
    for holder, piece in pieces:
        for block, slot, _, part in block_scores(
            scale, entry, cap, holder, query, piece, block_rows
        ):
            mine = slice(block * block_rows, (block + 1) * block_rows)
            scores_ref[at + slot, mine] = part
            peak_ref[mine] = jnp.maximum(peak_ref[mine], part)
        at += piece.shape[0] // block_rows
    peak = jnp.max(peak_ref[...], axis=1, keepdims=True)
    total = jnp.zeros((rows, block_rows), jnp.float32)
    for index in range(at):
        total = total + jnp.exp(scores_ref[index] - peak)
    return peak, jnp.sum(total, axis=1, keepdims=True)


def near_kernel(scale, cap, columns, wanted, queries, near, out, scores_ref, peak_ref):
    pieces = near_pieces(near, columns)
    peak, total = peak_and_total(scale, wanted, cap, queries, pieces, scores_ref, peak_ref)
    lane = lax.broadcasted_iota(jnp.int32, out.shape, 1)
    out[...] = jnp.where(lane == 0, peak, total)


def stats_kernel(scale, cap, columns, groups, wanted, queries, row_data, near_stat, *refs):
    fars, (stat, scores_ref, peak_ref) = refs[: groups - 1], refs[groups - 1 :]
    pieces = far_pieces(fars, columns, groups)
    far_peak, far_total = peak_and_total(
        scale, wanted, cap, queries, pieces, scores_ref, peak_ref
    )
    near_peak, near_total = near_stat[:, 0:1], near_stat[:, 1:2]
    peak = jnp.maximum(near_peak, far_peak)
    total = near_total * jnp.exp(near_peak - peak) + far_total * jnp.exp(far_peak - peak)
    lane = lax.broadcasted_iota(jnp.int32, (peak.shape[0], 128), 1)
    turned = jnp.where(lane == 0, peak, total).T
    stat[...] = row_data[...]
    stat[0:2] = turned[0:2]


def query_kernel(scale, cap, columns, groups, wanted, queries, stat, near, *refs):
    fars, (out, total, dscore_ref) = refs[: groups - 1], refs[groups - 1 :]
    query_blocks, block_rows, width = queries.shape
    rows = query_blocks * block_rows
    query = queries[...].reshape(rows, width)
    turned = jnp.concatenate(
        [stat[...], jnp.zeros((128 - stat.shape[0], rows), jnp.float32)], axis=0
    ).T
    peak, inverse = turned[:, 0:1], 1.0 / turned[:, 1:2]
    weight, positive = turned[:, 2:3], turned[:, 3:4]
    place = lax.broadcasted_iota(jnp.int32, (block_rows, block_rows), 1)
    total[...] = jnp.zeros_like(total)
    pieces = list(near_pieces(near, columns)) + list(far_pieces(fars, columns, groups))
    for holder, piece in pieces:
        for block, slot, listing, part in block_scores(
            scale, wanted, cap, holder, query, piece, block_rows
        ):
            mine = slice(block * block_rows, (block + 1) * block_rows)
            number = (place + listing * block_rows).astype(jnp.float32)
            target = jnp.where(positive[mine] == number, 1.0, 0.0)
            chance = jnp.exp(part - peak[mine]) * inverse[mine]
            dscore_ref[mine, slot * block_rows : (slot + 1) * block_rows] = (
                (chance - target) * weight[mine]
            ).astype(jnp.bfloat16)
        total[...] += jnp.dot(
            dscore_ref[:, : piece.shape[0]], piece, preferred_element_type=jnp.float32
        )
    out[...] = total[...].reshape(out.shape).astype(out.dtype)


def passage_kernel(scale, cap, near_cap, far_cap, columns, groups, unit_of, counts, *refs):
    asked, passages = refs[:2]
    query_count, stat_count = counts
    queries_in = refs[2 : 2 + query_count]
    stats_in = refs[2 + query_count : 2 + query_count + stat_count]
    out, total = refs[2 + query_count + stat_count :]
    near, far = owners_of(columns, groups)
    units = [(owner, near_cap) for owner in near] + [(owner, far_cap) for owner in far]
    query_blocks, block_rows, width = queries_in[0].shape
    rows = query_blocks * block_rows
    total[...] = jnp.zeros_like(total)
    lane = lax.broadcasted_iota(jnp.int32, (1, rows), 1)
    place = lax.broadcasted_iota(jnp.int32, (block_rows, rows), 0)
    for unit, (owner, slots) in enumerate(units):
        query, stat = unit_of(unit, queries_in, stats_in)
        query = query[...].reshape(rows, width)
        peak, inverse = stat[0:1], 1.0 / stat[1:2]
        weight, positive = stat[2:3], stat[3:4]
        held = [asked[slot, owner * query_blocks] for slot in range(slots)]
        mine = jnp.concatenate([passages[index] for index in held], axis=0)
        scores = (
            lax.dot_general(
                mine, query, (((1,), (1,)), ((), ())), preferred_element_type=jnp.float32
            )
            * scale
        )
        parts = []
        for slot in range(slots):
            listing = jnp.full((1, rows), asked[cap + slot, owner * query_blocks], jnp.int32)
            for block in range(1, query_blocks):
                later = asked[cap + slot, owner * query_blocks + block]
                listing = jnp.where(lane >= block * block_rows, later, listing)
            bias = jnp.where(listing >= 0, 0.0, -jnp.inf)
            number = (place + listing * block_rows).astype(jnp.float32)
            part = scores[slot * block_rows : (slot + 1) * block_rows] + bias
            target = jnp.where(positive == number, 1.0, 0.0)
            chance = jnp.exp(part - peak) * inverse
            parts.append(((chance - target) * weight).astype(jnp.bfloat16))
        term = jnp.dot(
            jnp.concatenate(parts, axis=0), query, preferred_element_type=jnp.float32
        ).astype(jnp.bfloat16)
        for slot, index in enumerate(held):
            total[index] += term[slot * block_rows : (slot + 1) * block_rows].astype(jnp.float32)
    out[...] = total[...].astype(out.dtype)


def shards(queries, passages, candidates, positives, row_weight, owner_map):
    columns = lax.axis_size("dp")
    groups = lax.axis_size("group")
    devices = columns * groups
    query_blocks, block_rows, width = queries.shape
    rows = query_blocks * block_rows
    blocks = passages.shape[0]
    listed = candidates.shape[1]
    near_cap = (NLOCAL + columns - 1) // columns
    far_cap = (listed - NLOCAL + groups - 2) // (groups - 1)
    cap = max(near_cap, far_cap)
    scale = 3.0 / math.sqrt(width)
    dtype = passages.dtype
    slots = columns * near_cap + (groups - 1) * far_cap
    table_rows = -(-(1 + query_blocks) * cap // 8) * 8
    all_lists = devices * query_blocks

    far_queries = {0: queries}
    far_queries[groups - 1] = swap(queries, "group", groups - 1)
    mask = groups // 2 - 1
    if mask:
        far_queries[mask] = swap(queries, "group", mask)
    near_queries = [queries] + [swap(queries, "dp", mask) for mask in range(2, columns, 2)]

    vmem = pl.BlockSpec(memory_space=pltpu.VMEM)
    hbm = pl.BlockSpec(memory_space=pltpu.HBM)
    far_shape = jax.ShapeDtypeStruct((far_cap, block_rows, width), dtype)
    *far_out, near_out, asked, wanted, row_data = pl.pallas_call(
        functools.partial(
            plan_kernel, scale, cap, near_cap, far_cap, columns, groups, query_blocks
        ),
        out_shape=[far_shape] * (groups - 1)
        + [
            jax.ShapeDtypeStruct((columns * near_cap, block_rows, width), dtype),
            jax.ShapeDtypeStruct((table_rows, all_lists), jnp.int32),
            jax.ShapeDtypeStruct((table_rows, devices), jnp.int32),
            jax.ShapeDtypeStruct((8, rows), jnp.float32),
        ],
        in_specs=[hbm] * 5,
        out_specs=[hbm] * groups + [vmem] * 3,
        scratch_shapes=[
            pltpu.VMEM((listed, all_lists), jnp.int32),
            pltpu.VMEM((1, owner_map.shape[0]), jnp.int32),
            pltpu.VMEM(row_weight.shape, jnp.float32),
            pltpu.VMEM(positives.shape, jnp.int32),
            pltpu.VMEM(passages.shape, dtype),
            pltpu.SMEM((table_rows, all_lists), jnp.int32),
            pltpu.SemaphoreType.DMA((5,)),
            pltpu.SemaphoreType.DMA((slots,)),
            pltpu.SemaphoreType.DMA,
        ],
        compiler_params=pltpu.CompilerParams(vmem_limit_bytes=PLAN_VMEM_BYTES),
        cost_estimate=pl.CostEstimate(flops=0, bytes_accessed=PLAN_BYTES, transcendentals=0),
    )(candidates.T, owner_map.reshape(1, -1), row_weight, positives, passages)
    far_out, near_out, near_queries, far_queries = lax.optimization_barrier(
        (far_out, near_out, near_queries, far_queries)
    )
    far_blocks = [swap(far_out[mask - 1], "group", mask) for mask in range(1, groups)]
    near_blocks = lax.all_to_all(near_out, "dp", split_axis=0, concat_axis=0, tiled=True)
    mask = groups // 2 - 1
    while mask:
        for at, piece in list(far_queries.items()):
            if at ^ mask not in far_queries:
                far_queries[at ^ mask] = swap(piece, "group", mask)
        mask >>= 1
    beside = swap(jnp.concatenate(near_queries), "dp", 1)

    near_slots, far_slots = columns * near_cap, (groups - 1) * far_cap
    near_stat = local_call(
        functools.partial(near_kernel, scale, cap, columns),
        [wanted],
        [queries, near_blocks],
        jax.ShapeDtypeStruct((rows, 128), jnp.float32),
        [
            pltpu.VMEM((near_slots, rows, block_rows), jnp.float32),
            pltpu.VMEM((rows, block_rows), jnp.float32),
        ],
        NEAR_BYTES,
    )
    stat = local_call(
        functools.partial(stats_kernel, scale, cap, columns, groups),
        [wanted],
        [queries, row_data, near_stat, *far_blocks],
        jax.ShapeDtypeStruct((8, rows), jnp.float32),
        [
            pltpu.VMEM((far_slots, rows, block_rows), jnp.float32),
            pltpu.VMEM((rows, block_rows), jnp.float32),
        ],
        0,
    )
    pair = jnp.stack([stat, swap(stat, "dp", 1)])
    near_stats = [pair] + [swap(pair, "dp", mask) for mask in range(2, columns, 2)]
    far_stats = [swap(stat, "group", mask) for mask in range(1, groups)]
    grad_query = local_call(
        functools.partial(query_kernel, scale, cap, columns, groups),
        [wanted],
        [queries, stat, near_blocks, *far_blocks],
        jax.ShapeDtypeStruct(queries.shape, dtype),
        [
            pltpu.VMEM((rows, width), jnp.float32),
            pltpu.VMEM((rows, cap * block_rows), dtype),
        ],
        2 * VMEM_BYTES,
    )

    query_inputs = near_queries + [beside] + [far_queries[mask] for mask in range(1, groups)]
    stat_inputs = near_stats + far_stats

    def unit_of(unit, queries_in, stats_in):
        pairs = columns // 2
        if unit >= columns:
            far = unit - columns
            return queries_in[pairs + 1 + far], stats_in[pairs + far]
        stat = stats_in[unit // 2].at[unit % 2]
        if unit % 2 == 0:
            return queries_in[unit // 2], stat
        return queries_in[pairs].at[pl.ds(unit // 2 * query_blocks, query_blocks)], stat

    grad_passage = local_call(
        functools.partial(
            passage_kernel,
            scale,
            cap,
            near_cap,
            far_cap,
            columns,
            groups,
            unit_of,
            (len(query_inputs), len(stat_inputs)),
        ),
        [asked],
        [passages, *query_inputs, *stat_inputs],
        jax.ShapeDtypeStruct(passages.shape, dtype),
        [pltpu.VMEM(passages.shape, jnp.float32)],
        0,
    )
    return (grad_query, grad_passage)


def solution(mesh):
    return jax.shard_map(
        shards,
        mesh=mesh,
        in_specs=(
            P(("group", "dp"), None, None),
            P(("group", "dp"), None, None),
            P(),
            P(("group", "dp"), None),
            P(("group", "dp"), None),
            P(),
        ),
        out_specs=(P(("group", "dp"), None, None), P(("group", "dp"), None, None)),
        check_vma=False,
    )
```

time: 114 us -> 71.8 us (0.63)
  waiting for transfers between devices: 53.3 us -> 26.7 us
  starting transfers between devices: 33.6 us -> 25.5 us
  local copies, waits for them, and re-layouts: 5.45 us -> 0.76 us
  other arithmetic: 3.27 us -> 1.13 us
    ppermute x18 -> x17, waiting for transfers between devices: 53.3 us -> 6.98 us  [swap(): return lax.ppermute(x, axis, [(i, i ^ mask) for i in range(size)])]
    all_to_all x1, waiting for transfers between devices: 0.01 us -> 19.8 us  [shards(): lax.all_to_all(near_out, 'dp', split_axis=0, concat_axis=0, tiled=True)]
    ppermute x18 -> x17, starting transfers between devices: 28.3 us -> 21.7 us  [swap(): return lax.ppermute(x, axis, [(i, i ^ mask) for i in range(size)])]
    unnamed x14 -> x26, local copies, waits for them, and re-layouts: 2.65 us -> 0.76 us
    all_to_all x1, starting transfers between devices: 5.3 us -> 3.73 us  [shards(): lax.all_to_all(near_out, 'dp', split_axis=0, concat_axis=0, tiled=True)]
    gather x2 -> x0, local copies, waits for them, and re-layouts: 1.47 us -> none  [shards(): my_places = jnp.take(owner_map, my_lists)]
    another operation x4 -> x0, other arithmetic: 1.23 us -> none  [the longest x2 1.15 us: gather_columns(): even = jnp.stack([held[mask] for mask in range(0, size, 2)])]
  transfers between devices with their start and end apart: 19 -> 18, of which waited for: 5 -> 6; matrix products, arithmetic and copies ran while one was open for 1% -> 2% of each run, Pallas kernels for 7% -> 17%
where the time goes in v2:
time: 71.8 us; the launch traced here: 71.5 us
  waiting for transfers between devices  26.7 us (37%)
  starting transfers between devices  25.5 us (36%)
  Pallas kernels  16.5 us (23%)
  other arithmetic  1.13 us (2%)
  between operations  0.85 us (1%)
  local copies, waits for them, and re-layouts  0.76 us (1%)
    ppermute x17, starting transfers between devices, swap(): return lax.ppermute(x, axis, [(i, i ^ mask) for i in range(size)])  21.7 us
    all_to_all x1, waiting for transfers between devices, shards(): lax.all_to_all(near_out, 'dp', split_axis=0, concat_axis=0, tiled=True)  19.8 us
    pallas_call x4, Pallas kernels, local_call(): pl.pallas_call(kernel, out_shape=outs, in_specs=[smem] * len(tables) + [v...  12.6 us
    ppermute x17, waiting for transfers between devices, swap(): return lax.ppermute(x, axis, [(i, i ^ mask) for i in range(size)])  6.98 us
    pallas_call x1, Pallas kernels, shards(): pl.pallas_call(functools.partial(plan_kernel, scale, cap, near_cap, far_c...  3.91 us
    all_to_all x1, starting transfers between devices, shards(): lax.all_to_all(near_out, 'dp', split_axis=0, concat_axis=0, tiled=True)  3.73 us
  transfers between devices with their start and end apart: 18, of which 6 were waited for; matrix products, arithmetic and copies ran while one was open for 2% of the time, Pallas kernels for 17%

profile of v2, /device:TPU:0, one launch (start us, length us, event | category | flops | bytes accessed | tf_op | source)
XLA Modules:
  0.0 71.5 jit_solution(15874272494979334594)
XLA Ops:
  0.6 5.1 %collective-permute-start.4 = (bf16[2,128,512]{2,1,0:T(8,128)(2,1)}, bf16[2,128,512]{2,1,0:T(8,128)(2,1)}, u32[]{:S(2)}, u32[]{:S(2)}) collective-permute-start(bf16[2,128,512]{2,1,0:T(8,128)(2,1)} %refs_2_.2), channel_id=1, source_target_pairs={{0,24},{8,16},{16,8},{24,0},{1,25},{9,17},{17,9},{25,1},{2,26},{10... | collective-permute-start | bytes 786440 | tf_op jit(solution)/shard_map/ppermute | solution.py:20
  5.7 2.4 %collective-permute-start.2 = (bf16[2,128,512]{2,1,0:T(8,128)(2,1)}, bf16[2,128,512]{2,1,0:T(8,128)(2,1)S(1)}, u32[]{:S(2)}, u32[]{:S(2)}) collective-permute-start(bf16[2,128,512]{2,1,0:T(8,128)(2,1)} %refs_2_.2), channel_id=1, source_target_pairs={{0,6},{1,7},{2,4},{3,5},{4,2},{5,3},{6,0},{7,1},{8,14},{9,15},{10,... | collective-permute-start | bytes 786440 | tf_op jit(solution)/shard_map/ppermute | solution.py:20
  8.2 0.5 collective-permute-start.1
  8.7 0.5 collective-permute-start
  9.2 3.9 %shard_map.77 = (bf16[2,128,512]{2,1,0:T(8,128)(2,1)}, bf16[2,128,512]{2,1,0:T(8,128)(2,1)}, bf16[2,128,512]{2,1,0:T(8,128)(2,1)}, bf16[16,128,512]{2,1,0:T(8,12...) custom-call(s32[16,64]{1,0:T(8,128)} %bitcast.5, s32[1,192]{1,0:T(1,128)} %bitcast.7, ...), custom_call_target="tpu_custom_call" | custom-call | bytes 16777216 | tf_op jit(solution)/shard_map/pallas_call | solution.py:339
  13.3 4.7 %collective-permute-done.3.refs_7_ = bf16[2,128,512]{2,1,0:T(8,128)(2,1)S(1)} collective-permute-done((bf16[2,128,512]{2,1,0:T(8,128)(2,1)}, bf16[2,128,512]{2,1,0:T(8,128)(2,1)S(1)}, u32[]{:S(2)}, u32[]{:S(2)}) %collective-permute-start.3) | collective-permute-done | bytes 262176 | tf_op jit(solution)/shard_map/ppermute | solution.py:20
  18.0 0.7 copy-done.8
  18.7 1.5 %collective-permute-done.1.refs_4_ = bf16[2,128,512]{2,1,0:T(8,128)(2,1)S(1)} collective-permute-done((bf16[2,128,512]{2,1,0:T(8,128)(2,1)}, bf16[2,128,512]{2,1,0:T(8,128)(2,1)S(1)}, u32[]{:S(2)}, u32[]{:S(2)}) %collective-permute-start.1) | collective-permute-done | bytes 262176 | tf_op jit(solution)/shard_map/ppermute | solution.py:20
  20.3 3.7 %all-to-all-start = ((bf16[16,128,512]{2,1,0:T(8,128)(2,1)}), bf16[16,128,512]{2,1,0:T(8,128)(2,1)S(1)}, u32[]{:S(2)}, u32[]{:S(2)}) async-start(bf16[16,128,512]{2,1,0:T(8,128)(2,1)} %get-tuple-element.25), calls=%async_computation | async-start | bytes 4194304 | tf_op jit(solution)/shard_map/all_to_all | solution.py:370
  24.1 1.1 %pad_maximum_fusion = bf16[8,128,512]{2,1,0:T(8,128)(2,1)} fusion(bf16[2,128,512]{2,1,0:T(8,128)(2,1)S(1)} %collective-permute-done.2.refs_5_, bf16[2,128,512]{2,1,0:T(8,128)(2,1)S(1)} %collective-permute-done.1.refs_4_, bf16[2,128,512]{2,1,0:T(8,128)(2,1)S(1)} %collective-permute-done.refs_3_, bf16[2,128,512]{2,1,0:T(8,128)(2,1)S(1)} %copy-done), kind=kLoop, calls=%fused_computation | loop fusion | flops 1572864 | bytes 2097152 | tf_op jit(solution)/shard_map/concatenate | solution.py:377
  25.7 1.7 %collective-permute-start.5 = (bf16[2,128,512]{2,1,0:T(8,128)(2,1)}, bf16[2,128,512]{2,1,0:T(8,128)(2,1)}, u32[]{:S(2)}, u32[]{:S(2)}) collective-permute-start(bf16[2,128,512]{2,1,0:T(8,128)(2,1)} %get-tuple-element.26), channel_id=1, source_target_pairs={{0,8},{8,0},{16,24},{24,16},{1,9},{9,1},{17,25},{25,17},{2,10},{10... | collective-permute-start | bytes 786440 | tf_op jit(solution)/shard_map/ppermute | solution.py:20
  27.4 2.6 %collective-permute-start.7 = (bf16[2,128,512]{2,1,0:T(8,128)(2,1)}, bf16[2,128,512]{2,1,0:T(8,128)(2,1)}, u32[]{:S(2)}, u32[]{:S(2)}) collective-permute-start(bf16[2,128,512]{2,1,0:T(8,128)(2,1)} %get-tuple-element.28), channel_id=1, source_target_pairs={{0,24},{8,16},{16,8},{24,0},{1,25},{9,17},{17,9},{25,1},{2,26},{10... | collective-permute-start | bytes 786440 | tf_op jit(solution)/shard_map/ppermute | solution.py:20
  30.1 0.8 %collective-permute-start.9 = (bf16[2,128,512]{2,1,0:T(8,128)(2,1)}, bf16[2,128,512]{2,1,0:T(8,128)(2,1)}, u32[]{:S(2)}, u32[]{:S(2)}) collective-permute-start(bf16[2,128,512]{2,1,0:T(8,128)(2,1)} %collective-permute-done.4.refs_9_), channel_id=1, source_target_pairs={{0,8},{8,0},{16,24},{24,16},{1,9},{9,1},{17,25},{25,17},{2,10},{10... | collective-permute-start | bytes 786440 | tf_op jit(solution)/shard_map/ppermute | solution.py:20
  30.9 19.8 %all-to-all-done.near = bf16[16,128,512]{2,1,0:T(8,128)(2,1)S(1)} async-done(((bf16[16,128,512]{2,1,0:T(8,128)(2,1)}), bf16[16,128,512]{2,1,0:T(8,128)(2,1)S(1)}, u32[]{:S(2)}, u32[]{:S(2)}) %all-to-all-start) | async-done | bytes 2097184 | tf_op jit(solution)/shard_map/all_to_all | solution.py:370
  50.7 1.7 %shard_map.78.near_stat = f32[256,128]{1,0:T(8,128)S(1)} custom-call(s32[8,32]{1,0:T(8,128)S(1)} %copy-done.10, bf16[2,128,512]{2,1,0:T(8,128)(2,1)S(1)} %copy-done, bf16[16,128,512]{2,1,0:T(8,128)(2,1)S(1)} %all-to-all-done.near), custom_call_target="tpu_custom_call" | custom-call | bytes 67108864 | tf_op jit(solution)/shard_map/pallas_call | solution.py:26
  52.5 2.4 %shard_map.79.stat = f32[8,256]{1,0:T(8,128)S(1)} custom-call(s32[8,32]{1,0:T(8,128)S(1)} %copy-done.10, bf16[2,128,512]{2,1,0:T(8,128)(2,1)S(1)} %copy-done, f32[8,256]{1,0:T(8,128)S(1)} %copy-done.11, f32[256,128]{1,0:T(8,128)S(1)} %shard_map.78.near_stat, bf16[2,128,512]{2,1,0:T(8,128)(2,1)} %collective-permute-done.5.refs_0_, ...), custom_call_target="tpu_custom_call" | custom-call | tf_op jit(solution)/shard_map/pallas_call | solution.py:26
  54.9 0.7 collective-permute-start.16
  56.1 0.6 collective-permute-start.13
  56.7 1.4 %collective-permute-start.12 = (f32[2,8,256]{2,1,0:T(8,128)S(1)}, f32[2,8,256]{2,1,0:T(8,128)S(1)}, u32[]{:S(2)}, u32[]{:S(2)}) collective-permute-start(f32[2,8,256]{2,1,0:T(8,128)S(1)} %pad_maximum_fusion.1.refs_10_), channel_id=1, source_target_pairs={{0,4},{1,5},{2,6},{3,7},{4,0},{5,1},{6,2},{7,3},{8,12},{9,13},{10,... | collective-permute-start | bytes 49160 | tf_op jit(solution)/shard_map/ppermute | solution.py:20
  58.1 1.5 %collective-permute-start.11 = (f32[2,8,256]{2,1,0:T(8,128)S(1)}, f32[2,8,256]{2,1,0:T(8,128)S(1)}, u32[]{:S(2)}, u32[]{:S(2)}) collective-permute-start(f32[2,8,256]{2,1,0:T(8,128)S(1)} %pad_maximum_fusion.1.refs_10_), channel_id=1, source_target_pairs={{0,2},{1,3},{2,0},{3,1},{4,6},{5,7},{6,4},{7,5},{8,10},{9,11},{10,... | collective-permute-start | bytes 49160 | tf_op jit(solution)/shard_map/ppermute | solution.py:20
  59.6 2.1 %collective-permute-start.15 = (f32[8,256]{1,0:T(8,128)S(1)}, f32[8,256]{1,0:T(8,128)S(1)}, u32[]{:S(2)}, u32[]{:S(2)}) collective-permute-start(f32[8,256]{1,0:T(8,128)S(1)} %shard_map.79.stat), channel_id=1, source_target_pairs={{0,16},{8,24},{16,0},{24,8},{1,17},{9,25},{17,1},{25,9},{2,18},{10... | collective-permute-start | bytes 24584 | tf_op jit(solution)/shard_map/ppermute | solution.py:20
  61.7 1.2 %collective-permute-start.14 = (f32[8,256]{1,0:T(8,128)S(1)}, f32[8,256]{1,0:T(8,128)S(1)}, u32[]{:S(2)}, u32[]{:S(2)}) collective-permute-start(f32[8,256]{1,0:T(8,128)S(1)} %shard_map.79.stat), channel_id=1, source_target_pairs={{0,8},{8,0},{16,24},{24,16},{1,9},{9,1},{17,25},{25,17},{2,10},{10... | collective-permute-start | bytes 24584 | tf_op jit(solution)/shard_map/ppermute | solution.py:20
  62.9 4.1 %shard_map.80 = bf16[2,128,512]{2,1,0:T(8,128)(2,1)} custom-call(s32[8,32]{1,0:T(8,128)S(1)} %copy-done.10, bf16[2,128,512]{2,1,0:T(8,128)(2,1)S(1)} %copy-done, f32[8,256]{1,0:T(8,128)S(1)} %shard_map.79.stat, bf16[16,128,512]{2,1,0:T(8,128)(2,1)S(1)} %all-to-all-done.near, bf16[2,128,512]{2,1,0:T(8,128)(2,1)} %collective-permute-done.5.refs_0_, ...), custom_call_target="tpu_custom_call" | custom-call | bytes 67108864 | tf_op jit(solution)/shard_map/pallas_call | solution.py:26
  67.1 4.4 %shard_map.81 = bf16[6,128,512]{2,1,0:T(8,128)(2,1)} custom-call(s32[8,64]{1,0:T(8,128)S(1)} %copy-done.12, bf16[6,128,512]{2,1,0:T(8,128)(2,1)S(1)} %copy-done.1, bf16[2,128,512]{2,1,0:T(8,128)(2,1)S(1)} %copy-done, bf16[2,128,512]{2,1,0:T(8,128)(2,1)S(1)} %copy-done.7, bf16[2,128,512]{2,1,0:T(8,128)(2,1)S(1)} %copy-done.5, ...), custom_call_target="tpu_custom_call" | custom-call | tf_op jit(solution)/shard_map/pallas_call | solution.py:26
  (45 shorter events, 1.2 us)
Async XLA Ops:
  0.6 12.7 %collective-permute-start.4 = (bf16[2,128,512]{2,1,0:T(8,128)(2,1)}, bf16[2,128,512]{2,1,0:T(8,128)(2,1)}, u32[]{:S(2)}, u32[]{:S(2)}) collective-permute-start(bf16[2,128,512]{2,1,0:T(8,128)(2,1)} %refs_2_.2), channel_id=1, source_target_pairs={{0,24},{8,16},{16,8},{24,0},{1,25},{9,17},{17,9},{25,1},{2,26},{10... | collective-permute-start | bytes 786440 | tf_op jit(solution)/shard_map/ppermute | solution.py:20
  5.7 12.2 %collective-permute-start.3 = (bf16[2,128,512]{2,1,0:T(8,128)(2,1)}, bf16[2,128,512]{2,1,0:T(8,128)(2,1)S(1)}, u32[]{:S(2)}, u32[]{:S(2)}) collective-permute-start(bf16[2,128,512]{2,1,0:T(8,128)(2,1)} %refs_2_.2), channel_id=1, source_target_pairs={{0,8},{8,0},{16,24},{24,16},{1,9},{9,1},{17,25},{25,17},{2,10},{10... | collective-permute-start | bytes 786440 | tf_op jit(solution)/shard_map/ppermute | solution.py:20
  5.7 12.9 %collective-permute-start.2 = (bf16[2,128,512]{2,1,0:T(8,128)(2,1)}, bf16[2,128,512]{2,1,0:T(8,128)(2,1)S(1)}, u32[]{:S(2)}, u32[]{:S(2)}) collective-permute-start(bf16[2,128,512]{2,1,0:T(8,128)(2,1)} %refs_2_.2), channel_id=1, source_target_pairs={{0,6},{1,7},{2,4},{3,5},{4,2},{5,3},{6,0},{7,1},{8,14},{9,15},{10,... | collective-permute-start | bytes 786440 | tf_op jit(solution)/shard_map/ppermute | solution.py:20
  8.2 12.0 %collective-permute-start.1 = (bf16[2,128,512]{2,1,0:T(8,128)(2,1)}, bf16[2,128,512]{2,1,0:T(8,128)(2,1)S(1)}, u32[]{:S(2)}, u32[]{:S(2)}) collective-permute-start(bf16[2,128,512]{2,1,0:T(8,128)(2,1)} %refs_2_.2), channel_id=1, source_target_pairs={{0,4},{1,5},{2,6},{3,7},{4,0},{5,1},{6,2},{7,3},{8,12},{9,13},{10,... | collective-permute-start | bytes 786440 | tf_op jit(solution)/shard_map/ppermute | solution.py:20
  8.7 11.6 %collective-permute-start = (bf16[2,128,512]{2,1,0:T(8,128)(2,1)}, bf16[2,128,512]{2,1,0:T(8,128)(2,1)S(1)}, u32[]{:S(2)}, u32[]{:S(2)}) collective-permute-start(bf16[2,128,512]{2,1,0:T(8,128)(2,1)} %refs_2_.2), channel_id=1, source_target_pairs={{0,2},{1,3},{2,0},{3,1},{4,6},{5,7},{6,4},{7,5},{8,10},{9,11},{10,... | collective-permute-start | bytes 786440 | tf_op jit(solution)/shard_map/ppermute | solution.py:20
  20.3 30.3 %all-to-all-start = ((bf16[16,128,512]{2,1,0:T(8,128)(2,1)}), bf16[16,128,512]{2,1,0:T(8,128)(2,1)S(1)}, u32[]{:S(2)}, u32[]{:S(2)}) async-start(bf16[16,128,512]{2,1,0:T(8,128)(2,1)} %get-tuple-element.25), calls=%async_computation | async-start | bytes 4194304 | tf_op jit(solution)/shard_map/all_to_all | solution.py:370
  24.1 26.5 %copy-start.10 = (s32[8,32]{1,0:T(8,128)S(1)}, s32[8,32]{1,0:T(8,128)}, u32[]{:S(2)}) copy-start(s32[8,32]{1,0:T(8,128)} %get-tuple-element.19.wanted) | copy-start | bytes 3076
  24.1 28.3 %copy-start.11 = (f32[8,256]{1,0:T(8,128)S(1)}, f32[8,256]{1,0:T(8,128)}, u32[]{:S(2)}) copy-start(f32[8,256]{1,0:T(8,128)} %get-tuple-element.20.row_data) | copy-start | bytes 24580
  25.3 34.3 %collective-permute-start.8 = (bf16[8,128,512]{2,1,0:T(8,128)(2,1)}, bf16[8,128,512]{2,1,0:T(8,128)(2,1)S(1)}, u32[]{:S(2)}, u32[]{:S(2)}) collective-permute-start(bf16[8,128,512]{2,1,0:T(8,128)(2,1)} %pad_maximum_fusion), channel_id=1, source_target_pairs={{0,1},{1,0},{2,3},{3,2},{4,5},{5,4},{6,7},{7,6},{8,9},{9,8},{10,11... | collective-permute-start | bytes 3145736 | tf_op jit(solution)/shard_map/ppermute | solution.py:20
  25.7 26.7 %collective-permute-start.5 = (bf16[2,128,512]{2,1,0:T(8,128)(2,1)}, bf16[2,128,512]{2,1,0:T(8,128)(2,1)}, u32[]{:S(2)}, u32[]{:S(2)}) collective-permute-start(bf16[2,128,512]{2,1,0:T(8,128)(2,1)} %get-tuple-element.26), channel_id=1, source_target_pairs={{0,8},{8,0},{16,24},{24,16},{1,9},{9,1},{17,25},{25,17},{2,10},{10... | collective-permute-start | bytes 786440 | tf_op jit(solution)/shard_map/ppermute | solution.py:20
  27.4 25.0 %collective-permute-start.6 = (bf16[2,128,512]{2,1,0:T(8,128)(2,1)}, bf16[2,128,512]{2,1,0:T(8,128)(2,1)}, u32[]{:S(2)}, u32[]{:S(2)}) collective-permute-start(bf16[2,128,512]{2,1,0:T(8,128)(2,1)} %get-tuple-element.27), channel_id=1, source_target_pairs={{0,16},{8,24},{16,0},{24,8},{1,17},{9,25},{17,1},{25,9},{2,18},{10... | collective-permute-start | bytes 786440 | tf_op jit(solution)/shard_map/ppermute | solution.py:20
  27.4 25.0 %collective-permute-start.7 = (bf16[2,128,512]{2,1,0:T(8,128)(2,1)}, bf16[2,128,512]{2,1,0:T(8,128)(2,1)}, u32[]{:S(2)}, u32[]{:S(2)}) collective-permute-start(bf16[2,128,512]{2,1,0:T(8,128)(2,1)} %get-tuple-element.28), channel_id=1, source_target_pairs={{0,24},{8,16},{16,8},{24,0},{1,25},{9,17},{17,9},{25,1},{2,26},{10... | collective-permute-start | bytes 786440 | tf_op jit(solution)/shard_map/ppermute | solution.py:20
  30.1 28.0 %collective-permute-start.9 = (bf16[2,128,512]{2,1,0:T(8,128)(2,1)}, bf16[2,128,512]{2,1,0:T(8,128)(2,1)}, u32[]{:S(2)}, u32[]{:S(2)}) collective-permute-start(bf16[2,128,512]{2,1,0:T(8,128)(2,1)} %collective-permute-done.4.refs_9_), channel_id=1, source_target_pairs={{0,8},{8,0},{16,24},{24,16},{1,9},{9,1},{17,25},{25,17},{2,10},{10... | collective-permute-start | bytes 786440 | tf_op jit(solution)/shard_map/ppermute | solution.py:20
  52.4 14.6 %copy-start.1 = (bf16[6,128,512]{2,1,0:T(8,128)(2,1)S(1)}, bf16[6,128,512]{2,1,0:T(8,128)(2,1)}, u32[]{:S(2)}) copy-start(bf16[6,128,512]{2,1,0:T(8,128)(2,1)} %refs_1_.1) | copy-start | bytes 2359300
  52.4 14.6 %copy-start.3 = (bf16[2,128,512]{2,1,0:T(8,128)(2,1)S(1)}, bf16[2,128,512]{2,1,0:T(8,128)(2,1)}, u32[]{:S(2)}) copy-start(bf16[2,128,512]{2,1,0:T(8,128)(2,1)} %copy-done.2) | copy-start | bytes 786436
  52.4 14.6 %copy-start.5 = (bf16[2,128,512]{2,1,0:T(8,128)(2,1)S(1)}, bf16[2,128,512]{2,1,0:T(8,128)(2,1)}, u32[]{:S(2)}) copy-start(bf16[2,128,512]{2,1,0:T(8,128)(2,1)} %copy-done.4) | copy-start | bytes 786436
  52.5 14.6 %copy-start.7 = (bf16[2,128,512]{2,1,0:T(8,128)(2,1)S(1)}, bf16[2,128,512]{2,1,0:T(8,128)(2,1)}, u32[]{:S(2)}) copy-start(bf16[2,128,512]{2,1,0:T(8,128)(2,1)} %copy-done.6) | copy-start | bytes 786436
  54.9 1.2 %collective-permute-start.10 = (f32[8,256]{1,0:T(8,128)S(1)}, f32[8,256]{1,0:T(8,128)S(1)}, u32[]{:S(2)}, u32[]{:S(2)}) collective-permute-start(f32[8,256]{1,0:T(8,128)S(1)} %shard_map.79.stat), channel_id=1, source_target_pairs={{0,1},{1,0},{2,3},{3,2},{4,5},{5,4},{6,7},{7,6},{8,9},{9,8},{10,11... | collective-permute-start | bytes 24584 | tf_op jit(solution)/shard_map/ppermute | solution.py:20
  54.9 6.8 %collective-permute-start.16 = (f32[8,256]{1,0:T(8,128)S(1)}, f32[8,256]{1,0:T(8,128)S(1)}, u32[]{:S(2)}, u32[]{:S(2)}) collective-permute-start(f32[8,256]{1,0:T(8,128)S(1)} %shard_map.79.stat), channel_id=1, source_target_pairs={{0,24},{8,16},{16,8},{24,0},{1,25},{9,17},{17,9},{25,1},{2,26},{10... | collective-permute-start | bytes 24584 | tf_op jit(solution)/shard_map/ppermute | solution.py:20
  56.1 10.9 %collective-permute-start.13 = (f32[2,8,256]{2,1,0:T(8,128)S(1)}, f32[2,8,256]{2,1,0:T(8,128)S(1)}, u32[]{:S(2)}, u32[]{:S(2)}) collective-permute-start(f32[2,8,256]{2,1,0:T(8,128)S(1)} %pad_maximum_fusion.1.refs_10_), channel_id=1, source_target_pairs={{0,6},{1,7},{2,4},{3,5},{4,2},{5,3},{6,0},{7,1},{8,14},{9,15},{10,... | collective-permute-start | bytes 49160 | tf_op jit(solution)/shard_map/ppermute | solution.py:20
  56.7 10.3 %collective-permute-start.12 = (f32[2,8,256]{2,1,0:T(8,128)S(1)}, f32[2,8,256]{2,1,0:T(8,128)S(1)}, u32[]{:S(2)}, u32[]{:S(2)}) collective-permute-start(f32[2,8,256]{2,1,0:T(8,128)S(1)} %pad_maximum_fusion.1.refs_10_), channel_id=1, source_target_pairs={{0,4},{1,5},{2,6},{3,7},{4,0},{5,1},{6,2},{7,3},{8,12},{9,13},{10,... | collective-permute-start | bytes 49160 | tf_op jit(solution)/shard_map/ppermute | solution.py:20
  58.1 8.9 %collective-permute-start.11 = (f32[2,8,256]{2,1,0:T(8,128)S(1)}, f32[2,8,256]{2,1,0:T(8,128)S(1)}, u32[]{:S(2)}, u32[]{:S(2)}) collective-permute-start(f32[2,8,256]{2,1,0:T(8,128)S(1)} %pad_maximum_fusion.1.refs_10_), channel_id=1, source_target_pairs={{0,2},{1,3},{2,0},{3,1},{4,6},{5,7},{6,4},{7,5},{8,10},{9,11},{10,... | collective-permute-start | bytes 49160 | tf_op jit(solution)/shard_map/ppermute | solution.py:20
  59.6 7.4 %collective-permute-start.15 = (f32[8,256]{1,0:T(8,128)S(1)}, f32[8,256]{1,0:T(8,128)S(1)}, u32[]{:S(2)}, u32[]{:S(2)}) collective-permute-start(f32[8,256]{1,0:T(8,128)S(1)} %shard_map.79.stat), channel_id=1, source_target_pairs={{0,16},{8,24},{16,0},{24,8},{1,17},{9,25},{17,1},{25,9},{2,18},{10... | collective-permute-start | bytes 24584 | tf_op jit(solution)/shard_map/ppermute | solution.py:20
  61.7 5.3 %collective-permute-start.14 = (f32[8,256]{1,0:T(8,128)S(1)}, f32[8,256]{1,0:T(8,128)S(1)}, u32[]{:S(2)}, u32[]{:S(2)}) collective-permute-start(f32[8,256]{1,0:T(8,128)S(1)} %shard_map.79.stat), channel_id=1, source_target_pairs={{0,8},{8,0},{16,24},{24,16},{1,9},{9,1},{17,25},{25,17},{2,10},{10... | collective-permute-start | bytes 24584 | tf_op jit(solution)/shard_map/ppermute | solution.py:20
  (7 other events, 46.7 us)

commit v3 on v2

--- a/solution.py
+++ b/solution.py
@@ -10,7 +10,7 @@
 
 NLOCAL = 12
 VMEM_BYTES = 32 * 1024 * 1024
-PLAN_VMEM_BYTES = 60 * 1024 * 1024
+PLAN_VMEM_BYTES = 63 * 1024 * 1024
 PLAN_BYTES = 16 * 1024 * 1024
 NEAR_BYTES = 64 * 1024 * 1024
 
@@ -77,8 +77,9 @@
 
 def plan_kernel(scale, cap, near_cap, far_cap, columns, groups, query_blocks, *refs):
     lists_in, owners_in, weight_in, positives_in, passages_in = refs[:5]
-    fars, (near_out, asked, wanted, row_data) = refs[5 : 4 + groups], refs[4 + groups : 8 + groups]
-    lists, owners, weight, positives, passages, scalars, sems, out_sems, scalar_sem = refs[8 + groups :]
+    fars, (near_out, asked, numbers, row_data) = refs[5 : 4 + groups], refs[4 + groups : 8 + groups]
+    lists, owners, weight, positives, passages, wanted = refs[8 + groups : 14 + groups]
+    scalars, wanted_scalars, sems, out_sems, scalar_sems = refs[14 + groups :]
     loads = start_all(
         (
             (lists_in, lists),
@@ -118,7 +119,7 @@
         return most > 0.0
 
     write_rows(slot_rows(listings, cap, of_device), asked)
-    to_scalars = pltpu.make_async_copy(asked, scalars, scalar_sem)
+    to_scalars = pltpu.make_async_copy(asked, scalars, scalar_sems.at[0])
     to_scalars.start()
     loads[2].wait()
     to_scalars.wait()
@@ -151,6 +152,8 @@
         for block in range(blocks)
     ]
     write_rows(slot_rows(listings, cap, lambda flags: flags)[cap:], wanted)
+    to_scalars = pltpu.make_async_copy(wanted, wanted_scalars, scalar_sems.at[1])
+    to_scalars.start()
     loads[3].wait()
     loads[4].wait()
     row_data[...] = jnp.zeros_like(row_data)
@@ -159,70 +162,72 @@
         mine = slice(block * block_rows, (block + 1) * block_rows)
         row_data[2:3, mine] = weight[block : block + 1] * scale
         row_data[3:4, mine] = positives[block : block + 1].astype(jnp.float32)
+    to_scalars.wait()
+    numbers[...] = jnp.full_like(numbers, -1.0)
+    place = lax.broadcasted_iota(jnp.int32, (1, block_rows), 1)
+    entries = [(group * columns + peer, slot) for peer in range(columns) for slot in range(near_cap)]
+    entries += [(owner, slot) for owner in far for slot in range(far_cap)]
+    for index, (owner, slot) in enumerate(entries):
+        for block in range(query_blocks):
+            listing = wanted_scalars[block * cap + slot, owner]
+            number = jnp.where(listing >= 0, place + listing * block_rows, -1)
+            numbers[block : block + 1, index * block_rows : (index + 1) * block_rows] = (
+                number.astype(jnp.float32)
+            )
     for copy in copies:
         copy.wait()
 
 
-def near_pieces(near, columns):
-    group = lax.axis_index("group")
-    cap = near.shape[0] // columns
-    for peer in range(columns):
-        piece = near[peer * cap : (peer + 1) * cap].reshape(-1, near.shape[-1])
-        yield group * columns + peer, piece
-
-
-def far_pieces(fars, columns, groups):
-    for ref, holder in zip(fars, owners_of(columns, groups)[1]):
-        yield holder, ref[...].reshape(-1, ref.shape[-1])
-
-
-def block_scores(scale, entry, cap, holder, query, piece, block_rows):
-    scores = (
-        lax.dot_general(query, piece, (((1,), (1,)), ((), ())), preferred_element_type=jnp.float32)
-        * scale
-    )
-    for block in range(query.shape[0] // block_rows):
-        for slot in range(piece.shape[0] // block_rows):
-            listing = entry[block * cap + slot, holder]
-            bias = jnp.where(listing >= 0, 0.0, -jnp.inf).astype(jnp.float32)
-            rows = slice(block * block_rows, (block + 1) * block_rows)
-            columns = slice(slot * block_rows, (slot + 1) * block_rows)
-            yield block, slot, listing, scores[rows, columns] + bias
-
-
-def peak_and_total(scale, entry, cap, queries, pieces, scores_ref, peak_ref):
+def score_blocks(scale, queries, pieces, numbers, first, scores, peak_ref):
     query_blocks, block_rows, width = queries.shape
     rows = query_blocks * block_rows
     query = queries[...].reshape(rows, width)
     peak_ref[...] = jnp.full_like(peak_ref, -jnp.inf)
     at = 0
-    for holder, piece in pieces:
-        for block, slot, _, part in block_scores(
-            scale, entry, cap, holder, query, piece, block_rows
-        ):
+    for piece in pieces:
+        size = piece.shape[0]
+        part = lax.dot_general(
+            query, piece, (((1,), (1,)), ((), ())), preferred_element_type=jnp.float32
+        )
+        for block in range(query_blocks):
             mine = slice(block * block_rows, (block + 1) * block_rows)
-            scores_ref[at + slot, mine] = part
-            peak_ref[mine] = jnp.maximum(peak_ref[mine], part)
-        at += piece.shape[0] // block_rows
+            number = numbers[block : block + 1, first + at : first + at + size]
+            own = jnp.where(number >= 0.0, part[mine] * scale, -jnp.inf)
+            scores[mine, at : at + size] = own
+            peak = peak_ref[mine]
+            for column in range(0, size, block_rows):
+                peak = jnp.maximum(peak, own[:, column : column + block_rows])
+            peak_ref[mine] = peak
+        at += size
     peak = jnp.max(peak_ref[...], axis=1, keepdims=True)
     total = jnp.zeros((rows, block_rows), jnp.float32)
-    for index in range(at):
-        total = total + jnp.exp(scores_ref[index] - peak)
+    for column in range(0, at, block_rows):
+        total = total + jnp.exp(scores[:, column : column + block_rows] - peak)
     return peak, jnp.sum(total, axis=1, keepdims=True)
 
 
-def near_kernel(scale, cap, columns, wanted, queries, near, out, scores_ref, peak_ref):
+def near_pieces(near, columns):
+    cap = near.shape[0] // columns
+    for peer in range(columns):
+        yield near[peer * cap : (peer + 1) * cap].reshape(-1, near.shape[-1])
+
+
+def far_pieces(fars):
+    for ref in fars:
+        yield ref[...].reshape(-1, ref.shape[-1])
+
+
+def near_kernel(scale, columns, queries, numbers, near, out, scores, peak_ref):
     pieces = near_pieces(near, columns)
-    peak, total = peak_and_total(scale, wanted, cap, queries, pieces, scores_ref, peak_ref)
+    peak, total = score_blocks(scale, queries, pieces, numbers, 0, scores, peak_ref)
     lane = lax.broadcasted_iota(jnp.int32, out.shape, 1)
     out[...] = jnp.where(lane == 0, peak, total)
 
 
-def stats_kernel(scale, cap, columns, groups, wanted, queries, row_data, near_stat, *refs):
-    fars, (stat, scores_ref, peak_ref) = refs[: groups - 1], refs[groups - 1 :]
-    pieces = far_pieces(fars, columns, groups)
-    far_peak, far_total = peak_and_total(
-        scale, wanted, cap, queries, pieces, scores_ref, peak_ref
+def stats_kernel(scale, first, queries, row_data, numbers, near_stat, *refs):
+    fars, (stat, scores, peak_ref) = refs[:-3], refs[-3:]
+    far_peak, far_total = score_blocks(
+        scale, queries, far_pieces(fars), numbers, first, scores, peak_ref
     )
     near_peak, near_total = near_stat[:, 0:1], near_stat[:, 1:2]
     peak = jnp.maximum(near_peak, far_peak)
@@ -233,33 +238,32 @@
     stat[0:2] = turned[0:2]
 
 
-def query_kernel(scale, cap, columns, groups, wanted, queries, stat, near, *refs):
-    fars, (out, total, dscore_ref) = refs[: groups - 1], refs[groups - 1 :]
-    query_blocks, block_rows, width = queries.shape
+def query_kernel(columns, numbers, stat, near_scores, far_scores, near, *refs):
+    fars, (out, total, dscore_ref) = refs[:-3], refs[-3:]
+    query_blocks, block_rows, width = out.shape
     rows = query_blocks * block_rows
-    query = queries[...].reshape(rows, width)
     turned = jnp.concatenate(
         [stat[...], jnp.zeros((128 - stat.shape[0], rows), jnp.float32)], axis=0
     ).T
     peak, inverse = turned[:, 0:1], 1.0 / turned[:, 1:2]
     weight, positive = turned[:, 2:3], turned[:, 3:4]
-    place = lax.broadcasted_iota(jnp.int32, (block_rows, block_rows), 1)
     total[...] = jnp.zeros_like(total)
-    pieces = list(near_pieces(near, columns)) + list(far_pieces(fars, columns, groups))
-    for holder, piece in pieces:
-        for block, slot, listing, part in block_scores(
-            scale, wanted, cap, holder, query, piece, block_rows
-        ):
-            mine = slice(block * block_rows, (block + 1) * block_rows)
-            number = (place + listing * block_rows).astype(jnp.float32)
-            target = jnp.where(positive[mine] == number, 1.0, 0.0)
-            chance = jnp.exp(part - peak[mine]) * inverse[mine]
-            dscore_ref[mine, slot * block_rows : (slot + 1) * block_rows] = (
-                (chance - target) * weight[mine]
-            ).astype(jnp.bfloat16)
-        total[...] += jnp.dot(
-            dscore_ref[:, : piece.shape[0]], piece, preferred_element_type=jnp.float32
-        )
+    first = 0
+    for scores, pieces in ((near_scores, near_pieces(near, columns)), (far_scores, far_pieces(fars))):
+        at = 0
+        for piece in pieces:
+            size = piece.shape[0]
+            for block in range(query_blocks):
+                mine = slice(block * block_rows, (block + 1) * block_rows)
+                number = numbers[block : block + 1, first + at : first + at + size]
+                chance = jnp.exp(scores[mine, at : at + size] - peak[mine]) * inverse[mine]
+                target = jnp.where(positive[mine] == number, 1.0, 0.0)
+                dscore_ref[mine, :size] = ((chance - target) * weight[mine]).astype(jnp.bfloat16)
+            total[...] += jnp.dot(
+                dscore_ref[:, :size], piece, preferred_element_type=jnp.float32
+            )
+            at += size
+        first += at
     out[...] = total[...].reshape(out.shape).astype(out.dtype)
 
 
@@ -275,12 +279,12 @@
     rows = query_blocks * block_rows
     total[...] = jnp.zeros_like(total)
     lane = lax.broadcasted_iota(jnp.int32, (1, rows), 1)
-    place = lax.broadcasted_iota(jnp.int32, (block_rows, rows), 0)
+    place = lax.broadcasted_iota(jnp.int32, (block_rows, rows), 0).astype(jnp.float32)
     for unit, (owner, slots) in enumerate(units):
         query, stat = unit_of(unit, queries_in, stats_in)
         query = query[...].reshape(rows, width)
-        peak, inverse = stat[0:1], 1.0 / stat[1:2]
-        weight, positive = stat[2:3], stat[3:4]
+        peak, weight, positive = stat[0:1], stat[2:3], stat[3:4]
+        share = weight / stat[1:2]
         held = [asked[slot, owner * query_blocks] for slot in range(slots)]
         mine = jnp.concatenate([passages[index] for index in held], axis=0)
         scores = (
@@ -295,12 +299,11 @@
             for block in range(1, query_blocks):
                 later = asked[cap + slot, owner * query_blocks + block]
                 listing = jnp.where(lane >= block * block_rows, later, listing)
-            bias = jnp.where(listing >= 0, 0.0, -jnp.inf)
-            number = (place + listing * block_rows).astype(jnp.float32)
-            part = scores[slot * block_rows : (slot + 1) * block_rows] + bias
-            target = jnp.where(positive == number, 1.0, 0.0)
-            chance = jnp.exp(part - peak) * inverse
-            parts.append(((chance - target) * weight).astype(jnp.bfloat16))
+            bias = jnp.where(listing >= 0, -peak, -jnp.inf)
+            row = positive - (listing * block_rows).astype(jnp.float32)
+            part = scores[slot * block_rows : (slot + 1) * block_rows]
+            target = jnp.where(row == place, weight, 0.0)
+            parts.append((jnp.exp(part + bias) * share - target).astype(jnp.bfloat16))
         term = jnp.dot(
             jnp.concatenate(parts, axis=0), query, preferred_element_type=jnp.float32
         ).astype(jnp.bfloat16)
@@ -336,7 +339,7 @@
     vmem = pl.BlockSpec(memory_space=pltpu.VMEM)
     hbm = pl.BlockSpec(memory_space=pltpu.HBM)
     far_shape = jax.ShapeDtypeStruct((far_cap, block_rows, width), dtype)
-    *far_out, near_out, asked, wanted, row_data = pl.pallas_call(
+    *far_out, near_out, asked, numbers, row_data = pl.pallas_call(
         functools.partial(
             plan_kernel, scale, cap, near_cap, far_cap, columns, groups, query_blocks
         ),
@@ -344,7 +347,7 @@
         + [
             jax.ShapeDtypeStruct((columns * near_cap, block_rows, width), dtype),
             jax.ShapeDtypeStruct((table_rows, all_lists), jnp.int32),
-            jax.ShapeDtypeStruct((table_rows, devices), jnp.int32),
+            jax.ShapeDtypeStruct((8, slots * block_rows), jnp.float32),
             jax.ShapeDtypeStruct((8, rows), jnp.float32),
         ],
         in_specs=[hbm] * 5,
@@ -355,10 +358,12 @@
             pltpu.VMEM(row_weight.shape, jnp.float32),
             pltpu.VMEM(positives.shape, jnp.int32),
             pltpu.VMEM(passages.shape, dtype),
+            pltpu.VMEM((table_rows, devices), jnp.int32),
             pltpu.SMEM((table_rows, all_lists), jnp.int32),
+            pltpu.SMEM((table_rows, devices), jnp.int32),
             pltpu.SemaphoreType.DMA((5,)),
             pltpu.SemaphoreType.DMA((slots,)),
-            pltpu.SemaphoreType.DMA,
+            pltpu.SemaphoreType.DMA((2,)),
         ],
         compiler_params=pltpu.CompilerParams(vmem_limit_bytes=PLAN_VMEM_BYTES),
         cost_estimate=pl.CostEstimate(flops=0, bytes_accessed=PLAN_BYTES, transcendentals=0),
@@ -377,35 +382,36 @@
     beside = swap(jnp.concatenate(near_queries), "dp", 1)
 
     near_slots, far_slots = columns * near_cap, (groups - 1) * far_cap
-    near_stat = local_call(
-        functools.partial(near_kernel, scale, cap, columns),
-        [wanted],
-        [queries, near_blocks],
-        jax.ShapeDtypeStruct((rows, 128), jnp.float32),
+    near_stat, near_scores = local_call(
+        functools.partial(near_kernel, scale, columns),
+        [],
+        [queries, numbers, near_blocks],
         [
-            pltpu.VMEM((near_slots, rows, block_rows), jnp.float32),
-            pltpu.VMEM((rows, block_rows), jnp.float32),
+            jax.ShapeDtypeStruct((rows, 128), jnp.float32),
+            jax.ShapeDtypeStruct((rows, near_slots * block_rows), jnp.float32),
         ],
+        [pltpu.VMEM((rows, block_rows), jnp.float32)],
         NEAR_BYTES,
     )
-    stat = local_call(
-        functools.partial(stats_kernel, scale, cap, columns, groups),
-        [wanted],
-        [queries, row_data, near_stat, *far_blocks],
-        jax.ShapeDtypeStruct((8, rows), jnp.float32),
+    stat, far_scores = local_call(
+        functools.partial(stats_kernel, scale, near_slots * block_rows),
+        [],
+        [queries, row_data, numbers, near_stat, *far_blocks],
         [
-            pltpu.VMEM((far_slots, rows, block_rows), jnp.float32),
-            pltpu.VMEM((rows, block_rows), jnp.float32),
+            jax.ShapeDtypeStruct((8, rows), jnp.float32),
+            jax.ShapeDtypeStruct((rows, far_slots * block_rows), jnp.float32),
         ],
+        [pltpu.VMEM((rows, block_rows), jnp.float32)],
         0,
     )
     pair = jnp.stack([stat, swap(stat, "dp", 1)])
     near_stats = [pair] + [swap(pair, "dp", mask) for mask in range(2, columns, 2)]
-    far_stats = [swap(stat, "group", mask) for mask in range(1, groups)]
+    far_pair = jnp.stack([stat, swap(stat, "group", 1)])
+    far_stats = [far_pair] + [swap(far_pair, "group", mask) for mask in range(2, groups, 2)]
     grad_query = local_call(
-        functools.partial(query_kernel, scale, cap, columns, groups),
-        [wanted],
-        [queries, stat, near_blocks, *far_blocks],
+        functools.partial(query_kernel, columns),
+        [],
+        [numbers, stat, near_scores, far_scores, near_blocks, *far_blocks],
         jax.ShapeDtypeStruct(queries.shape, dtype),
         [
             pltpu.VMEM((rows, width), jnp.float32),
@@ -421,7 +427,8 @@
         pairs = columns // 2
         if unit >= columns:
             far = unit - columns
-            return queries_in[pairs + 1 + far], stats_in[pairs + far]
+            place = (far + 1) // 2
+            return queries_in[pairs + 1 + far], stats_in[pairs + place].at[(far + 1) % 2]
         stat = stats_in[unit // 2].at[unit % 2]
         if unit % 2 == 0:
             return queries_in[unit // 2], stat

time: 71.8 us -> 70.4 us (0.981)
  waiting for transfers between devices: 26.7 us -> 31 us
  Pallas kernels: 16.5 us -> 12.7 us
  starting transfers between devices: 25.5 us -> 24.5 us
  local copies, waits for them, and re-layouts: 0.76 us -> 0.03 us
    pallas_call x4, Pallas kernels: 12.6 us -> 8.79 us  [local_call(): pl.pallas_call(kernel, out_shape=outs, in_specs=[smem] * len(tables) + [v...]
    ppermute x17 -> x16, waiting for transfers between devices: 6.98 us -> 10.4 us  [swap(): return lax.ppermute(x, axis, [(i, i ^ mask) for i in range(size)])]
    ppermute x17 -> x16, starting transfers between devices: 21.7 us -> 20.7 us  [swap(): return lax.ppermute(x, axis, [(i, i ^ mask) for i in range(size)])]
    all_to_all x1, waiting for transfers between devices: 19.8 us -> 20.6 us  [shards(): lax.all_to_all(near_out, 'dp', split_axis=0, concat_axis=0, tiled=True)]
    unnamed x26 -> x18, local copies, waits for them, and re-layouts: 0.76 us -> 0.03 us
  transfers between devices with their start and end apart: 18 -> 17, of which waited for: 6 -> 5; matrix products, arithmetic and copies ran while one was open for 2% -> 2% of each run, Pallas kernels for 17% -> 12%
where the time goes in v3:
time: 70.4 us; the launch traced here: 70.2 us
  waiting for transfers between devices  31 us (44%)
  starting transfers between devices  24.5 us (35%)
  Pallas kernels  12.7 us (18%)
  other arithmetic  1.1 us (2%)
  between operations  0.75 us (1%)
    ppermute x16, starting transfers between devices, swap(): return lax.ppermute(x, axis, [(i, i ^ mask) for i in range(size)])  20.7 us
    all_to_all x1, waiting for transfers between devices, shards(): lax.all_to_all(near_out, 'dp', split_axis=0, concat_axis=0, tiled=True)  20.6 us
    ppermute x16, waiting for transfers between devices, swap(): return lax.ppermute(x, axis, [(i, i ^ mask) for i in range(size)])  10.4 us
    pallas_call x4, Pallas kernels, local_call(): pl.pallas_call(kernel, out_shape=outs, in_specs=[smem] * len(tables) + [v...  8.79 us
    pallas_call x1, Pallas kernels, shards(): pl.pallas_call(functools.partial(plan_kernel, scale, cap, near_cap, far_c...  3.94 us
    all_to_all x1, starting transfers between devices, shards(): lax.all_to_all(near_out, 'dp', split_axis=0, concat_axis=0, tiled=True)  3.86 us
  transfers between devices with their start and end apart: 17, of which 5 were waited for; matrix products, arithmetic and copies ran while one was open for 2% of the time, Pallas kernels for 12%

profile of v3, /device:TPU:0, one launch (start us, length us, event | category | flops | bytes accessed | tf_op | source)
XLA Modules:
  0.0 70.2 jit_solution(13408787586712168000)
XLA Ops:
  0.6 3.0 %collective-permute-start = (bf16[2,128,512]{2,1,0:T(8,128)(2,1)}, bf16[2,128,512]{2,1,0:T(8,128)(2,1)S(1)}, u32[]{:S(2)}, u32[]{:S(2)}) collective-permute-start(bf16[2,128,512]{2,1,0:T(8,128)(2,1)} %refs_2_.2), channel_id=1, source_target_pairs={{0,2},{1,3},{2,0},{3,1},{4,6},{5,7},{6,4},{7,5},{8,10},{9,11},{10,... | collective-permute-start | bytes 786440 | tf_op jit(solution)/shard_map/ppermute | solution.py:20
  3.6 1.5 %collective-permute-start.1 = (bf16[2,128,512]{2,1,0:T(8,128)(2,1)}, bf16[2,128,512]{2,1,0:T(8,128)(2,1)S(1)}, u32[]{:S(2)}, u32[]{:S(2)}) collective-permute-start(bf16[2,128,512]{2,1,0:T(8,128)(2,1)} %refs_2_.2), channel_id=1, source_target_pairs={{0,4},{1,5},{2,6},{3,7},{4,0},{5,1},{6,2},{7,3},{8,12},{9,13},{10,... | collective-permute-start | bytes 786440 | tf_op jit(solution)/shard_map/ppermute | solution.py:20
  5.2 2.0 %collective-permute-start.3 = (bf16[2,128,512]{2,1,0:T(8,128)(2,1)}, bf16[2,128,512]{2,1,0:T(8,128)(2,1)}, u32[]{:S(2)}, u32[]{:S(2)}) collective-permute-start(bf16[2,128,512]{2,1,0:T(8,128)(2,1)} %refs_2_.2), channel_id=1, source_target_pairs={{0,8},{8,0},{16,24},{24,16},{1,9},{9,1},{17,25},{25,17},{2,10},{10... | collective-permute-start | bytes 786440 | tf_op jit(solution)/shard_map/ppermute | solution.py:20
  7.2 2.5 %collective-permute-start.4 = (bf16[2,128,512]{2,1,0:T(8,128)(2,1)}, bf16[2,128,512]{2,1,0:T(8,128)(2,1)}, u32[]{:S(2)}, u32[]{:S(2)}) collective-permute-start(bf16[2,128,512]{2,1,0:T(8,128)(2,1)} %refs_2_.2), channel_id=1, source_target_pairs={{0,24},{8,16},{16,8},{24,0},{1,25},{9,17},{17,9},{25,1},{2,26},{10... | collective-permute-start | bytes 786440 | tf_op jit(solution)/shard_map/ppermute | solution.py:20
  9.7 3.9 %shard_map.77 = (bf16[2,128,512]{2,1,0:T(8,128)(2,1)}, bf16[2,128,512]{2,1,0:T(8,128)(2,1)}, bf16[2,128,512]{2,1,0:T(8,128)(2,1)}, bf16[16,128,512]{2,1,0:T(8,12...) custom-call(s32[16,64]{1,0:T(8,128)} %bitcast.6, s32[1,192]{1,0:T(1,128)} %bitcast.9, ...), custom_call_target="tpu_custom_call" | custom-call | bytes 16777216 | tf_op jit(solution)/shard_map/pallas_call | solution.py:342
  13.6 3.6 %collective-permute-done.1.refs_4_ = bf16[2,128,512]{2,1,0:T(8,128)(2,1)S(1)} collective-permute-done((bf16[2,128,512]{2,1,0:T(8,128)(2,1)}, bf16[2,128,512]{2,1,0:T(8,128)(2,1)S(1)}, u32[]{:S(2)}, u32[]{:S(2)}) %collective-permute-start.1) | collective-permute-done | bytes 262176 | tf_op jit(solution)/shard_map/ppermute | solution.py:20
  17.2 3.7 %collective-permute-done.4.refs_9_ = bf16[2,128,512]{2,1,0:T(8,128)(2,1)} collective-permute-done((bf16[2,128,512]{2,1,0:T(8,128)(2,1)}, bf16[2,128,512]{2,1,0:T(8,128)(2,1)}, u32[]{:S(2)}, u32[]{:S(2)}) %collective-permute-start.4) | collective-permute-done | bytes 262176 | tf_op jit(solution)/shard_map/ppermute | solution.py:20
  20.9 3.9 %all-to-all-start = ((bf16[16,128,512]{2,1,0:T(8,128)(2,1)}), bf16[16,128,512]{2,1,0:T(8,128)(2,1)S(1)}, u32[]{:S(2)}, u32[]{:S(2)}) async-start(bf16[16,128,512]{2,1,0:T(8,128)(2,1)} %get-tuple-element.29), calls=%async_computation | async-start | bytes 4194304 | tf_op jit(solution)/shard_map/all_to_all | solution.py:375
  24.8 1.1 %pad_maximum_fusion = bf16[8,128,512]{2,1,0:T(8,128)(2,1)} fusion(bf16[2,128,512]{2,1,0:T(8,128)(2,1)S(1)} %collective-permute-done.2.refs_5_, bf16[2,128,512]{2,1,0:T(8,128)(2,1)S(1)} %collective-permute-done.1.refs_4_, bf16[2,128,512]{2,1,0:T(8,128)(2,1)S(1)} %collective-permute-done.refs_3_, bf16[2,128,512]{2,1,0:T(8,128)(2,1)S(1)} %copy-done), kind=kLoop, calls=%fused_computation | loop fusion | flops 1572864 | bytes 2097152 | tf_op jit(solution)/shard_map/concatenate | solution.py:382
  26.4 0.6 collective-permute-start.5
  27.0 1.4 %collective-permute-start.6 = (bf16[2,128,512]{2,1,0:T(8,128)(2,1)}, bf16[2,128,512]{2,1,0:T(8,128)(2,1)S(1)}, u32[]{:S(2)}, u32[]{:S(2)}) collective-permute-start(bf16[2,128,512]{2,1,0:T(8,128)(2,1)} %get-tuple-element.32), channel_id=1, source_target_pairs={{0,16},{8,24},{16,0},{24,8},{1,17},{9,25},{17,1},{25,9},{2,18},{10... | collective-permute-start | bytes 786440 | tf_op jit(solution)/shard_map/ppermute | solution.py:20
  28.4 2.3 %collective-permute-start.7 = (bf16[2,128,512]{2,1,0:T(8,128)(2,1)}, bf16[2,128,512]{2,1,0:T(8,128)(2,1)S(1)}, u32[]{:S(2)}, u32[]{:S(2)}) collective-permute-start(bf16[2,128,512]{2,1,0:T(8,128)(2,1)} %get-tuple-element.33), channel_id=1, source_target_pairs={{0,24},{8,16},{16,8},{24,0},{1,25},{9,17},{17,9},{25,1},{2,26},{10... | collective-permute-start | bytes 786440 | tf_op jit(solution)/shard_map/ppermute | solution.py:20
  30.8 20.6 %all-to-all-done.near = bf16[16,128,512]{2,1,0:T(8,128)(2,1)S(1)} async-done(((bf16[16,128,512]{2,1,0:T(8,128)(2,1)}), bf16[16,128,512]{2,1,0:T(8,128)(2,1)S(1)}, u32[]{:S(2)}, u32[]{:S(2)}) %all-to-all-start) | async-done | bytes 2097184 | tf_op jit(solution)/shard_map/all_to_all | solution.py:375
  51.4 1.1 %shard_map.78 = (f32[256,128]{1,0:T(8,128)S(1)}, f32[256,2048]{1,0:T(8,128)S(1)}) custom-call(bf16[2,128,512]{2,1,0:T(8,128)(2,1)S(1)} %copy-done, f32[8,2816]{1,0:T(8,128)S(1)} %copy-done.6, bf16[16,128,512]{2,1,0:T(8,128)(2,1)S(1)} %all-to-all-done.near), custom_call_target="tpu_custom_call" | custom-call | bytes 67108864 | tf_op jit(solution)/shard_map/pallas_call | solution.py:26
  52.6 1.2 %shard_map.79 = (f32[8,256]{1,0:T(8,128)S(1)}, f32[256,768]{1,0:T(8,128)S(1)}) custom-call(bf16[2,128,512]{2,1,0:T(8,128)(2,1)S(1)} %copy-done, f32[8,256]{1,0:T(8,128)S(1)} %copy-done.7, f32[8,2816]{1,0:T(8,128)S(1)} %copy-done.6, f32[256,128]{1,0:T(8,128)S(1)} %get-tuple-element.30.near_stat, bf16[2,128,512]{2,1,0:T(8,128)(2,1)S(1)} %collective-permute-done.5.refs_0_, ...), custom_call_target="tpu_custom_call" | custom-call | tf_op jit(solution)/shard_map/pallas_call | solution.py:26
  53.7 1.0 %collective-permute-start.14 = (f32[8,256]{1,0:T(8,128)S(1)}, f32[8,256]{1,0:T(8,128)S(1)}, u32[]{:S(2)}, u32[]{:S(2)}) collective-permute-start(f32[8,256]{1,0:T(8,128)S(1)} %get-tuple-element.34.stat), channel_id=1, source_target_pairs={{0,8},{8,0},{16,24},{24,16},{1,9},{9,1},{17,25},{25,17},{2,10},{10... | collective-permute-start | bytes 24584 | tf_op jit(solution)/shard_map/ppermute | solution.py:20
  54.8 2.6 %collective-permute-done.14 = f32[8,256]{1,0:T(8,128)S(1)} collective-permute-done((f32[8,256]{1,0:T(8,128)S(1)}, f32[8,256]{1,0:T(8,128)S(1)}, u32[]{:S(2)}, u32[]{:S(2)}) %collective-permute-start.14) | collective-permute-done | bytes 8224 | tf_op jit(solution)/shard_map/ppermute | solution.py:20
  57.4 1.0 %collective-permute-start.11 = (f32[2,8,256]{2,1,0:T(8,128)S(1)}, f32[2,8,256]{2,1,0:T(8,128)S(1)}, u32[]{:S(2)}, u32[]{:S(2)}) collective-permute-start(f32[2,8,256]{2,1,0:T(8,128)S(1)} %get-tuple-element.45.refs_10_), channel_id=1, source_target_pairs={{0,2},{1,3},{2,0},{3,1},{4,6},{5,7},{6,4},{7,5},{8,10},{9,11},{10,... | collective-permute-start | bytes 49160 | tf_op jit(solution)/shard_map/ppermute | solution.py:20
  58.4 1.5 %collective-permute-start.12 = (f32[2,8,256]{2,1,0:T(8,128)S(1)}, f32[2,8,256]{2,1,0:T(8,128)S(1)}, u32[]{:S(2)}, u32[]{:S(2)}) collective-permute-start(f32[2,8,256]{2,1,0:T(8,128)S(1)} %get-tuple-element.45.refs_10_), channel_id=1, source_target_pairs={{0,4},{1,5},{2,6},{3,7},{4,0},{5,1},{6,2},{7,3},{8,12},{9,13},{10,... | collective-permute-start | bytes 49160 | tf_op jit(solution)/shard_map/ppermute | solution.py:20
  59.9 1.0 %collective-permute-start.13 = (f32[2,8,256]{2,1,0:T(8,128)S(1)}, f32[2,8,256]{2,1,0:T(8,128)S(1)}, u32[]{:S(2)}, u32[]{:S(2)}) collective-permute-start(f32[2,8,256]{2,1,0:T(8,128)S(1)} %get-tuple-element.45.refs_10_), channel_id=1, source_target_pairs={{0,6},{1,7},{2,4},{3,5},{4,2},{5,3},{6,0},{7,1},{8,14},{9,15},{10,... | collective-permute-start | bytes 49160 | tf_op jit(solution)/shard_map/ppermute | solution.py:20
  60.9 2.2 %collective-permute-start.15 = (f32[2,8,256]{2,1,0:T(8,128)S(1)}, f32[2,8,256]{2,1,0:T(8,128)S(1)}, u32[]{:S(2)}, u32[]{:S(2)}) collective-permute-start(f32[2,8,256]{2,1,0:T(8,128)S(1)} %get-tuple-element.44.refs_14_), channel_id=1, source_target_pairs={{0,16},{8,24},{16,0},{24,8},{1,17},{9,25},{17,1},{25,9},{2,18},{10... | collective-permute-start | bytes 49160 | tf_op jit(solution)/shard_map/ppermute | solution.py:20
  63.1 1.9 %shard_map.80 = bf16[2,128,512]{2,1,0:T(8,128)(2,1)} custom-call(f32[8,2816]{1,0:T(8,128)S(1)} %copy-done.6, f32[8,256]{1,0:T(8,128)S(1)} %get-tuple-element.34.stat, f32[256,2048]{1,0:T(8,128)S(1)} %get-tuple-element.35.near_scores, f32[256,768]{1,0:T(8,128)S(1)} %get-tuple-element.36.far_scores, bf16[16,128,512]{2,1,0:T(8,128)(2,1)S(1)} %all-to-all-done.near, ...), custom_call_target="tpu_custom_call" | custom-call | bytes 67108864 | tf_op jit(solution)/shard_map/pallas_call | solution.py:26
  65.0 0.5 collective-permute-done.15.refs_15_
  65.6 4.6 %shard_map.81 = bf16[6,128,512]{2,1,0:T(8,128)(2,1)} custom-call(s32[8,64]{1,0:T(8,128)S(1)} %copy-done.8, bf16[6,128,512]{2,1,0:T(8,128)(2,1)S(1)} %copy-done.1, bf16[2,128,512]{2,1,0:T(8,128)(2,1)S(1)} %copy-done, bf16[2,128,512]{2,1,0:T(8,128)(2,1)S(1)} %collective-permute-done.refs_3_, bf16[2,128,512]{2,1,0:T(8,128)(2,1)S(1)} %copy-done.3, ...), custom_call_target="tpu_custom_call" | custom-call | tf_op jit(solution)/shard_map/pallas_call | solution.py:26
  (35 shorter events, 0.6 us)
Async XLA Ops:
  0.6 13.0 %collective-permute-start = (bf16[2,128,512]{2,1,0:T(8,128)(2,1)}, bf16[2,128,512]{2,1,0:T(8,128)(2,1)S(1)}, u32[]{:S(2)}, u32[]{:S(2)}) collective-permute-start(bf16[2,128,512]{2,1,0:T(8,128)(2,1)} %refs_2_.2), channel_id=1, source_target_pairs={{0,2},{1,3},{2,0},{3,1},{4,6},{5,7},{6,4},{7,5},{8,10},{9,11},{10,... | collective-permute-start | bytes 786440 | tf_op jit(solution)/shard_map/ppermute | solution.py:20
  3.6 13.6 %collective-permute-start.1 = (bf16[2,128,512]{2,1,0:T(8,128)(2,1)}, bf16[2,128,512]{2,1,0:T(8,128)(2,1)S(1)}, u32[]{:S(2)}, u32[]{:S(2)}) collective-permute-start(bf16[2,128,512]{2,1,0:T(8,128)(2,1)} %refs_2_.2), channel_id=1, source_target_pairs={{0,4},{1,5},{2,6},{3,7},{4,0},{5,1},{6,2},{7,3},{8,12},{9,13},{10,... | collective-permute-start | bytes 786440 | tf_op jit(solution)/shard_map/ppermute | solution.py:20
  5.2 12.1 %collective-permute-start.2 = (bf16[2,128,512]{2,1,0:T(8,128)(2,1)}, bf16[2,128,512]{2,1,0:T(8,128)(2,1)S(1)}, u32[]{:S(2)}, u32[]{:S(2)}) collective-permute-start(bf16[2,128,512]{2,1,0:T(8,128)(2,1)} %refs_2_.2), channel_id=1, source_target_pairs={{0,6},{1,7},{2,4},{3,5},{4,2},{5,3},{6,0},{7,1},{8,14},{9,15},{10,... | collective-permute-start | bytes 786440 | tf_op jit(solution)/shard_map/ppermute | solution.py:20
  5.2 12.1 %collective-permute-start.3 = (bf16[2,128,512]{2,1,0:T(8,128)(2,1)}, bf16[2,128,512]{2,1,0:T(8,128)(2,1)}, u32[]{:S(2)}, u32[]{:S(2)}) collective-permute-start(bf16[2,128,512]{2,1,0:T(8,128)(2,1)} %refs_2_.2), channel_id=1, source_target_pairs={{0,8},{8,0},{16,24},{24,16},{1,9},{9,1},{17,25},{25,17},{2,10},{10... | collective-permute-start | bytes 786440 | tf_op jit(solution)/shard_map/ppermute | solution.py:20
  7.2 13.7 %collective-permute-start.4 = (bf16[2,128,512]{2,1,0:T(8,128)(2,1)}, bf16[2,128,512]{2,1,0:T(8,128)(2,1)}, u32[]{:S(2)}, u32[]{:S(2)}) collective-permute-start(bf16[2,128,512]{2,1,0:T(8,128)(2,1)} %refs_2_.2), channel_id=1, source_target_pairs={{0,24},{8,16},{16,8},{24,0},{1,25},{9,17},{17,9},{25,1},{2,26},{10... | collective-permute-start | bytes 786440 | tf_op jit(solution)/shard_map/ppermute | solution.py:20
  17.2 7.5 %copy-start.2 = (bf16[2,128,512]{2,1,0:T(8,128)(2,1)}, bf16[2,128,512]{2,1,0:T(8,128)(2,1)S(1)}, u32[]{:S(2)}) copy-start(bf16[2,128,512]{2,1,0:T(8,128)(2,1)S(1)} %collective-permute-done.1.refs_4_) | copy-start | bytes 786436
  17.2 7.5 %copy-start.4 = (bf16[2,128,512]{2,1,0:T(8,128)(2,1)}, bf16[2,128,512]{2,1,0:T(8,128)(2,1)S(1)}, u32[]{:S(2)}) copy-start(bf16[2,128,512]{2,1,0:T(8,128)(2,1)S(1)} %collective-permute-done.2.refs_5_) | copy-start | bytes 786436
  20.9 3.9 %copy-start = (bf16[2,128,512]{2,1,0:T(8,128)(2,1)S(1)}, bf16[2,128,512]{2,1,0:T(8,128)(2,1)}, u32[]{:S(2)}) copy-start(bf16[2,128,512]{2,1,0:T(8,128)(2,1)} %refs_2_.2) | copy-start | bytes 786436
  20.9 30.5 %all-to-all-start = ((bf16[16,128,512]{2,1,0:T(8,128)(2,1)}), bf16[16,128,512]{2,1,0:T(8,128)(2,1)S(1)}, u32[]{:S(2)}, u32[]{:S(2)}) async-start(bf16[16,128,512]{2,1,0:T(8,128)(2,1)} %get-tuple-element.29), calls=%async_computation | async-start | bytes 4194304 | tf_op jit(solution)/shard_map/all_to_all | solution.py:375
  24.8 26.6 %copy-start.6 = (f32[8,2816]{1,0:T(8,128)S(1)}, f32[8,2816]{1,0:T(8,128)}, u32[]{:S(2)}) copy-start(f32[8,2816]{1,0:T(8,128)} %get-tuple-element.23.numbers) | copy-start | bytes 270340
  24.8 27.8 %copy-start.7 = (f32[8,256]{1,0:T(8,128)S(1)}, f32[8,256]{1,0:T(8,128)}, u32[]{:S(2)}) copy-start(f32[8,256]{1,0:T(8,128)} %get-tuple-element.24.row_data) | copy-start | bytes 24580
  25.9 39.1 %collective-permute-start.8 = (bf16[8,128,512]{2,1,0:T(8,128)(2,1)}, bf16[8,128,512]{2,1,0:T(8,128)(2,1)}, u32[]{:S(2)}, u32[]{:S(2)}) collective-permute-start(bf16[8,128,512]{2,1,0:T(8,128)(2,1)} %pad_maximum_fusion), channel_id=1, source_target_pairs={{0,1},{1,0},{2,3},{3,2},{4,5},{5,4},{6,7},{7,6},{8,9},{9,8},{10,11... | collective-permute-start | bytes 3145736 | tf_op jit(solution)/shard_map/ppermute | solution.py:20
  26.4 26.1 %collective-permute-start.5 = (bf16[2,128,512]{2,1,0:T(8,128)(2,1)}, bf16[2,128,512]{2,1,0:T(8,128)(2,1)S(1)}, u32[]{:S(2)}, u32[]{:S(2)}) collective-permute-start(bf16[2,128,512]{2,1,0:T(8,128)(2,1)} %get-tuple-element.31), channel_id=1, source_target_pairs={{0,8},{8,0},{16,24},{24,16},{1,9},{9,1},{17,25},{25,17},{2,10},{10... | collective-permute-start | bytes 786440 | tf_op jit(solution)/shard_map/ppermute | solution.py:20
  27.0 25.5 %collective-permute-start.6 = (bf16[2,128,512]{2,1,0:T(8,128)(2,1)}, bf16[2,128,512]{2,1,0:T(8,128)(2,1)S(1)}, u32[]{:S(2)}, u32[]{:S(2)}) collective-permute-start(bf16[2,128,512]{2,1,0:T(8,128)(2,1)} %get-tuple-element.32), channel_id=1, source_target_pairs={{0,16},{8,24},{16,0},{24,8},{1,17},{9,25},{17,1},{25,9},{2,18},{10... | collective-permute-start | bytes 786440 | tf_op jit(solution)/shard_map/ppermute | solution.py:20
  28.4 24.1 %collective-permute-start.7 = (bf16[2,128,512]{2,1,0:T(8,128)(2,1)}, bf16[2,128,512]{2,1,0:T(8,128)(2,1)S(1)}, u32[]{:S(2)}, u32[]{:S(2)}) collective-permute-start(bf16[2,128,512]{2,1,0:T(8,128)(2,1)} %get-tuple-element.33), channel_id=1, source_target_pairs={{0,24},{8,16},{16,8},{24,0},{1,25},{9,17},{17,9},{25,1},{2,26},{10... | collective-permute-start | bytes 786440 | tf_op jit(solution)/shard_map/ppermute | solution.py:20
  30.8 30.1 %collective-permute-start.9 = (bf16[2,128,512]{2,1,0:T(8,128)(2,1)}, bf16[2,128,512]{2,1,0:T(8,128)(2,1)}, u32[]{:S(2)}, u32[]{:S(2)}) collective-permute-start(bf16[2,128,512]{2,1,0:T(8,128)(2,1)} %collective-permute-done.4.refs_9_), channel_id=1, source_target_pairs={{0,8},{8,0},{16,24},{24,16},{1,9},{9,1},{17,25},{25,17},{2,10},{10... | collective-permute-start | bytes 786440 | tf_op jit(solution)/shard_map/ppermute | solution.py:20
  53.7 3.7 %collective-permute-start.14 = (f32[8,256]{1,0:T(8,128)S(1)}, f32[8,256]{1,0:T(8,128)S(1)}, u32[]{:S(2)}, u32[]{:S(2)}) collective-permute-start(f32[8,256]{1,0:T(8,128)S(1)} %get-tuple-element.34.stat), channel_id=1, source_target_pairs={{0,8},{8,0},{16,24},{24,16},{1,9},{9,1},{17,25},{25,17},{2,10},{10... | collective-permute-start | bytes 24584 | tf_op jit(solution)/shard_map/ppermute | solution.py:20
  54.7 2.7 %collective-permute-start.10 = (f32[8,256]{1,0:T(8,128)S(1)}, f32[8,256]{1,0:T(8,128)S(1)}, u32[]{:S(2)}, u32[]{:S(2)}) collective-permute-start(f32[8,256]{1,0:T(8,128)S(1)} %get-tuple-element.34.stat), channel_id=1, source_target_pairs={{0,1},{1,0},{2,3},{3,2},{4,5},{5,4},{6,7},{7,6},{8,9},{9,8},{10,11... | collective-permute-start | bytes 24584 | tf_op jit(solution)/shard_map/ppermute | solution.py:20
  57.4 7.6 %collective-permute-start.11 = (f32[2,8,256]{2,1,0:T(8,128)S(1)}, f32[2,8,256]{2,1,0:T(8,128)S(1)}, u32[]{:S(2)}, u32[]{:S(2)}) collective-permute-start(f32[2,8,256]{2,1,0:T(8,128)S(1)} %get-tuple-element.45.refs_10_), channel_id=1, source_target_pairs={{0,2},{1,3},{2,0},{3,1},{4,6},{5,7},{6,4},{7,5},{8,10},{9,11},{10,... | collective-permute-start | bytes 49160 | tf_op jit(solution)/shard_map/ppermute | solution.py:20
  58.4 6.6 %collective-permute-start.12 = (f32[2,8,256]{2,1,0:T(8,128)S(1)}, f32[2,8,256]{2,1,0:T(8,128)S(1)}, u32[]{:S(2)}, u32[]{:S(2)}) collective-permute-start(f32[2,8,256]{2,1,0:T(8,128)S(1)} %get-tuple-element.45.refs_10_), channel_id=1, source_target_pairs={{0,4},{1,5},{2,6},{3,7},{4,0},{5,1},{6,2},{7,3},{8,12},{9,13},{10,... | collective-permute-start | bytes 49160 | tf_op jit(solution)/shard_map/ppermute | solution.py:20
  59.9 5.2 %collective-permute-start.13 = (f32[2,8,256]{2,1,0:T(8,128)S(1)}, f32[2,8,256]{2,1,0:T(8,128)S(1)}, u32[]{:S(2)}, u32[]{:S(2)}) collective-permute-start(f32[2,8,256]{2,1,0:T(8,128)S(1)} %get-tuple-element.45.refs_10_), channel_id=1, source_target_pairs={{0,6},{1,7},{2,4},{3,5},{4,2},{5,3},{6,0},{7,1},{8,14},{9,15},{10,... | collective-permute-start | bytes 49160 | tf_op jit(solution)/shard_map/ppermute | solution.py:20
  60.9 4.6 %collective-permute-start.15 = (f32[2,8,256]{2,1,0:T(8,128)S(1)}, f32[2,8,256]{2,1,0:T(8,128)S(1)}, u32[]{:S(2)}, u32[]{:S(2)}) collective-permute-start(f32[2,8,256]{2,1,0:T(8,128)S(1)} %get-tuple-element.44.refs_14_), channel_id=1, source_target_pairs={{0,16},{8,24},{16,0},{24,8},{1,17},{9,25},{17,1},{25,9},{2,18},{10... | collective-permute-start | bytes 49160 | tf_op jit(solution)/shard_map/ppermute | solution.py:20
  63.1 2.4 %copy-start.5 = (bf16[2,128,512]{2,1,0:T(8,128)(2,1)S(1)}, bf16[2,128,512]{2,1,0:T(8,128)(2,1)}, u32[]{:S(2)}) copy-start(bf16[2,128,512]{2,1,0:T(8,128)(2,1)} %copy-done.4) | copy-start | bytes 786436
  63.1 2.4 %copy-start.8 = (s32[8,64]{1,0:T(8,128)S(1)}, s32[8,64]{1,0:T(8,128)}, u32[]{:S(2)}) copy-start(s32[8,64]{1,0:T(8,128)} %get-tuple-element.37.refs_0_) | copy-start | bytes 6148
  (2 other events, 4.8 us)

commit v4 on v3

--- a/solution.py
+++ b/solution.py
@@ -368,9 +368,12 @@
         compiler_params=pltpu.CompilerParams(vmem_limit_bytes=PLAN_VMEM_BYTES),
         cost_estimate=pl.CostEstimate(flops=0, bytes_accessed=PLAN_BYTES, transcendentals=0),
     )(candidates.T, owner_map.reshape(1, -1), row_weight, positives, passages)
-    far_out, near_out, near_queries, far_queries = lax.optimization_barrier(
-        (far_out, near_out, near_queries, far_queries)
-    )
+    farthest = far_queries.pop(groups - 1)
+    farthest, near_queries, far_queries, far_out, near_out = lax.optimization_barrier(
+        (farthest, near_queries[::-1], far_queries, far_out, near_out)
+    )
+    near_queries = near_queries[::-1]
+    far_queries[groups - 1] = farthest
     far_blocks = [swap(far_out[mask - 1], "group", mask) for mask in range(1, groups)]
     near_blocks = lax.all_to_all(near_out, "dp", split_axis=0, concat_axis=0, tiled=True)
     mask = groups // 2 - 1

time: 70.4 us -> 69.7 us (0.990)
  starting transfers between devices: 24.5 us -> 22.2 us
  waiting for transfers between devices: 31 us -> 32.7 us
    ppermute x16, starting transfers between devices: 20.7 us -> 18.4 us  [swap(): return lax.ppermute(x, axis, [(i, i ^ mask) for i in range(size)])]
    ppermute x16, waiting for transfers between devices: 10.4 us -> 12.1 us  [swap(): return lax.ppermute(x, axis, [(i, i ^ mask) for i in range(size)])]
  transfers between devices with their start and end apart: 17 -> 17, of which waited for: 5 -> 8; matrix products, arithmetic and copies ran while one was open for 2% -> 2% of each run, Pallas kernels for 12% -> 12%
where the time goes in v4:
time: 69.7 us; the launch traced here: 69.5 us
  waiting for transfers between devices  32.7 us (47%)
  starting transfers between devices  22.2 us (32%)
  Pallas kernels  12.8 us (18%)
  other arithmetic  1.1 us (2%)
  between operations  0.74 us (1%)
    all_to_all x1, waiting for transfers between devices, shards(): lax.all_to_all(near_out, 'dp', split_axis=0, concat_axis=0, tiled=True)  20.6 us
    ppermute x16, starting transfers between devices, swap(): return lax.ppermute(x, axis, [(i, i ^ mask) for i in range(size)])  18.4 us
    ppermute x16, waiting for transfers between devices, swap(): return lax.ppermute(x, axis, [(i, i ^ mask) for i in range(size)])  12.1 us
    pallas_call x4, Pallas kernels, local_call(): pl.pallas_call(kernel, out_shape=outs, in_specs=[smem] * len(tables) + [v...  8.82 us
    pallas_call x1, Pallas kernels, shards(): pl.pallas_call(functools.partial(plan_kernel, scale, cap, near_cap, far_c...  3.94 us
    all_to_all x1, starting transfers between devices, shards(): lax.all_to_all(near_out, 'dp', split_axis=0, concat_axis=0, tiled=True)  3.74 us
  transfers between devices with their start and end apart: 17, of which 8 were waited for; matrix products, arithmetic and copies ran while one was open for 2% of the time, Pallas kernels for 12%

profile of v4, /device:TPU:0, one launch (start us, length us, event | category | flops | bytes accessed | tf_op | source)
XLA Modules:
  0.0 69.5 jit_solution(3299723930244538367)
XLA Ops:
  0.6 5.1 %collective-permute-start = (bf16[2,128,512]{2,1,0:T(8,128)(2,1)}, bf16[2,128,512]{2,1,0:T(8,128)(2,1)}, u32[]{:S(2)}, u32[]{:S(2)}) collective-permute-start(bf16[2,128,512]{2,1,0:T(8,128)(2,1)} %refs_2_.2), channel_id=1, source_target_pairs={{0,24},{8,16},{16,8},{24,0},{1,25},{9,17},{17,9},{25,1},{2,26},{10... | collective-permute-start | bytes 786440 | tf_op jit(solution)/shard_map/ppermute | solution.py:20
  5.7 2.4 %collective-permute-start.1 = (bf16[2,128,512]{2,1,0:T(8,128)(2,1)}, bf16[2,128,512]{2,1,0:T(8,128)(2,1)S(1)}, u32[]{:S(2)}, u32[]{:S(2)}) collective-permute-start(bf16[2,128,512]{2,1,0:T(8,128)(2,1)} %refs_2_.2), channel_id=1, source_target_pairs={{0,6},{1,7},{2,4},{3,5},{4,2},{5,3},{6,0},{7,1},{8,14},{9,15},{10,... | collective-permute-start | bytes 786440 | tf_op jit(solution)/shard_map/ppermute | solution.py:20
  8.2 0.5 collective-permute-start.2
  8.7 0.5 collective-permute-start.3
  9.2 3.9 %shard_map.77 = (bf16[2,128,512]{2,1,0:T(8,128)(2,1)}, bf16[2,128,512]{2,1,0:T(8,128)(2,1)}, bf16[2,128,512]{2,1,0:T(8,128)(2,1)}, bf16[16,128,512]{2,1,0:T(8,12...) custom-call(s32[16,64]{1,0:T(8,128)} %bitcast.6, s32[1,192]{1,0:T(1,128)} %bitcast.9, ...), custom_call_target="tpu_custom_call" | custom-call | bytes 16777216 | tf_op jit(solution)/shard_map/pallas_call | solution.py:342
  13.2 2.9 %collective-permute-done.1.refs_5_ = bf16[2,128,512]{2,1,0:T(8,128)(2,1)S(1)} collective-permute-done((bf16[2,128,512]{2,1,0:T(8,128)(2,1)}, bf16[2,128,512]{2,1,0:T(8,128)(2,1)S(1)}, u32[]{:S(2)}, u32[]{:S(2)}) %collective-permute-start.1) | collective-permute-done | bytes 262176 | tf_op jit(solution)/shard_map/ppermute | solution.py:20
  16.1 4.1 %collective-permute-done.2.refs_4_ = bf16[2,128,512]{2,1,0:T(8,128)(2,1)S(1)} collective-permute-done((bf16[2,128,512]{2,1,0:T(8,128)(2,1)}, bf16[2,128,512]{2,1,0:T(8,128)(2,1)S(1)}, u32[]{:S(2)}, u32[]{:S(2)}) %collective-permute-start.2) | collective-permute-done | bytes 262176 | tf_op jit(solution)/shard_map/ppermute | solution.py:20
  20.3 3.7 %all-to-all-start = ((bf16[16,128,512]{2,1,0:T(8,128)(2,1)}), bf16[16,128,512]{2,1,0:T(8,128)(2,1)S(1)}, u32[]{:S(2)}, u32[]{:S(2)}) async-start(bf16[16,128,512]{2,1,0:T(8,128)(2,1)} %get-tuple-element.29), calls=%async_computation | async-start | bytes 4194304 | tf_op jit(solution)/shard_map/all_to_all | solution.py:378
  24.1 1.1 %pad_maximum_fusion = bf16[8,128,512]{2,1,0:T(8,128)(2,1)} fusion(bf16[2,128,512]{2,1,0:T(8,128)(2,1)S(1)} %collective-permute-done.1.refs_5_, bf16[2,128,512]{2,1,0:T(8,128)(2,1)S(1)} %collective-permute-done.2.refs_4_, bf16[2,128,512]{2,1,0:T(8,128)(2,1)S(1)} %collective-permute-done.3.refs_3_, bf16[2,128,512]{2,1,0:T(8,128)(2,1)S(1)} %copy-done), kind=kLoop, calls=%fused_computation | loop fusion | flops 1572864 | bytes 2097152 | tf_op jit(solution)/shard_map/concatenate | solution.py:385
  25.6 2.0 %collective-permute-start.6 = (bf16[2,128,512]{2,1,0:T(8,128)(2,1)}, bf16[2,128,512]{2,1,0:T(8,128)(2,1)S(1)}, u32[]{:S(2)}, u32[]{:S(2)}) collective-permute-start(bf16[2,128,512]{2,1,0:T(8,128)(2,1)} %get-tuple-element.32), channel_id=1, source_target_pairs={{0,16},{8,24},{16,0},{24,8},{1,17},{9,25},{17,1},{25,9},{2,18},{10... | collective-permute-start | bytes 786440 | tf_op jit(solution)/shard_map/ppermute | solution.py:20
  27.7 2.3 %collective-permute-start.7 = (bf16[2,128,512]{2,1,0:T(8,128)(2,1)}, bf16[2,128,512]{2,1,0:T(8,128)(2,1)S(1)}, u32[]{:S(2)}, u32[]{:S(2)}) collective-permute-start(bf16[2,128,512]{2,1,0:T(8,128)(2,1)} %get-tuple-element.33), channel_id=1, source_target_pairs={{0,24},{8,16},{16,8},{24,0},{1,25},{9,17},{17,9},{25,1},{2,26},{10... | collective-permute-start | bytes 786440 | tf_op jit(solution)/shard_map/ppermute | solution.py:20
  30.0 20.6 %all-to-all-done.near = bf16[16,128,512]{2,1,0:T(8,128)(2,1)S(1)} async-done(((bf16[16,128,512]{2,1,0:T(8,128)(2,1)}), bf16[16,128,512]{2,1,0:T(8,128)(2,1)S(1)}, u32[]{:S(2)}, u32[]{:S(2)}) %all-to-all-start) | async-done | bytes 2097184 | tf_op jit(solution)/shard_map/all_to_all | solution.py:378
  50.7 1.1 %shard_map.78 = (f32[256,128]{1,0:T(8,128)S(1)}, f32[256,2048]{1,0:T(8,128)S(1)}) custom-call(bf16[2,128,512]{2,1,0:T(8,128)(2,1)S(1)} %copy-done, f32[8,2816]{1,0:T(8,128)S(1)} %copy-done.6, bf16[16,128,512]{2,1,0:T(8,128)(2,1)S(1)} %all-to-all-done.near), custom_call_target="tpu_custom_call" | custom-call | bytes 67108864 | tf_op jit(solution)/shard_map/pallas_call | solution.py:26
  51.8 1.2 %shard_map.79 = (f32[8,256]{1,0:T(8,128)S(1)}, f32[256,768]{1,0:T(8,128)S(1)}) custom-call(bf16[2,128,512]{2,1,0:T(8,128)(2,1)S(1)} %copy-done, f32[8,256]{1,0:T(8,128)S(1)} %copy-done.7, f32[8,2816]{1,0:T(8,128)S(1)} %copy-done.6, f32[256,128]{1,0:T(8,128)S(1)} %get-tuple-element.30.near_stat, bf16[2,128,512]{2,1,0:T(8,128)(2,1)S(1)} %collective-permute-done.5.refs_0_, ...), custom_call_target="tpu_custom_call" | custom-call | tf_op jit(solution)/shard_map/pallas_call | solution.py:26
  53.0 0.8 %collective-permute-start.14 = (f32[8,256]{1,0:T(8,128)S(1)}, f32[8,256]{1,0:T(8,128)S(1)}, u32[]{:S(2)}, u32[]{:S(2)}) collective-permute-start(f32[8,256]{1,0:T(8,128)S(1)} %get-tuple-element.34.stat), channel_id=1, source_target_pairs={{0,8},{8,0},{16,24},{24,16},{1,9},{9,1},{17,25},{25,17},{2,10},{10... | collective-permute-start | bytes 24584 | tf_op jit(solution)/shard_map/ppermute | solution.py:20
  53.8 2.9 %collective-permute-done.14 = f32[8,256]{1,0:T(8,128)S(1)} collective-permute-done((f32[8,256]{1,0:T(8,128)S(1)}, f32[8,256]{1,0:T(8,128)S(1)}, u32[]{:S(2)}, u32[]{:S(2)}) %collective-permute-start.14) | collective-permute-done | bytes 8224 | tf_op jit(solution)/shard_map/ppermute | solution.py:20
  56.7 0.7 collective-permute-start.11
  57.3 1.5 %collective-permute-start.12 = (f32[2,8,256]{2,1,0:T(8,128)S(1)}, f32[2,8,256]{2,1,0:T(8,128)S(1)}, u32[]{:S(2)}, u32[]{:S(2)}) collective-permute-start(f32[2,8,256]{2,1,0:T(8,128)S(1)} %get-tuple-element.45.refs_10_), channel_id=1, source_target_pairs={{0,4},{1,5},{2,6},{3,7},{4,0},{5,1},{6,2},{7,3},{8,12},{9,13},{10,... | collective-permute-start | bytes 49160 | tf_op jit(solution)/shard_map/ppermute | solution.py:20
  58.8 1.3 %collective-permute-start.13 = (f32[2,8,256]{2,1,0:T(8,128)S(1)}, f32[2,8,256]{2,1,0:T(8,128)S(1)}, u32[]{:S(2)}, u32[]{:S(2)}) collective-permute-start(f32[2,8,256]{2,1,0:T(8,128)S(1)} %get-tuple-element.45.refs_10_), channel_id=1, source_target_pairs={{0,6},{1,7},{2,4},{3,5},{4,2},{5,3},{6,0},{7,1},{8,14},{9,15},{10,... | collective-permute-start | bytes 49160 | tf_op jit(solution)/shard_map/ppermute | solution.py:20
  60.2 0.8 %collective-permute-start.15 = (f32[2,8,256]{2,1,0:T(8,128)S(1)}, f32[2,8,256]{2,1,0:T(8,128)S(1)}, u32[]{:S(2)}, u32[]{:S(2)}) collective-permute-start(f32[2,8,256]{2,1,0:T(8,128)S(1)} %get-tuple-element.44.refs_14_), channel_id=1, source_target_pairs={{0,16},{8,24},{16,0},{24,8},{1,17},{9,25},{17,1},{25,9},{2,18},{10... | collective-permute-start | bytes 49160 | tf_op jit(solution)/shard_map/ppermute | solution.py:20
  60.9 1.9 %shard_map.80 = bf16[2,128,512]{2,1,0:T(8,128)(2,1)} custom-call(f32[8,2816]{1,0:T(8,128)S(1)} %copy-done.6, f32[8,256]{1,0:T(8,128)S(1)} %get-tuple-element.34.stat, f32[256,2048]{1,0:T(8,128)S(1)} %get-tuple-element.35.near_scores, f32[256,768]{1,0:T(8,128)S(1)} %get-tuple-element.36.far_scores, bf16[16,128,512]{2,1,0:T(8,128)(2,1)S(1)} %all-to-all-done.near, ...), custom_call_target="tpu_custom_call" | custom-call | bytes 67108864 | tf_op jit(solution)/shard_map/pallas_call | solution.py:26
  62.8 0.6 collective-permute-done.13.refs_13_
  63.5 1.4 %collective-permute-done.15.refs_15_ = f32[2,8,256]{2,1,0:T(8,128)S(1)} collective-permute-done((f32[2,8,256]{2,1,0:T(8,128)S(1)}, f32[2,8,256]{2,1,0:T(8,128)S(1)}, u32[]{:S(2)}, u32[]{:S(2)}) %collective-permute-start.15) | collective-permute-done | bytes 16416 | tf_op jit(solution)/shard_map/ppermute | solution.py:20
  64.8 4.7 %shard_map.81 = bf16[6,128,512]{2,1,0:T(8,128)(2,1)} custom-call(s32[8,64]{1,0:T(8,128)S(1)} %copy-done.8, bf16[6,128,512]{2,1,0:T(8,128)(2,1)S(1)} %copy-done.1, bf16[2,128,512]{2,1,0:T(8,128)(2,1)S(1)} %copy-done, bf16[2,128,512]{2,1,0:T(8,128)(2,1)S(1)} %copy-done.5, bf16[2,128,512]{2,1,0:T(8,128)(2,1)S(1)} %copy-done.3, ...), custom_call_target="tpu_custom_call" | custom-call | tf_op jit(solution)/shard_map/pallas_call | solution.py:26
  (35 shorter events, 0.6 us)
Async XLA Ops:
  0.6 12.6 %collective-permute-start = (bf16[2,128,512]{2,1,0:T(8,128)(2,1)}, bf16[2,128,512]{2,1,0:T(8,128)(2,1)}, u32[]{:S(2)}, u32[]{:S(2)}) collective-permute-start(bf16[2,128,512]{2,1,0:T(8,128)(2,1)} %refs_2_.2), channel_id=1, source_target_pairs={{0,24},{8,16},{16,8},{24,0},{1,25},{9,17},{17,9},{25,1},{2,26},{10... | collective-permute-start | bytes 786440 | tf_op jit(solution)/shard_map/ppermute | solution.py:20
  5.7 10.4 %collective-permute-start.1 = (bf16[2,128,512]{2,1,0:T(8,128)(2,1)}, bf16[2,128,512]{2,1,0:T(8,128)(2,1)S(1)}, u32[]{:S(2)}, u32[]{:S(2)}) collective-permute-start(bf16[2,128,512]{2,1,0:T(8,128)(2,1)} %refs_2_.2), channel_id=1, source_target_pairs={{0,6},{1,7},{2,4},{3,5},{4,2},{5,3},{6,0},{7,1},{8,14},{9,15},{10,... | collective-permute-start | bytes 786440 | tf_op jit(solution)/shard_map/ppermute | solution.py:20
  8.2 12.0 %collective-permute-start.2 = (bf16[2,128,512]{2,1,0:T(8,128)(2,1)}, bf16[2,128,512]{2,1,0:T(8,128)(2,1)S(1)}, u32[]{:S(2)}, u32[]{:S(2)}) collective-permute-start(bf16[2,128,512]{2,1,0:T(8,128)(2,1)} %refs_2_.2), channel_id=1, source_target_pairs={{0,4},{1,5},{2,6},{3,7},{4,0},{5,1},{6,2},{7,3},{8,12},{9,13},{10,... | collective-permute-start | bytes 786440 | tf_op jit(solution)/shard_map/ppermute | solution.py:20
  8.7 11.6 %collective-permute-start.3 = (bf16[2,128,512]{2,1,0:T(8,128)(2,1)}, bf16[2,128,512]{2,1,0:T(8,128)(2,1)S(1)}, u32[]{:S(2)}, u32[]{:S(2)}) collective-permute-start(bf16[2,128,512]{2,1,0:T(8,128)(2,1)} %refs_2_.2), channel_id=1, source_target_pairs={{0,2},{1,3},{2,0},{3,1},{4,6},{5,7},{6,4},{7,5},{8,10},{9,11},{10,... | collective-permute-start | bytes 786440 | tf_op jit(solution)/shard_map/ppermute | solution.py:20
  9.2 11.1 %collective-permute-start.4 = (bf16[2,128,512]{2,1,0:T(8,128)(2,1)}, bf16[2,128,512]{2,1,0:T(8,128)(2,1)}, u32[]{:S(2)}, u32[]{:S(2)}) collective-permute-start(bf16[2,128,512]{2,1,0:T(8,128)(2,1)} %refs_2_.2), channel_id=1, source_target_pairs={{0,8},{8,0},{16,24},{24,16},{1,9},{9,1},{17,25},{25,17},{2,10},{10... | collective-permute-start | bytes 786440 | tf_op jit(solution)/shard_map/ppermute | solution.py:20
  20.2 3.9 %copy-start.2 = (bf16[2,128,512]{2,1,0:T(8,128)(2,1)}, bf16[2,128,512]{2,1,0:T(8,128)(2,1)S(1)}, u32[]{:S(2)}) copy-start(bf16[2,128,512]{2,1,0:T(8,128)(2,1)S(1)} %collective-permute-done.2.refs_4_) | copy-start | bytes 786436
  20.3 30.3 %all-to-all-start = ((bf16[16,128,512]{2,1,0:T(8,128)(2,1)}), bf16[16,128,512]{2,1,0:T(8,128)(2,1)S(1)}, u32[]{:S(2)}, u32[]{:S(2)}) async-start(bf16[16,128,512]{2,1,0:T(8,128)(2,1)} %get-tuple-element.29), calls=%async_computation | async-start | bytes 4194304 | tf_op jit(solution)/shard_map/all_to_all | solution.py:378
  24.1 26.5 %copy-start.6 = (f32[8,2816]{1,0:T(8,128)S(1)}, f32[8,2816]{1,0:T(8,128)}, u32[]{:S(2)}) copy-start(f32[8,2816]{1,0:T(8,128)} %get-tuple-element.23.numbers) | copy-start | bytes 270340
  24.1 27.7 %copy-start.7 = (f32[8,256]{1,0:T(8,128)S(1)}, f32[8,256]{1,0:T(8,128)}, u32[]{:S(2)}) copy-start(f32[8,256]{1,0:T(8,128)} %get-tuple-element.24.row_data) | copy-start | bytes 24580
  25.2 37.6 %collective-permute-start.8 = (bf16[8,128,512]{2,1,0:T(8,128)(2,1)}, bf16[8,128,512]{2,1,0:T(8,128)(2,1)}, u32[]{:S(2)}, u32[]{:S(2)}) collective-permute-start(bf16[8,128,512]{2,1,0:T(8,128)(2,1)} %pad_maximum_fusion), channel_id=1, source_target_pairs={{0,1},{1,0},{2,3},{3,2},{4,5},{5,4},{6,7},{7,6},{8,9},{9,8},{10,11... | collective-permute-start | bytes 3145736 | tf_op jit(solution)/shard_map/ppermute | solution.py:20
  25.6 26.2 %collective-permute-start.5 = (bf16[2,128,512]{2,1,0:T(8,128)(2,1)}, bf16[2,128,512]{2,1,0:T(8,128)(2,1)S(1)}, u32[]{:S(2)}, u32[]{:S(2)}) collective-permute-start(bf16[2,128,512]{2,1,0:T(8,128)(2,1)} %get-tuple-element.31), channel_id=1, source_target_pairs={{0,8},{8,0},{16,24},{24,16},{1,9},{9,1},{17,25},{25,17},{2,10},{10... | collective-permute-start | bytes 786440 | tf_op jit(solution)/shard_map/ppermute | solution.py:20
  25.6 26.2 %collective-permute-start.6 = (bf16[2,128,512]{2,1,0:T(8,128)(2,1)}, bf16[2,128,512]{2,1,0:T(8,128)(2,1)S(1)}, u32[]{:S(2)}, u32[]{:S(2)}) collective-permute-start(bf16[2,128,512]{2,1,0:T(8,128)(2,1)} %get-tuple-element.32), channel_id=1, source_target_pairs={{0,16},{8,24},{16,0},{24,8},{1,17},{9,25},{17,1},{25,9},{2,18},{10... | collective-permute-start | bytes 786440 | tf_op jit(solution)/shard_map/ppermute | solution.py:20
  27.7 24.1 %collective-permute-start.7 = (bf16[2,128,512]{2,1,0:T(8,128)(2,1)}, bf16[2,128,512]{2,1,0:T(8,128)(2,1)S(1)}, u32[]{:S(2)}, u32[]{:S(2)}) collective-permute-start(bf16[2,128,512]{2,1,0:T(8,128)(2,1)} %get-tuple-element.33), channel_id=1, source_target_pairs={{0,24},{8,16},{16,8},{24,0},{1,25},{9,17},{17,9},{25,1},{2,26},{10... | collective-permute-start | bytes 786440 | tf_op jit(solution)/shard_map/ppermute | solution.py:20
  30.0 30.1 %collective-permute-start.9 = (bf16[2,128,512]{2,1,0:T(8,128)(2,1)}, bf16[2,128,512]{2,1,0:T(8,128)(2,1)}, u32[]{:S(2)}, u32[]{:S(2)}) collective-permute-start(bf16[2,128,512]{2,1,0:T(8,128)(2,1)} %collective-permute-done.refs_9_), channel_id=1, source_target_pairs={{0,8},{8,0},{16,24},{24,16},{1,9},{9,1},{17,25},{25,17},{2,10},{10... | collective-permute-start | bytes 786440 | tf_op jit(solution)/shard_map/ppermute | solution.py:20
  53.0 3.7 %collective-permute-start.14 = (f32[8,256]{1,0:T(8,128)S(1)}, f32[8,256]{1,0:T(8,128)S(1)}, u32[]{:S(2)}, u32[]{:S(2)}) collective-permute-start(f32[8,256]{1,0:T(8,128)S(1)} %get-tuple-element.34.stat), channel_id=1, source_target_pairs={{0,8},{8,0},{16,24},{24,16},{1,9},{9,1},{17,25},{25,17},{2,10},{10... | collective-permute-start | bytes 24584 | tf_op jit(solution)/shard_map/ppermute | solution.py:20
  53.8 2.9 %collective-permute-start.10 = (f32[8,256]{1,0:T(8,128)S(1)}, f32[8,256]{1,0:T(8,128)S(1)}, u32[]{:S(2)}, u32[]{:S(2)}) collective-permute-start(f32[8,256]{1,0:T(8,128)S(1)} %get-tuple-element.34.stat), channel_id=1, source_target_pairs={{0,1},{1,0},{2,3},{3,2},{4,5},{5,4},{6,7},{7,6},{8,9},{9,8},{10,11... | collective-permute-start | bytes 24584 | tf_op jit(solution)/shard_map/ppermute | solution.py:20
  56.7 6.1 %collective-permute-start.11 = (f32[2,8,256]{2,1,0:T(8,128)S(1)}, f32[2,8,256]{2,1,0:T(8,128)S(1)}, u32[]{:S(2)}, u32[]{:S(2)}) collective-permute-start(f32[2,8,256]{2,1,0:T(8,128)S(1)} %get-tuple-element.45.refs_10_), channel_id=1, source_target_pairs={{0,2},{1,3},{2,0},{3,1},{4,6},{5,7},{6,4},{7,5},{8,10},{9,11},{10,... | collective-permute-start | bytes 49160 | tf_op jit(solution)/shard_map/ppermute | solution.py:20
  57.3 5.5 %collective-permute-start.12 = (f32[2,8,256]{2,1,0:T(8,128)S(1)}, f32[2,8,256]{2,1,0:T(8,128)S(1)}, u32[]{:S(2)}, u32[]{:S(2)}) collective-permute-start(f32[2,8,256]{2,1,0:T(8,128)S(1)} %get-tuple-element.45.refs_10_), channel_id=1, source_target_pairs={{0,4},{1,5},{2,6},{3,7},{4,0},{5,1},{6,2},{7,3},{8,12},{9,13},{10,... | collective-permute-start | bytes 49160 | tf_op jit(solution)/shard_map/ppermute | solution.py:20
  58.8 4.6 %collective-permute-start.13 = (f32[2,8,256]{2,1,0:T(8,128)S(1)}, f32[2,8,256]{2,1,0:T(8,128)S(1)}, u32[]{:S(2)}, u32[]{:S(2)}) collective-permute-start(f32[2,8,256]{2,1,0:T(8,128)S(1)} %get-tuple-element.45.refs_10_), channel_id=1, source_target_pairs={{0,6},{1,7},{2,4},{3,5},{4,2},{5,3},{6,0},{7,1},{8,14},{9,15},{10,... | collective-permute-start | bytes 49160 | tf_op jit(solution)/shard_map/ppermute | solution.py:20
  60.2 4.6 %collective-permute-start.15 = (f32[2,8,256]{2,1,0:T(8,128)S(1)}, f32[2,8,256]{2,1,0:T(8,128)S(1)}, u32[]{:S(2)}, u32[]{:S(2)}) collective-permute-start(f32[2,8,256]{2,1,0:T(8,128)S(1)} %get-tuple-element.44.refs_14_), channel_id=1, source_target_pairs={{0,16},{8,24},{16,0},{24,8},{1,17},{9,25},{17,1},{25,9},{2,18},{10... | collective-permute-start | bytes 49160 | tf_op jit(solution)/shard_map/ppermute | solution.py:20
  60.9 3.9 %copy-start.1 = (bf16[6,128,512]{2,1,0:T(8,128)(2,1)S(1)}, bf16[6,128,512]{2,1,0:T(8,128)(2,1)}, u32[]{:S(2)}) copy-start(bf16[6,128,512]{2,1,0:T(8,128)(2,1)} %refs_1_.1) | copy-start | bytes 2359300
  60.9 3.9 %copy-start.3 = (bf16[2,128,512]{2,1,0:T(8,128)(2,1)S(1)}, bf16[2,128,512]{2,1,0:T(8,128)(2,1)}, u32[]{:S(2)}) copy-start(bf16[2,128,512]{2,1,0:T(8,128)(2,1)} %copy-done.2) | copy-start | bytes 786436
  60.9 3.9 %copy-start.5 = (bf16[2,128,512]{2,1,0:T(8,128)(2,1)S(1)}, bf16[2,128,512]{2,1,0:T(8,128)(2,1)}, u32[]{:S(2)}) copy-start(bf16[2,128,512]{2,1,0:T(8,128)(2,1)} %copy-done.4) | copy-start | bytes 786436
  60.9 3.9 %copy-start.8 = (s32[8,64]{1,0:T(8,128)S(1)}, s32[8,64]{1,0:T(8,128)}, u32[]{:S(2)}) copy-start(s32[8,64]{1,0:T(8,128)} %get-tuple-element.37.refs_0_) | copy-start | bytes 6148
  (2 other events, 7.5 us)

commit v5 on v4

--- a/solution.py
+++ b/solution.py
@@ -213,7 +213,7 @@
 
 
 def far_pieces(fars):
-    for ref in fars:
+    for ref in fars[::-1]:
         yield ref[...].reshape(-1, ref.shape[-1])
 
 
@@ -399,7 +399,7 @@
     stat, far_scores = local_call(
         functools.partial(stats_kernel, scale, near_slots * block_rows),
         [],
-        [queries, row_data, numbers, near_stat, *far_blocks],
+        [queries, row_data, numbers, near_stat, *far_blocks[::-1]],
         [
             jax.ShapeDtypeStruct((8, rows), jnp.float32),
             jax.ShapeDtypeStruct((rows, far_slots * block_rows), jnp.float32),
@@ -414,7 +414,7 @@
     grad_query = local_call(
         functools.partial(query_kernel, columns),
         [],
-        [numbers, stat, near_scores, far_scores, near_blocks, *far_blocks],
+        [numbers, stat, near_scores, far_scores, near_blocks, *far_blocks[::-1]],
         jax.ShapeDtypeStruct(queries.shape, dtype),
         [
             pltpu.VMEM((rows, width), jnp.float32),

time: 69.7 us -> 69.7 us (level)
  starting transfers between devices: 22.2 us -> 20.8 us
  waiting for transfers between devices: 32.7 us -> 34.1 us
    ppermute x16, starting transfers between devices: 18.4 us -> 17 us  [swap(): return lax.ppermute(x, axis, [(i, i ^ mask) for i in range(size)])]
    ppermute x16, waiting for transfers between devices: 12.1 us -> 13.4 us  [swap(): return lax.ppermute(x, axis, [(i, i ^ mask) for i in range(size)])]
where the time goes in v5:
time: 69.7 us; the launch traced here: 69.5 us
  waiting for transfers between devices  34.1 us (49%)
  starting transfers between devices  20.8 us (30%)
  Pallas kernels  12.8 us (18%)
  other arithmetic  1.1 us (2%)
  between operations  0.78 us (1%)
    all_to_all x1, waiting for transfers between devices, shards(): lax.all_to_all(near_out, 'dp', split_axis=0, concat_axis=0, tiled=True)  20.6 us
    ppermute x16, starting transfers between devices, swap(): return lax.ppermute(x, axis, [(i, i ^ mask) for i in range(size)])  17 us
    ppermute x16, waiting for transfers between devices, swap(): return lax.ppermute(x, axis, [(i, i ^ mask) for i in range(size)])  13.4 us
    pallas_call x4, Pallas kernels, local_call(): pl.pallas_call(kernel, out_shape=outs, in_specs=[smem] * len(tables) + [v...  8.82 us
    pallas_call x1, Pallas kernels, shards(): pl.pallas_call(functools.partial(plan_kernel, scale, cap, near_cap, far_c...  3.94 us
    all_to_all x1, starting transfers between devices, shards(): lax.all_to_all(near_out, 'dp', split_axis=0, concat_axis=0, tiled=True)  3.74 us
  transfers between devices with their start and end apart: 17, of which 8 were waited for; matrix products, arithmetic and copies ran while one was open for 2% of the time, Pallas kernels for 12%

profile of v5, /device:TPU:0, one launch (start us, length us, event | category | flops | bytes accessed | tf_op | source)
XLA Modules:
  0.0 69.5 jit_solution(18392283192459124238)
XLA Ops:
  0.6 5.1 %collective-permute-start = (bf16[2,128,512]{2,1,0:T(8,128)(2,1)}, bf16[2,128,512]{2,1,0:T(8,128)(2,1)}, u32[]{:S(2)}, u32[]{:S(2)}) collective-permute-start(bf16[2,128,512]{2,1,0:T(8,128)(2,1)} %refs_2_.2), channel_id=1, source_target_pairs={{0,24},{8,16},{16,8},{24,0},{1,25},{9,17},{17,9},{25,1},{2,26},{10... | collective-permute-start | bytes 786440 | tf_op jit(solution)/shard_map/ppermute | solution.py:20
  5.7 2.4 %collective-permute-start.1 = (bf16[2,128,512]{2,1,0:T(8,128)(2,1)}, bf16[2,128,512]{2,1,0:T(8,128)(2,1)S(1)}, u32[]{:S(2)}, u32[]{:S(2)}) collective-permute-start(bf16[2,128,512]{2,1,0:T(8,128)(2,1)} %refs_2_.2), channel_id=1, source_target_pairs={{0,6},{1,7},{2,4},{3,5},{4,2},{5,3},{6,0},{7,1},{8,14},{9,15},{10,... | collective-permute-start | bytes 786440 | tf_op jit(solution)/shard_map/ppermute | solution.py:20
  8.2 0.5 collective-permute-start.2
  8.7 0.5 collective-permute-start.3
  9.2 3.9 %shard_map.77 = (bf16[2,128,512]{2,1,0:T(8,128)(2,1)}, bf16[2,128,512]{2,1,0:T(8,128)(2,1)}, bf16[2,128,512]{2,1,0:T(8,128)(2,1)}, bf16[16,128,512]{2,1,0:T(8,12...) custom-call(s32[16,64]{1,0:T(8,128)} %bitcast.6, s32[1,192]{1,0:T(1,128)} %bitcast.9, ...), custom_call_target="tpu_custom_call" | custom-call | bytes 16777216 | tf_op jit(solution)/shard_map/pallas_call | solution.py:342
  13.2 2.9 %collective-permute-done.1.refs_5_ = bf16[2,128,512]{2,1,0:T(8,128)(2,1)S(1)} collective-permute-done((bf16[2,128,512]{2,1,0:T(8,128)(2,1)}, bf16[2,128,512]{2,1,0:T(8,128)(2,1)S(1)}, u32[]{:S(2)}, u32[]{:S(2)}) %collective-permute-start.1) | collective-permute-done | bytes 262176 | tf_op jit(solution)/shard_map/ppermute | solution.py:20
  16.1 4.1 %collective-permute-done.2.refs_4_ = bf16[2,128,512]{2,1,0:T(8,128)(2,1)S(1)} collective-permute-done((bf16[2,128,512]{2,1,0:T(8,128)(2,1)}, bf16[2,128,512]{2,1,0:T(8,128)(2,1)S(1)}, u32[]{:S(2)}, u32[]{:S(2)}) %collective-permute-start.2) | collective-permute-done | bytes 262176 | tf_op jit(solution)/shard_map/ppermute | solution.py:20
  20.2 0.1 collective-permute-done.3.refs_3_
  20.3 3.7 %all-to-all-start = ((bf16[16,128,512]{2,1,0:T(8,128)(2,1)}), bf16[16,128,512]{2,1,0:T(8,128)(2,1)S(1)}, u32[]{:S(2)}, u32[]{:S(2)}) async-start(bf16[16,128,512]{2,1,0:T(8,128)(2,1)} %get-tuple-element.29), calls=%async_computation | async-start | bytes 4194304 | tf_op jit(solution)/shard_map/all_to_all | solution.py:378
  24.1 1.1 %pad_maximum_fusion = bf16[8,128,512]{2,1,0:T(8,128)(2,1)} fusion(bf16[2,128,512]{2,1,0:T(8,128)(2,1)S(1)} %collective-permute-done.1.refs_5_, bf16[2,128,512]{2,1,0:T(8,128)(2,1)S(1)} %collective-permute-done.2.refs_4_, bf16[2,128,512]{2,1,0:T(8,128)(2,1)S(1)} %collective-permute-done.3.refs_3_, bf16[2,128,512]{2,1,0:T(8,128)(2,1)S(1)} %copy-done), kind=kLoop, calls=%fused_computation | loop fusion | flops 1572864 | bytes 2097152 | tf_op jit(solution)/shard_map/concatenate | solution.py:385
  25.2 0.4 collective-permute-start.8
  25.6 1.5 %collective-permute-start.5 = (bf16[2,128,512]{2,1,0:T(8,128)(2,1)}, bf16[2,128,512]{2,1,0:T(8,128)(2,1)S(1)}, u32[]{:S(2)}, u32[]{:S(2)}) collective-permute-start(bf16[2,128,512]{2,1,0:T(8,128)(2,1)} %get-tuple-element.31), channel_id=1, source_target_pairs={{0,24},{8,16},{16,8},{24,0},{1,25},{9,17},{17,9},{25,1},{2,26},{10... | collective-permute-start | bytes 786440 | tf_op jit(solution)/shard_map/ppermute | solution.py:20
  27.1 2.9 %collective-permute-start.7 = (bf16[2,128,512]{2,1,0:T(8,128)(2,1)}, bf16[2,128,512]{2,1,0:T(8,128)(2,1)S(1)}, u32[]{:S(2)}, u32[]{:S(2)}) collective-permute-start(bf16[2,128,512]{2,1,0:T(8,128)(2,1)} %get-tuple-element.33), channel_id=1, source_target_pairs={{0,8},{8,0},{16,24},{24,16},{1,9},{9,1},{17,25},{25,17},{2,10},{10... | collective-permute-start | bytes 786440 | tf_op jit(solution)/shard_map/ppermute | solution.py:20
  30.1 20.6 %all-to-all-done.near = bf16[16,128,512]{2,1,0:T(8,128)(2,1)S(1)} async-done(((bf16[16,128,512]{2,1,0:T(8,128)(2,1)}), bf16[16,128,512]{2,1,0:T(8,128)(2,1)S(1)}, u32[]{:S(2)}, u32[]{:S(2)}) %all-to-all-start) | async-done | bytes 2097184 | tf_op jit(solution)/shard_map/all_to_all | solution.py:378
  50.7 1.1 %shard_map.78 = (f32[256,128]{1,0:T(8,128)S(1)}, f32[256,2048]{1,0:T(8,128)S(1)}) custom-call(bf16[2,128,512]{2,1,0:T(8,128)(2,1)S(1)} %copy-done, f32[8,2816]{1,0:T(8,128)S(1)} %copy-done.6, bf16[16,128,512]{2,1,0:T(8,128)(2,1)S(1)} %all-to-all-done.near), custom_call_target="tpu_custom_call" | custom-call | bytes 67108864 | tf_op jit(solution)/shard_map/pallas_call | solution.py:26
  51.8 1.2 %shard_map.79 = (f32[8,256]{1,0:T(8,128)S(1)}, f32[256,768]{1,0:T(8,128)S(1)}) custom-call(bf16[2,128,512]{2,1,0:T(8,128)(2,1)S(1)} %copy-done, f32[8,256]{1,0:T(8,128)S(1)} %copy-done.7, f32[8,2816]{1,0:T(8,128)S(1)} %copy-done.6, f32[256,128]{1,0:T(8,128)S(1)} %get-tuple-element.30.near_stat, bf16[2,128,512]{2,1,0:T(8,128)(2,1)S(1)} %collective-permute-done.5.refs_0_, ...), custom_call_target="tpu_custom_call" | custom-call | tf_op jit(solution)/shard_map/pallas_call | solution.py:26
  53.1 3.6 %collective-permute-done.14 = f32[8,256]{1,0:T(8,128)S(1)} collective-permute-done((f32[8,256]{1,0:T(8,128)S(1)}, f32[8,256]{1,0:T(8,128)S(1)}, u32[]{:S(2)}, u32[]{:S(2)}) %collective-permute-start.14) | collective-permute-done | bytes 8224 | tf_op jit(solution)/shard_map/ppermute | solution.py:20
  56.7 0.5 collective-permute-start.11
  57.2 1.3 %collective-permute-start.12 = (f32[2,8,256]{2,1,0:T(8,128)S(1)}, f32[2,8,256]{2,1,0:T(8,128)S(1)}, u32[]{:S(2)}, u32[]{:S(2)}) collective-permute-start(f32[2,8,256]{2,1,0:T(8,128)S(1)} %get-tuple-element.45.refs_10_), channel_id=1, source_target_pairs={{0,4},{1,5},{2,6},{3,7},{4,0},{5,1},{6,2},{7,3},{8,12},{9,13},{10,... | collective-permute-start | bytes 49160 | tf_op jit(solution)/shard_map/ppermute | solution.py:20
  58.5 1.7 %collective-permute-start.13 = (f32[2,8,256]{2,1,0:T(8,128)S(1)}, f32[2,8,256]{2,1,0:T(8,128)S(1)}, u32[]{:S(2)}, u32[]{:S(2)}) collective-permute-start(f32[2,8,256]{2,1,0:T(8,128)S(1)} %get-tuple-element.45.refs_10_), channel_id=1, source_target_pairs={{0,6},{1,7},{2,4},{3,5},{4,2},{5,3},{6,0},{7,1},{8,14},{9,15},{10,... | collective-permute-start | bytes 49160 | tf_op jit(solution)/shard_map/ppermute | solution.py:20
  60.2 1.9 %shard_map.80 = bf16[2,128,512]{2,1,0:T(8,128)(2,1)} custom-call(f32[8,2816]{1,0:T(8,128)S(1)} %copy-done.6, f32[8,256]{1,0:T(8,128)S(1)} %get-tuple-element.34.stat, f32[256,2048]{1,0:T(8,128)S(1)} %get-tuple-element.35.near_scores, f32[256,768]{1,0:T(8,128)S(1)} %get-tuple-element.36.far_scores, bf16[16,128,512]{2,1,0:T(8,128)(2,1)S(1)} %all-to-all-done.near, ...), custom_call_target="tpu_custom_call" | custom-call | bytes 67108864 | tf_op jit(solution)/shard_map/pallas_call | solution.py:26
  62.1 1.0 %collective-permute-done.13.refs_13_ = f32[2,8,256]{2,1,0:T(8,128)S(1)} collective-permute-done((f32[2,8,256]{2,1,0:T(8,128)S(1)}, f32[2,8,256]{2,1,0:T(8,128)S(1)}, u32[]{:S(2)}, u32[]{:S(2)}) %collective-permute-start.13) | collective-permute-done | bytes 16416 | tf_op jit(solution)/shard_map/ppermute | solution.py:20
  63.1 1.7 %collective-permute-done.15.refs_15_ = f32[2,8,256]{2,1,0:T(8,128)S(1)} collective-permute-done((f32[2,8,256]{2,1,0:T(8,128)S(1)}, f32[2,8,256]{2,1,0:T(8,128)S(1)}, u32[]{:S(2)}, u32[]{:S(2)}) %collective-permute-start.15) | collective-permute-done | bytes 16416 | tf_op jit(solution)/shard_map/ppermute | solution.py:20
  64.8 4.7 %shard_map.81 = bf16[6,128,512]{2,1,0:T(8,128)(2,1)} custom-call(s32[8,64]{1,0:T(8,128)S(1)} %copy-done.8, bf16[6,128,512]{2,1,0:T(8,128)(2,1)S(1)} %copy-done.1, bf16[2,128,512]{2,1,0:T(8,128)(2,1)S(1)} %copy-done, bf16[2,128,512]{2,1,0:T(8,128)(2,1)S(1)} %copy-done.5, bf16[2,128,512]{2,1,0:T(8,128)(2,1)S(1)} %copy-done.3, ...), custom_call_target="tpu_custom_call" | custom-call | tf_op jit(solution)/shard_map/pallas_call | solution.py:26
  (35 shorter events, 0.3 us)
Async XLA Ops:
  0.6 12.6 %collective-permute-start = (bf16[2,128,512]{2,1,0:T(8,128)(2,1)}, bf16[2,128,512]{2,1,0:T(8,128)(2,1)}, u32[]{:S(2)}, u32[]{:S(2)}) collective-permute-start(bf16[2,128,512]{2,1,0:T(8,128)(2,1)} %refs_2_.2), channel_id=1, source_target_pairs={{0,24},{8,16},{16,8},{24,0},{1,25},{9,17},{17,9},{25,1},{2,26},{10... | collective-permute-start | bytes 786440 | tf_op jit(solution)/shard_map/ppermute | solution.py:20
  5.7 10.4 %collective-permute-start.1 = (bf16[2,128,512]{2,1,0:T(8,128)(2,1)}, bf16[2,128,512]{2,1,0:T(8,128)(2,1)S(1)}, u32[]{:S(2)}, u32[]{:S(2)}) collective-permute-start(bf16[2,128,512]{2,1,0:T(8,128)(2,1)} %refs_2_.2), channel_id=1, source_target_pairs={{0,6},{1,7},{2,4},{3,5},{4,2},{5,3},{6,0},{7,1},{8,14},{9,15},{10,... | collective-permute-start | bytes 786440 | tf_op jit(solution)/shard_map/ppermute | solution.py:20
  8.2 12.0 %collective-permute-start.2 = (bf16[2,128,512]{2,1,0:T(8,128)(2,1)}, bf16[2,128,512]{2,1,0:T(8,128)(2,1)S(1)}, u32[]{:S(2)}, u32[]{:S(2)}) collective-permute-start(bf16[2,128,512]{2,1,0:T(8,128)(2,1)} %refs_2_.2), channel_id=1, source_target_pairs={{0,4},{1,5},{2,6},{3,7},{4,0},{5,1},{6,2},{7,3},{8,12},{9,13},{10,... | collective-permute-start | bytes 786440 | tf_op jit(solution)/shard_map/ppermute | solution.py:20
  8.7 11.6 %collective-permute-start.3 = (bf16[2,128,512]{2,1,0:T(8,128)(2,1)}, bf16[2,128,512]{2,1,0:T(8,128)(2,1)S(1)}, u32[]{:S(2)}, u32[]{:S(2)}) collective-permute-start(bf16[2,128,512]{2,1,0:T(8,128)(2,1)} %refs_2_.2), channel_id=1, source_target_pairs={{0,2},{1,3},{2,0},{3,1},{4,6},{5,7},{6,4},{7,5},{8,10},{9,11},{10,... | collective-permute-start | bytes 786440 | tf_op jit(solution)/shard_map/ppermute | solution.py:20
  9.2 11.1 %collective-permute-start.4 = (bf16[2,128,512]{2,1,0:T(8,128)(2,1)}, bf16[2,128,512]{2,1,0:T(8,128)(2,1)}, u32[]{:S(2)}, u32[]{:S(2)}) collective-permute-start(bf16[2,128,512]{2,1,0:T(8,128)(2,1)} %refs_2_.2), channel_id=1, source_target_pairs={{0,8},{8,0},{16,24},{24,16},{1,9},{9,1},{17,25},{25,17},{2,10},{10... | collective-permute-start | bytes 786440 | tf_op jit(solution)/shard_map/ppermute | solution.py:20
  20.2 3.9 %copy-start.2 = (bf16[2,128,512]{2,1,0:T(8,128)(2,1)}, bf16[2,128,512]{2,1,0:T(8,128)(2,1)S(1)}, u32[]{:S(2)}) copy-start(bf16[2,128,512]{2,1,0:T(8,128)(2,1)S(1)} %collective-permute-done.2.refs_4_) | copy-start | bytes 786436
  20.3 30.3 %all-to-all-start = ((bf16[16,128,512]{2,1,0:T(8,128)(2,1)}), bf16[16,128,512]{2,1,0:T(8,128)(2,1)S(1)}, u32[]{:S(2)}, u32[]{:S(2)}) async-start(bf16[16,128,512]{2,1,0:T(8,128)(2,1)} %get-tuple-element.29), calls=%async_computation | async-start | bytes 4194304 | tf_op jit(solution)/shard_map/all_to_all | solution.py:378
  24.1 26.5 %copy-start.6 = (f32[8,2816]{1,0:T(8,128)S(1)}, f32[8,2816]{1,0:T(8,128)}, u32[]{:S(2)}) copy-start(f32[8,2816]{1,0:T(8,128)} %get-tuple-element.23.numbers) | copy-start | bytes 270340
  24.1 27.7 %copy-start.7 = (f32[8,256]{1,0:T(8,128)S(1)}, f32[8,256]{1,0:T(8,128)}, u32[]{:S(2)}) copy-start(f32[8,256]{1,0:T(8,128)} %get-tuple-element.24.row_data) | copy-start | bytes 24580
  25.2 36.8 %collective-permute-start.8 = (bf16[8,128,512]{2,1,0:T(8,128)(2,1)}, bf16[8,128,512]{2,1,0:T(8,128)(2,1)}, u32[]{:S(2)}, u32[]{:S(2)}) collective-permute-start(bf16[8,128,512]{2,1,0:T(8,128)(2,1)} %pad_maximum_fusion), channel_id=1, source_target_pairs={{0,1},{1,0},{2,3},{3,2},{4,5},{5,4},{6,7},{7,6},{8,9},{9,8},{10,11... | collective-permute-start | bytes 3145736 | tf_op jit(solution)/shard_map/ppermute | solution.py:20
  25.6 26.2 %collective-permute-start.5 = (bf16[2,128,512]{2,1,0:T(8,128)(2,1)}, bf16[2,128,512]{2,1,0:T(8,128)(2,1)S(1)}, u32[]{:S(2)}, u32[]{:S(2)}) collective-permute-start(bf16[2,128,512]{2,1,0:T(8,128)(2,1)} %get-tuple-element.31), channel_id=1, source_target_pairs={{0,24},{8,16},{16,8},{24,0},{1,25},{9,17},{17,9},{25,1},{2,26},{10... | collective-permute-start | bytes 786440 | tf_op jit(solution)/shard_map/ppermute | solution.py:20
  27.1 24.7 %collective-permute-start.6 = (bf16[2,128,512]{2,1,0:T(8,128)(2,1)}, bf16[2,128,512]{2,1,0:T(8,128)(2,1)S(1)}, u32[]{:S(2)}, u32[]{:S(2)}) collective-permute-start(bf16[2,128,512]{2,1,0:T(8,128)(2,1)} %get-tuple-element.32), channel_id=1, source_target_pairs={{0,16},{8,24},{16,0},{24,8},{1,17},{9,25},{17,1},{25,9},{2,18},{10... | collective-permute-start | bytes 786440 | tf_op jit(solution)/shard_map/ppermute | solution.py:20
  27.1 24.7 %collective-permute-start.7 = (bf16[2,128,512]{2,1,0:T(8,128)(2,1)}, bf16[2,128,512]{2,1,0:T(8,128)(2,1)S(1)}, u32[]{:S(2)}, u32[]{:S(2)}) collective-permute-start(bf16[2,128,512]{2,1,0:T(8,128)(2,1)} %get-tuple-element.33), channel_id=1, source_target_pairs={{0,8},{8,0},{16,24},{24,16},{1,9},{9,1},{17,25},{25,17},{2,10},{10... | collective-permute-start | bytes 786440 | tf_op jit(solution)/shard_map/ppermute | solution.py:20
  30.0 30.1 %collective-permute-start.9 = (bf16[2,128,512]{2,1,0:T(8,128)(2,1)}, bf16[2,128,512]{2,1,0:T(8,128)(2,1)}, u32[]{:S(2)}, u32[]{:S(2)}) collective-permute-start(bf16[2,128,512]{2,1,0:T(8,128)(2,1)} %collective-permute-done.refs_9_), channel_id=1, source_target_pairs={{0,8},{8,0},{16,24},{24,16},{1,9},{9,1},{17,25},{25,17},{2,10},{10... | collective-permute-start | bytes 786440 | tf_op jit(solution)/shard_map/ppermute | solution.py:20
  53.0 3.7 %collective-permute-start.14 = (f32[8,256]{1,0:T(8,128)S(1)}, f32[8,256]{1,0:T(8,128)S(1)}, u32[]{:S(2)}, u32[]{:S(2)}) collective-permute-start(f32[8,256]{1,0:T(8,128)S(1)} %get-tuple-element.34.stat), channel_id=1, source_target_pairs={{0,8},{8,0},{16,24},{24,16},{1,9},{9,1},{17,25},{25,17},{2,10},{10... | collective-permute-start | bytes 24584 | tf_op jit(solution)/shard_map/ppermute | solution.py:20
  53.0 3.6 %collective-permute-start.10 = (f32[8,256]{1,0:T(8,128)S(1)}, f32[8,256]{1,0:T(8,128)S(1)}, u32[]{:S(2)}, u32[]{:S(2)}) collective-permute-start(f32[8,256]{1,0:T(8,128)S(1)} %get-tuple-element.34.stat), channel_id=1, source_target_pairs={{0,1},{1,0},{2,3},{3,2},{4,5},{5,4},{6,7},{7,6},{8,9},{9,8},{10,11... | collective-permute-start | bytes 24584 | tf_op jit(solution)/shard_map/ppermute | solution.py:20
  56.7 5.4 %collective-permute-start.11 = (f32[2,8,256]{2,1,0:T(8,128)S(1)}, f32[2,8,256]{2,1,0:T(8,128)S(1)}, u32[]{:S(2)}, u32[]{:S(2)}) collective-permute-start(f32[2,8,256]{2,1,0:T(8,128)S(1)} %get-tuple-element.45.refs_10_), channel_id=1, source_target_pairs={{0,2},{1,3},{2,0},{3,1},{4,6},{5,7},{6,4},{7,5},{8,10},{9,11},{10,... | collective-permute-start | bytes 49160 | tf_op jit(solution)/shard_map/ppermute | solution.py:20
  57.2 4.9 %collective-permute-start.12 = (f32[2,8,256]{2,1,0:T(8,128)S(1)}, f32[2,8,256]{2,1,0:T(8,128)S(1)}, u32[]{:S(2)}, u32[]{:S(2)}) collective-permute-start(f32[2,8,256]{2,1,0:T(8,128)S(1)} %get-tuple-element.45.refs_10_), channel_id=1, source_target_pairs={{0,4},{1,5},{2,6},{3,7},{4,0},{5,1},{6,2},{7,3},{8,12},{9,13},{10,... | collective-permute-start | bytes 49160 | tf_op jit(solution)/shard_map/ppermute | solution.py:20
  58.5 4.6 %collective-permute-start.13 = (f32[2,8,256]{2,1,0:T(8,128)S(1)}, f32[2,8,256]{2,1,0:T(8,128)S(1)}, u32[]{:S(2)}, u32[]{:S(2)}) collective-permute-start(f32[2,8,256]{2,1,0:T(8,128)S(1)} %get-tuple-element.45.refs_10_), channel_id=1, source_target_pairs={{0,6},{1,7},{2,4},{3,5},{4,2},{5,3},{6,0},{7,1},{8,14},{9,15},{10,... | collective-permute-start | bytes 49160 | tf_op jit(solution)/shard_map/ppermute | solution.py:20
  60.2 4.6 %collective-permute-start.15 = (f32[2,8,256]{2,1,0:T(8,128)S(1)}, f32[2,8,256]{2,1,0:T(8,128)S(1)}, u32[]{:S(2)}, u32[]{:S(2)}) collective-permute-start(f32[2,8,256]{2,1,0:T(8,128)S(1)} %get-tuple-element.44.refs_14_), channel_id=1, source_target_pairs={{0,16},{8,24},{16,0},{24,8},{1,17},{9,25},{17,1},{25,9},{2,18},{10... | collective-permute-start | bytes 49160 | tf_op jit(solution)/shard_map/ppermute | solution.py:20
  60.2 4.6 %copy-start.1 = (bf16[6,128,512]{2,1,0:T(8,128)(2,1)S(1)}, bf16[6,128,512]{2,1,0:T(8,128)(2,1)}, u32[]{:S(2)}) copy-start(bf16[6,128,512]{2,1,0:T(8,128)(2,1)} %refs_1_.1) | copy-start | bytes 2359300
  60.2 4.6 %copy-start.3 = (bf16[2,128,512]{2,1,0:T(8,128)(2,1)S(1)}, bf16[2,128,512]{2,1,0:T(8,128)(2,1)}, u32[]{:S(2)}) copy-start(bf16[2,128,512]{2,1,0:T(8,128)(2,1)} %copy-done.2) | copy-start | bytes 786436
  60.2 4.6 %copy-start.5 = (bf16[2,128,512]{2,1,0:T(8,128)(2,1)S(1)}, bf16[2,128,512]{2,1,0:T(8,128)(2,1)}, u32[]{:S(2)}) copy-start(bf16[2,128,512]{2,1,0:T(8,128)(2,1)} %copy-done.4) | copy-start | bytes 786436
  60.2 4.6 %copy-start.8 = (s32[8,64]{1,0:T(8,128)S(1)}, s32[8,64]{1,0:T(8,128)}, u32[]{:S(2)}) copy-start(s32[8,64]{1,0:T(8,128)} %get-tuple-element.37.refs_0_) | copy-start | bytes 6148
  (2 other events, 7.5 us)
